TPU v7x, 128 devices: a whole 4x4x4 slice. The times are simulated.
128 devices in a mesh: lat: 16 (over y, x_lo, core), ch: 8 (over z, x_hi).
Axes of the slice: x: 4 (x_hi: 2, x_lo: 2; x = x_hi * 2 + x_lo), y: 4, z: 4, core: 2. Of those that a mesh axis runs over, the one named last changes fastest.
Arguments:
- inputs: float32 [384, 80, 180], P('ch', 'lat'), may hold values from -44 to 44
- cotangent: float32 [384, 80, 180], P('ch', 'lat'), may hold values from -1.5 to 1.5
- first_gain: float32 [4, 384], P(None, 'ch'), may hold values from 0.5 to 1.5
- first_shift: float32 [4, 384], P(None, 'ch'), may hold values from -3 to 3
- filter_inner: float32 [4, 2, 8, 48, 48], P(None, None, 'ch'), may hold values from -0.625 to 0.625
- filter_inner_bias: float32 [4, 2, 8, 48], P(None, None, 'ch'), may hold values from -3 to 3
- filter_outer: float32 [4, 2, 8, 48, 48], P(None, None, 'ch'), may hold values from -0.625 to 0.625
- filter_outer_bias: float32 [4, 2, 8, 48], P(None, None, 'ch'), may hold values from -3 to 3
- second_gain: float32 [4, 384], P(None, 'ch'), may hold values from 0.5 to 1.5
- second_shift: float32 [4, 384], P(None, 'ch'), may hold values from -3 to 3
- up_weight: bfloat16 [4, 384, 1536], P(None, None, 'ch'), may hold values from -0.3125 to 0.3125
- up_bias: float32 [4, 1536], P(None, 'ch'), may hold values from -3 to 3
- down_weight: bfloat16 [4, 1536, 384], P(None, 'ch'), may hold values from -0.15625 to 0.15625
- down_bias: float32 [4, 384], P(None, 'ch'), may hold values from -3 to 3
- kept_lat: int32 [60], replicated, may hold values from 0 to 79, as said below
- kept_lon: int32 [64], replicated, may hold values from 0 to 90, as said below
Outputs:
- outputs: float32 [384, 80, 180], P('ch', 'lat')
- input_grad: float32 [384, 80, 180], P('ch', 'lat')
- first_gain_grad: float32 [4, 384], P(None, 'ch')
- first_shift_grad: float32 [4, 384], P(None, 'ch')
- inner_weight_grad: float32 [4, 2, 8, 48, 48], P(None, None, 'ch')
- inner_bias_grad: float32 [4, 2, 8, 48], P(None, None, 'ch')
- outer_weight_grad: float32 [4, 2, 8, 48, 48], P(None, None, 'ch')
- outer_bias_grad: float32 [4, 2, 8, 48], P(None, None, 'ch')
- second_gain_grad: float32 [4, 384], P(None, 'ch')
- second_shift_grad: float32 [4, 384], P(None, 'ch')
- up_weight_grad: float32 [4, 384, 1536], P(None, None, 'ch')
- up_bias_grad: float32 [4, 1536], P(None, 'ch')
- down_weight_grad: float32 [4, 1536, 384], P(None, 'ch')
- down_bias_grad: float32 [4, 384], P(None, 'ch')
Inputs may be any that keep to these rules, and one draw needn't show every extreme that they name: `kept_lat`: 60 distinct latitude mode numbers, among them 0 and 79. `kept_lon`: 64 distinct longitude mode numbers, among them 0 and 90.
All inputs are finite; a program needn't handle non-finite values.
Results may differ from a plain program's by a relative error of at most 0.025.
Values may be sent and summed in bfloat16 or wider, within the bound.
A program may use at most 128 MiB of HBM per device.

v0:
```python
import math

import jax
import jax.numpy as jnp
from jax import lax
from jax.sharding import PartitionSpec as P

shrink_level = 0.01
norm_eps = 1e-05
highest = lax.Precision.HIGHEST


def gelu_exact(values):
    return 0.5 * values * (1.0 + lax.erf(values * 0.7071067811865476))


def gelu_slope(values):
    return (
        0.5 * (1.0 + lax.erf(values * 0.7071067811865476))
        + values * jnp.exp(-0.5 * values * values) * 0.3989422804014327
    )


def soft_shrink(values):
    return values - shrink_level * jnp.tanh(values / shrink_level)


def complex_mix(real_part, imag_part, weight, bias_pair):
    real_out = jnp.einsum("bimk,bij->bjmk", real_part, weight[0], precision=highest) - jnp.einsum(
        "bimk,bij->bjmk", imag_part, weight[1], precision=highest
    )
    imag_out = jnp.einsum("bimk,bij->bjmk", imag_part, weight[0], precision=highest) + jnp.einsum(
        "bimk,bij->bjmk", real_part, weight[1], precision=highest
    )
    return (real_out + bias_pair[0][:, :, None, None], imag_out + bias_pair[1][:, :, None, None])


def block_mlp(real_part, imag_part, weight_in, bias_in, weight_out, bias_out):
    hidden_re, hidden_im = complex_mix(real_part, imag_part, weight_in, bias_in)
    out_re, out_im = complex_mix(gelu_exact(hidden_re), gelu_exact(hidden_im), weight_out, bias_out)
    return (soft_shrink(out_re), soft_shrink(out_im))


def lat_tables(kept_lat, lat_cells):
    cell_index = jnp.arange(lat_cells, dtype=jnp.int32)
    phase_index = kept_lat[:, None] * cell_index[None, :] % lat_cells
    angles = phase_index.astype(jnp.float32) * (2.0 * math.pi / lat_cells)
    norm_scale = 1.0 / math.sqrt(lat_cells)
    return (jnp.cos(angles) * norm_scale, jnp.sin(angles) * norm_scale)


def lon_tables(kept_lon, lon_cells):
    cell_index = jnp.arange(lon_cells, dtype=jnp.int32)
    phase_index = kept_lon[:, None] * cell_index[None, :] % lon_cells
    angles = phase_index.astype(jnp.float32) * (2.0 * math.pi / lon_cells)
    norm_scale = 1.0 / math.sqrt(lon_cells)
    mode_weight = jnp.where((kept_lon == 0) | (2 * kept_lon == lon_cells), 1.0, 2.0).astype(
        jnp.float32
    )[:, None]
    forward_table = (
        jnp.stack([jnp.cos(angles), -jnp.sin(angles)], axis=1).reshape(-1, lon_cells).T * norm_scale
    )
    inverse_table = (
        jnp.stack([jnp.cos(angles) * mode_weight, -jnp.sin(angles) * mode_weight], axis=1).reshape(
            -1, lon_cells
        )
        * norm_scale
    )
    return (forward_table, inverse_table)


def spectral_local(spectrum, weight_in, bias_in, weight_out, bias_out, cos_lat, sin_lat):
    chan_count, lat_cells, pair_count = spectrum.shape
    mode_span = pair_count // 2
    paired = spectrum.reshape(chan_count, lat_cells, mode_span, 2)
    real_in = paired[..., 0]
    imag_in = paired[..., 1]
    mode_re = jnp.einsum("mh,chk->cmk", cos_lat, real_in, precision=highest) + jnp.einsum(
        "mh,chk->cmk", sin_lat, imag_in, precision=highest
    )
    mode_im = jnp.einsum("mh,chk->cmk", cos_lat, imag_in, precision=highest) - jnp.einsum(
        "mh,chk->cmk", sin_lat, real_in, precision=highest
    )
    blocks = weight_in.shape[1]
    block_shape = (blocks, chan_count // blocks, cos_lat.shape[0], mode_span)
    out_re, out_im = block_mlp(
        mode_re.reshape(block_shape),
        mode_im.reshape(block_shape),
        weight_in,
        bias_in,
        weight_out,
        bias_out,
    )
    out_re = out_re.reshape(chan_count, cos_lat.shape[0], mode_span)
    out_im = out_im.reshape(chan_count, cos_lat.shape[0], mode_span)
    back_re = jnp.einsum("mh,cmk->chk", cos_lat, out_re, precision=highest) - jnp.einsum(
        "mh,cmk->chk", sin_lat, out_im, precision=highest
    )
    back_im = jnp.einsum("mh,cmk->chk", cos_lat, out_im, precision=highest) + jnp.einsum(
        "mh,cmk->chk", sin_lat, out_re, precision=highest
    )
    return jnp.stack([back_re, back_im], axis=-1).reshape(chan_count, lat_cells, pair_count)


def norm_sums(values):
    return lax.psum((jnp.sum(values, axis=0), jnp.sum(values * values, axis=0)), "ch")


def stats_from(sum_first, sum_second, channel_total):
    mean_value = sum_first / channel_total
    spread = sum_second / channel_total - mean_value * mean_value
    return (mean_value, lax.rsqrt(spread + norm_eps))


def norm_back_sums(scaled_grad, normed):
    return lax.psum((jnp.sum(scaled_grad, axis=0), jnp.sum(scaled_grad * normed, axis=0)), "ch")


def to_modes(values):
    return lax.all_to_all(values, "lat", split_axis=2, concat_axis=1, tiled=True)


def to_rows(values):
    return lax.all_to_all(values, "lat", split_axis=1, concat_axis=2, tiled=True)


def body(
    inputs,
    cotangent,
    first_gain,
    first_shift,
    filter_inner,
    filter_inner_bias,
    filter_outer,
    filter_outer_bias,
    second_gain,
    second_shift,
    up_weight,
    up_bias,
    down_weight,
    down_bias,
    kept_lat,
    kept_lon,
):
    chan_count, row_count, lon_cells = inputs.shape
    lat_cells = row_count * lax.axis_size("lat")
    channel_total = chan_count * lax.axis_size("ch")
    layer_count = first_gain.shape[0]
    lon_forward, lon_inverse = lon_tables(kept_lon, lon_cells)
    cos_lat, sin_lat = lat_tables(kept_lat, lat_cells)
    current = inputs
    saved_layers = []
    for layer_index in range(layer_count):
        sum_first, sum_second = norm_sums(current)
        mean_one, rstd_one = stats_from(sum_first, sum_second, channel_total)
        normed_one = (current - mean_one) * rstd_one
        mixed_one = (
            normed_one * first_gain[layer_index][:, None, None]
            + first_shift[layer_index][:, None, None]
        )
        spectrum = to_modes(jnp.einsum("crw,wp->crp", mixed_one, lon_forward, precision=highest))
        filtered = spectral_local(
            spectrum,
            filter_inner[layer_index],
            filter_inner_bias[layer_index],
            filter_outer[layer_index],
            filter_outer_bias[layer_index],
            cos_lat,
            sin_lat,
        )
        back_field = jnp.einsum("crp,pw->crw", to_rows(filtered), lon_inverse, precision=highest)
        inner_field = current + mixed_one + back_field
        up_layer = up_weight[layer_index]
        down_layer = down_weight[layer_index]
        sum_first, sum_second = norm_sums(inner_field)
        mean_two, rstd_two = stats_from(sum_first, sum_second, channel_total)
        normed_two = (inner_field - mean_two) * rstd_two
        gain_two = second_gain[layer_index]
        lifted_part = (
            normed_two * gain_two[:, None, None] + second_shift[layer_index][:, None, None]
        ).astype(jnp.bfloat16)
        lifted = lax.all_gather(lifted_part, "ch", axis=0, tiled=True)
        pre_act = (
            jnp.einsum("crw,cf->frw", lifted, up_layer, preferred_element_type=jnp.float32)
            + up_bias[layer_index][:, None, None]
        )
        hidden_act = gelu_exact(pre_act).astype(jnp.bfloat16)
        summed = lax.psum_scatter(
            jnp.einsum(
                "frw,fc->crw", hidden_act, down_layer, preferred_element_type=jnp.float32
            ).astype(jnp.bfloat16),
            "ch",
            scatter_dimension=0,
            tiled=True,
        ).astype(jnp.float32)
        next_field = inner_field + summed + down_bias[layer_index][:, None, None]
        saved_layers.append(
            (
                normed_one,
                rstd_one,
                spectrum,
                normed_two,
                rstd_two,
                lifted,
                pre_act,
                hidden_act,
                gain_two,
            )
        )
        current = next_field
    grad_now = cotangent
    collected = []
    for layer_index in reversed(range(layer_count)):
        (
            normed_one,
            rstd_one,
            spectrum,
            normed_two,
            rstd_two,
            lifted,
            pre_act,
            hidden_act,
            gain_two,
        ) = saved_layers[layer_index]
        up_layer = up_weight[layer_index]
        down_layer = down_weight[layer_index]
        down_shift_grad = jnp.sum(grad_now, axis=(1, 2))
        full_cot = lax.all_gather(grad_now.astype(jnp.bfloat16), "ch", axis=0, tiled=True)
        hidden_grad = jnp.einsum(
            "crw,fc->frw", full_cot, down_layer, preferred_element_type=jnp.float32
        )
        down_grad = jnp.einsum(
            "frw,crw->fc", hidden_act, full_cot, preferred_element_type=jnp.float32
        )
        pre_grad = hidden_grad * gelu_slope(pre_act)
        pre_round = pre_grad.astype(jnp.bfloat16)
        up_shift_grad = jnp.sum(pre_grad, axis=(1, 2))
        up_grad = jnp.einsum("crw,frw->cf", lifted, pre_round, preferred_element_type=jnp.float32)
        lift_grad = lax.psum_scatter(
            jnp.einsum(
                "frw,cf->crw", pre_round, up_layer, preferred_element_type=jnp.float32
            ).astype(jnp.bfloat16),
            "ch",
            scatter_dimension=0,
            tiled=True,
        ).astype(jnp.float32)
        gain_two_grad = jnp.sum(lift_grad * normed_two, axis=(1, 2))
        shift_two_grad = jnp.sum(lift_grad, axis=(1, 2))
        scaled_two = lift_grad * gain_two[:, None, None]
        sum_plain, sum_cross = norm_back_sums(scaled_two, normed_two)
        inner_grad = grad_now + rstd_two * (
            scaled_two - sum_plain / channel_total - normed_two * (sum_cross / channel_total)
        )
        mode_grad = to_modes(jnp.einsum("crw,pw->crp", inner_grad, lon_inverse, precision=highest))

        def local_filter(spec_in, weight_in, bias_in, weight_out, bias_out):
            return spectral_local(
                spec_in, weight_in, bias_in, weight_out, bias_out, cos_lat, sin_lat
            )

        spectral_value, filter_vjp = jax.vjp(
            local_filter,
            spectrum,
            filter_inner[layer_index],
            filter_inner_bias[layer_index],
            filter_outer[layer_index],
            filter_outer_bias[layer_index],
        )
        spectrum_grad, first_w_grad, first_b_grad, second_w_grad, second_b_grad = filter_vjp(
            mode_grad
        )
        mixed_grad = inner_grad + jnp.einsum(
            "crp,wp->crw", to_rows(spectrum_grad), lon_forward, precision=highest
        )
        gain_one_grad = jnp.sum(mixed_grad * normed_one, axis=(1, 2))
        shift_one_grad = jnp.sum(mixed_grad, axis=(1, 2))
        scaled_one = mixed_grad * first_gain[layer_index][:, None, None]
        sum_plain, sum_cross = norm_back_sums(scaled_one, normed_one)
        grad_now = inner_grad + rstd_one * (
            scaled_one - sum_plain / channel_total - normed_one * (sum_cross / channel_total)
        )
        layer_terms = (
            gain_one_grad,
            shift_one_grad,
            first_w_grad,
            first_b_grad,
            second_w_grad,
            second_b_grad,
            gain_two_grad,
            shift_two_grad,
            up_grad,
            up_shift_grad,
            down_grad,
            down_shift_grad,
        )
        collected.append(layer_terms)
    collected = collected[::-1]
    stacked = tuple((jnp.stack([terms[position] for terms in collected]) for position in range(12)))
    stacked = lax.psum(stacked, "lat")
    return (current, grad_now) + tuple(stacked)


def solution(mesh):
    placed = (
        P("ch", "lat", None),
        P("ch", "lat", None),
        P(None, "ch"),
        P(None, "ch"),
        P(None, None, "ch", None, None),
        P(None, None, "ch", None),
        P(None, None, "ch", None, None),
        P(None, None, "ch", None),
        P(None, "ch"),
        P(None, "ch"),
        P(None, None, "ch"),
        P(None, "ch"),
        P(None, "ch", None),
        P(None, "ch"),
        P(),
        P(),
    )
    return jax.shard_map(
        body,
        mesh=mesh,
        in_specs=placed,
        out_specs=(
            P("ch", "lat", None),
            P("ch", "lat", None),
            P(None, "ch"),
            P(None, "ch"),
            P(None, None, "ch", None, None),
            P(None, None, "ch", None),
            P(None, None, "ch", None, None),
            P(None, None, "ch", None),
            P(None, "ch"),
            P(None, "ch"),
            P(None, None, "ch"),
            P(None, "ch"),
            P(None, "ch", None),
            P(None, "ch"),
        ),
        check_vma=False,
    )
```

profile of v0, /device:TPU:1, one launch (start us, length us, event | category | flops | bytes accessed | tf_op | source)
XLA Modules:
  0.0 1993.5 jit_solution(16905084202889143613)
XLA Ops:
  13.0 36.8 %all-reduce.73 = (f32[5,180]{1,0:T(8,128)S(1)}, f32[5,180]{1,0:T(8,128)S(1)}) all-reduce(f32[5,180]{1,0:T(8,128)S(1)} %get-tuple-element.123, f32[5,180]{1,0:T(8,128)S(1)} %get-tuple-element.122), channel_id=1, replica_groups=mesh['lat'=16,'ch'=8] {'ch'}, use_global_device_ids=true, to_apply=%region_3.4 | all-reduce | flops 1800 | bytes 14400 | tf_op jit(solution)/shard_map/psum | solution.py:106
  51.5 12.4 all-to-all-start
  66.5 3.5 all-to-all-done
  80.6 3.9 all-to-all-start.1
  85.1 5.5 all-to-all-done.1
  92.5 30.1 %all-reduce.72 = (f32[5,180]{1,0:T(8,128)S(1)}, f32[5,180]{1,0:T(8,128)S(1)}) all-reduce(f32[5,180]{1,0:T(8,128)S(1)} %get-tuple-element.121, f32[5,180]{1,0:T(8,128)S(1)} %get-tuple-element.120), channel_id=1, replica_groups=mesh['lat'=16,'ch'=8] {'ch'}, use_global_device_ids=true, to_apply=%region_7.8 | all-reduce | flops 1800 | bytes 14400 | tf_op jit(solution)/shard_map/psum | solution.py:106
  122.7 32.3 %all_gather.24 = bf16[384,5,180]{2,0,1:T(8,128)(2,1)S(1)} all-gather(bf16[48,5,180]{2,0,1:T(8,128)(2,1)S(1)} %add_convert_fusion.3), channel_id=1, replica_groups=mesh['lat'=16,'ch'=8] {'ch'}, dimensions={0}, use_global_device_ids=true | all-gather | bytes 777600 | tf_op jit(solution)/shard_map/all_gather | solution.py:182
  162.8 78.4 %reduce-scatter.9.cloned.1.call-done = bf16[48,5,180]{2,1,0:T(8,128)(2,1)} async-done(((bf16[384,5,180]{2,1,0:T(8,128)(2,1)}), bf16[48,5,180]{2,1,0:T(8,128)(2,1)}) %reduce-scatter.9.cloned.1.call-update) | async-done | bytes 86416 | tf_op jit(solution)/shard_map/reduce_scatter | solution.py:188
  242.2 32.5 %all-reduce.71 = (f32[5,180]{1,0:T(8,128)S(1)}, f32[5,180]{1,0:T(8,128)S(1)}) all-reduce(f32[5,180]{1,0:T(8,128)S(1)} %get-tuple-element.119, f32[5,180]{1,0:T(8,128)S(1)} %get-tuple-element.118), channel_id=1, replica_groups=mesh['lat'=16,'ch'=8] {'ch'}, use_global_device_ids=true, to_apply=%region_12.13 | all-reduce | flops 1800 | bytes 14400 | tf_op jit(solution)/shard_map/psum | solution.py:106
  275.8 19.8 all_to_all.264
  305.2 9.2 all_to_all.265
  316.2 30.1 %all-reduce.70 = (f32[5,180]{1,0:T(8,128)S(1)}, f32[5,180]{1,0:T(8,128)S(1)}) all-reduce(f32[5,180]{1,0:T(8,128)S(1)} %get-tuple-element.117, f32[5,180]{1,0:T(8,128)S(1)} %get-tuple-element.116), channel_id=1, replica_groups=mesh['lat'=16,'ch'=8] {'ch'}, use_global_device_ids=true, to_apply=%region_16.17 | all-reduce | flops 1800 | bytes 14400 | tf_op jit(solution)/shard_map/psum | solution.py:106
  346.4 32.3 %all_gather.25 = bf16[384,5,180]{2,0,1:T(8,128)(2,1)S(1)} all-gather(bf16[48,5,180]{2,0,1:T(8,128)(2,1)S(1)} %add_convert_fusion.2), channel_id=1, replica_groups=mesh['lat'=16,'ch'=8] {'ch'}, dimensions={0}, use_global_device_ids=true | all-gather | bytes 777600 | tf_op jit(solution)/shard_map/all_gather | solution.py:182
  386.9 79.5 %reduce-scatter.11.cloned.1.call-done = bf16[48,5,180]{2,1,0:T(8,128)(2,1)} async-done(((bf16[384,5,180]{2,1,0:T(8,128)(2,1)}), bf16[48,5,180]{2,1,0:T(8,128)(2,1)}) %reduce-scatter.11.cloned.1.call-update) | async-done | bytes 86416 | tf_op jit(solution)/shard_map/reduce_scatter | solution.py:188
  467.5 32.1 %all-reduce.69 = (f32[5,180]{1,0:T(8,128)S(1)}, f32[5,180]{1,0:T(8,128)S(1)}) all-reduce(f32[5,180]{1,0:T(8,128)S(1)} %get-tuple-element.115, f32[5,180]{1,0:T(8,128)S(1)} %get-tuple-element.114), channel_id=1, replica_groups=mesh['lat'=16,'ch'=8] {'ch'}, use_global_device_ids=true, to_apply=%region_21.22 | all-reduce | flops 1800 | bytes 14400 | tf_op jit(solution)/shard_map/psum | solution.py:106
  502.4 20.3 %all_to_all.266 = f32[16,1,1920]{2,1,0:T(1,128)S(1)} all-to-all(f32[16,1,1920]{2,1,0:T(1,128)S(1)} %reshape.1489), channel_id=1, replica_groups=mesh['lat'=16,'ch'=8] {'lat'}, dimensions={0} | all-to-all | bytes 245760 | tf_op jit(solution)/shard_map/all_to_all | solution.py:120
  538.6 9.2 all_to_all.267
  550.3 30.1 %all-reduce.68 = (f32[5,180]{1,0:T(8,128)S(1)}, f32[5,180]{1,0:T(8,128)S(1)}) all-reduce(f32[5,180]{1,0:T(8,128)S(1)} %get-tuple-element.113, f32[5,180]{1,0:T(8,128)S(1)} %get-tuple-element.112), channel_id=1, replica_groups=mesh['lat'=16,'ch'=8] {'ch'}, use_global_device_ids=true, to_apply=%region_25.26 | all-reduce | flops 1800 | bytes 14400 | tf_op jit(solution)/shard_map/psum | solution.py:106
  581.1 31.4 %all_gather.26 = bf16[384,5,180]{2,0,1:T(8,128)(2,1)S(1)} all-gather(bf16[48,5,180]{2,0,1:T(8,128)(2,1)S(1)} %add_convert_fusion.1), channel_id=1, replica_groups=mesh['lat'=16,'ch'=8] {'ch'}, dimensions={0}, use_global_device_ids=true | all-gather | bytes 777600 | tf_op jit(solution)/shard_map/all_gather | solution.py:182
  620.6 80.4 %reduce-scatter.13.cloned.1.call-done = bf16[48,5,180]{2,1,0:T(8,128)(2,1)} async-done(((bf16[384,5,180]{2,1,0:T(8,128)(2,1)}), bf16[48,5,180]{2,1,0:T(8,128)(2,1)}) %reduce-scatter.13.cloned.1.call-update) | async-done | bytes 86416 | tf_op jit(solution)/shard_map/reduce_scatter | solution.py:188
  703.7 32.5 %all-reduce.67 = (f32[5,180]{1,0:T(8,128)}, f32[5,180]{1,0:T(8,128)}) all-reduce(f32[5,180]{1,0:T(8,128)} %get-tuple-element.111, f32[5,180]{1,0:T(8,128)} %get-tuple-element.110), channel_id=1, replica_groups=mesh['lat'=16,'ch'=8] {'ch'}, use_global_device_ids=true, to_apply=%region_30.31 | all-reduce | flops 1800 | bytes 14400 | tf_op jit(solution)/shard_map/psum | solution.py:106
  743.5 20.6 %all_to_all.268 = f32[16,1,1920]{2,1,0:T(1,128)} all-to-all(f32[16,1,1920]{2,1,0:T(1,128)} %reshape.1493), channel_id=1, replica_groups=mesh['lat'=16,'ch'=8] {'lat'}, dimensions={0} | all-to-all | bytes 245760 | tf_op jit(solution)/shard_map/all_to_all | solution.py:120
  792.2 4.5 all-to-all-start.7
  796.8 33.8 %all_gather.28 = bf16[384,5,180]{2,0,1:T(8,128)(2,1)} all-gather(bf16[48,5,180]{2,0,1:T(8,128)(2,1)} %get-tuple-element.341), channel_id=1, replica_groups=mesh['lat'=16,'ch'=8] {'ch'}, dimensions={0}, use_global_device_ids=true | all-gather | bytes 777600 | tf_op jit(solution)/shard_map/all_gather | solution.py:228
  834.8 3.1 fusion.950
  837.9 33.7 %all-reduce.66 = (f32[5,180]{1,0:T(8,128)}, f32[5,180]{1,0:T(8,128)}) all-reduce(f32[5,180]{1,0:T(8,128)} %get-tuple-element.109, f32[5,180]{1,0:T(8,128)} %get-tuple-element.108), channel_id=1, replica_groups=mesh['lat'=16,'ch'=8] {'ch'}, use_global_device_ids=true, to_apply=%region_34.35 | all-reduce | flops 1800 | bytes 14400 | tf_op jit(solution)/shard_map/psum | solution.py:106
  873.4 33.0 %all_gather.27 = bf16[384,5,180]{2,0,1:T(8,128)(2,1)S(1)} all-gather(bf16[48,5,180]{2,0,1:T(8,128)(2,1)S(1)} %add_convert_fusion), channel_id=1, replica_groups=mesh['lat'=16,'ch'=8] {'ch'}, dimensions={0}, use_global_device_ids=true | all-gather | bytes 777600 | tf_op jit(solution)/shard_map/all_gather | solution.py:182
  923.2 78.3 %reduce-scatter.17.cloned.1.call-done = bf16[48,5,180]{2,1,0:T(8,128)(2,1)} async-done(((bf16[384,5,180]{2,1,0:T(8,128)(2,1)}), bf16[48,5,180]{2,1,0:T(8,128)(2,1)}) %reduce-scatter.17.cloned.1.call-update) | async-done | bytes 86416 | tf_op jit(solution)/shard_map/reduce_scatter | solution.py:239
  1003.9 32.6 %all-reduce.65 = (f32[5,180]{1,0:T(8,128)}, f32[5,180]{1,0:T(8,128)}) all-reduce(f32[5,180]{1,0:T(8,128)} %get-tuple-element.99, f32[5,180]{1,0:T(8,128)} %get-tuple-element.124), channel_id=1, replica_groups=mesh['lat'=16,'ch'=8] {'ch'}, use_global_device_ids=true, to_apply=%region_40.41 | all-reduce | flops 1800 | bytes 14400 | tf_op jit(solution)/shard_map/psum | solution.py:116
  1039.2 37.9 %reduce-scatter.15.cloned.1.call-done = bf16[48,5,180]{2,1,0:T(8,128)(2,1)} async-done(((bf16[384,5,180]{2,1,0:T(8,128)(2,1)}), bf16[48,5,180]{2,1,0:T(8,128)(2,1)}) %reduce-scatter.15.cloned.1.call-update) | async-done | bytes 86416 | tf_op jit(solution)/shard_map/reduce_scatter | solution.py:188
  1084.8 6.3 all-to-all-start.8
  1093.7 3.5 all-to-all-done.8
  1127.6 4.5 all-to-all-start.9
  1135.2 3.2 all-to-all-done.9
  1142.6 3.4 multiply_reduce_fusion
  1145.9 34.0 %all-reduce.64 = (f32[5,180]{1,0:T(8,128)}, f32[5,180]{1,0:T(8,128)}) all-reduce(f32[5,180]{1,0:T(8,128)} %get-tuple-element.91, f32[5,180]{1,0:T(8,128)} %get-tuple-element.100), channel_id=1, replica_groups=mesh['lat'=16,'ch'=8] {'ch'}, use_global_device_ids=true, to_apply=%region_44.45 | all-reduce | flops 1800 | bytes 14400 | tf_op jit(solution)/shard_map/psum | solution.py:116
  1184.1 30.6 %all_gather.29 = bf16[384,5,180]{2,0,1:T(8,128)(2,1)S(1)} all-gather(bf16[48,5,180]{2,0,1:T(8,128)(2,1)S(1)} %convert_element_type.172), channel_id=1, replica_groups=mesh['lat'=16,'ch'=8] {'ch'}, dimensions={0}, use_global_device_ids=true | all-gather | bytes 777600 | tf_op jit(solution)/shard_map/all_gather | solution.py:228
  1235.6 68.8 %reduce-scatter.19.cloned.1.call-done = bf16[48,5,180]{2,1,0:T(8,128)(2,1)} async-done(((bf16[384,5,180]{2,1,0:T(8,128)(2,1)}), bf16[48,5,180]{2,1,0:T(8,128)(2,1)}) %reduce-scatter.19.cloned.1.call-update) | async-done | bytes 86416 | tf_op jit(solution)/shard_map/reduce_scatter | solution.py:239
  1306.8 33.0 %all-reduce.63 = (f32[5,180]{1,0:T(8,128)}, f32[5,180]{1,0:T(8,128)}) all-reduce(f32[5,180]{1,0:T(8,128)} %get-tuple-element.97, f32[5,180]{1,0:T(8,128)} %get-tuple-element.125), channel_id=1, replica_groups=mesh['lat'=16,'ch'=8] {'ch'}, use_global_device_ids=true, to_apply=%region_49.50 | all-reduce | flops 1800 | bytes 14400 | tf_op jit(solution)/shard_map/psum | solution.py:116
  1348.1 14.3 all-to-all-start.10
  1364.8 3.8 all-to-all-done.10
  1386.5 4.5 all-to-all-start.11
  1391.8 5.4 all-to-all-done.11
  1401.5 3.1 multiply_reduce_fusion.1
  1404.6 30.1 %all-reduce.62 = (f32[5,180]{1,0:T(8,128)S(1)}, f32[5,180]{1,0:T(8,128)S(1)}) all-reduce(f32[5,180]{1,0:T(8,128)S(1)} %get-tuple-element.89, f32[5,180]{1,0:T(8,128)S(1)} %get-tuple-element.101), channel_id=1, replica_groups=mesh['lat'=16,'ch'=8] {'ch'}, use_global_device_ids=true, to_apply=%region_53.54 | all-reduce | flops 1800 | bytes 14400 | tf_op jit(solution)/shard_map/psum | solution.py:116
  1437.2 31.6 %all_gather.30 = bf16[384,5,180]{2,0,1:T(8,128)(2,1)S(1)} all-gather(bf16[48,5,180]{2,0,1:T(8,128)(2,1)S(1)} %convert_element_type.177), channel_id=1, replica_groups=mesh['lat'=16,'ch'=8] {'ch'}, dimensions={0}, use_global_device_ids=true | all-gather | bytes 777600 | tf_op jit(solution)/shard_map/all_gather | solution.py:228
  1473.3 2.8 copy.667
  1485.6 71.2 %reduce-scatter.21.cloned.1.call-done = bf16[48,5,180]{2,1,0:T(8,128)(2,1)} async-done(((bf16[384,5,180]{2,1,0:T(8,128)(2,1)}), bf16[48,5,180]{2,1,0:T(8,128)(2,1)}) %reduce-scatter.21.cloned.1.call-update) | async-done | bytes 86416 | tf_op jit(solution)/shard_map/reduce_scatter | solution.py:239
  1559.1 32.1 %all-reduce.61 = (f32[5,180]{1,0:T(8,128)S(1)}, f32[5,180]{1,0:T(8,128)S(1)}) all-reduce(f32[5,180]{1,0:T(8,128)S(1)} %get-tuple-element.95, f32[5,180]{1,0:T(8,128)S(1)} %get-tuple-element.126), channel_id=1, replica_groups=mesh['lat'=16,'ch'=8] {'ch'}, use_global_device_ids=true, to_apply=%region_58.59 | all-reduce | flops 1800 | bytes 14400 | tf_op jit(solution)/shard_map/psum | solution.py:116
  1595.6 14.1 all-to-all-start.12
  1612.1 3.7 all-to-all-done.12
  1629.2 3.9 all-to-all-start.13
  1634.5 4.7 all-to-all-done.13
  1641.7 30.1 %all-reduce.60 = (f32[5,180]{1,0:T(8,128)S(1)}, f32[5,180]{1,0:T(8,128)S(1)}) all-reduce(f32[5,180]{1,0:T(8,128)S(1)} %get-tuple-element.87, f32[5,180]{1,0:T(8,128)S(1)} %get-tuple-element.102), channel_id=1, replica_groups=mesh['lat'=16,'ch'=8] {'ch'}, use_global_device_ids=true, to_apply=%region_62.63 | all-reduce | flops 1800 | bytes 14400 | tf_op jit(solution)/shard_map/psum | solution.py:116
  1672.6 31.4 %all_gather.31 = bf16[384,5,180]{2,0,1:T(8,128)(2,1)S(1)} all-gather(bf16[48,5,180]{2,0,1:T(8,128)(2,1)S(1)} %convert_element_type.182), channel_id=1, replica_groups=mesh['lat'=16,'ch'=8] {'ch'}, dimensions={0}, use_global_device_ids=true | all-gather | bytes 777600 | tf_op jit(solution)/shard_map/all_gather | solution.py:228
  1722.5 69.9 %reduce-scatter.23.cloned.1.call-done = bf16[48,5,180]{2,1,0:T(8,128)(2,1)} async-done(((bf16[384,5,180]{2,1,0:T(8,128)(2,1)}), bf16[48,5,180]{2,1,0:T(8,128)(2,1)}) %reduce-scatter.23.cloned.1.call-update) | async-done | bytes 86416 | tf_op jit(solution)/shard_map/reduce_scatter | solution.py:239
  1793.5 32.1 %all-reduce.59 = (f32[5,180]{1,0:T(8,128)S(1)}, f32[5,180]{1,0:T(8,128)S(1)}) all-reduce(f32[5,180]{1,0:T(8,128)S(1)} %get-tuple-element.93, f32[5,180]{1,0:T(8,128)S(1)} %get-tuple-element.127), channel_id=1, replica_groups=mesh['lat'=16,'ch'=8] {'ch'}, use_global_device_ids=true, to_apply=%region_67.68 | all-reduce | flops 1800 | bytes 14400 | tf_op jit(solution)/shard_map/psum | solution.py:116
  1827.4 14.1 all-to-all-start.14
  1841.9 5.7 all-to-all-done.14
  1860.0 4.0 all-to-all-start.15
  1864.1 6.0 all-to-all-done.15
  1872.1 50.6 %all-reduce.56 = (f32[4,48]{1,0:T(4,128)}, f32[4,48]{1,0:T(4,128)}, f32[4,2,1,48]{3,1,2,0:T(2,128)}, f32[4,2,1,48]{3,1,2,0:T(2,128)}, f32[4,48]{1,0:T(4,128)}, /...) all-reduce(f32[4,48]{1,0:T(4,128)S(1)} %pad_maximum_fusion.11, ...), channel_id=1, replica_groups=mesh['lat'=16,'ch'=8] {'lat'}, use_global_device_ids=true, to_apply=%region_76.77 | all-reduce | flops 2496 | bytes 19968 | tf_op jit(solution)/shard_map/psum | solution.py:299
  1922.7 30.1 %all-reduce.58 = (f32[5,180]{1,0:T(8,128)S(1)}, f32[5,180]{1,0:T(8,128)S(1)}) all-reduce(f32[5,180]{1,0:T(8,128)S(1)} %get-tuple-element.85, f32[5,180]{1,0:T(8,128)S(1)} %get-tuple-element.103), channel_id=1, replica_groups=mesh['lat'=16,'ch'=8] {'ch'}, use_global_device_ids=true, to_apply=%region_71.72 | all-reduce | flops 1800 | bytes 14400 | tf_op jit(solution)/shard_map/psum | solution.py:116
  1953.6 26.0 %all-reduce.76.cloned.1.call-done = (f32[4,2,1,48,48]{3,4,1,2,0:T(8,128)}, f32[4,2,1,48,48]{3,4,1,2,0:T(8,128)}, f32[4,384,192]{1,2,0:T(8,128)}, f32[4,192,384]{2,1,0:T(8,128)}) async-done(((f32[4,2,1,48,48]{3,4,1,2,0:T(8,128)}, f32[4,2,1,48,48]{3,4,1,2,0:T(8,128)}, f32[4,384,192]{1,2,0:T(8,128)}, f32[4,192,384]{2,1,0:T(8,128)}), (f32[4,2,1,48,48]{3,4,1,2,0:T(8,128)}, f32[4,2,1,48,48]{3,4,1,2,0:T(8,128)}, ...) | async-done | bytes 2506768 | tf_op jit(solution)/shard_map/psum | solution.py:299
  (847 shorter events, 342.8 us)
Async XLA Ops:
  7.2 42.7 %copy-start.1 = (f32[48,5,180]{2,0,1:T(8,128)S(1)}, f32[48,5,180]{2,0,1:T(8,128)}, u32[]{:S(2)}) copy-start(f32[48,5,180]{2,0,1:T(8,128)} %param.16) | copy-start | bytes 518404
  9.3 82.4 %copy-start.151 = (f32[48]{0:T(128)}, f32[48]{0:T(128)S(1)}, u32[]{:S(2)}) copy-start(f32[48]{0:T(128)S(1)} %get-tuple-element.259) | copy-start | bytes 580
  9.3 265.5 %copy-start.153 = (f32[48]{0:T(128)}, f32[48]{0:T(128)S(1)}, u32[]{:S(2)}) copy-start(f32[48]{0:T(128)S(1)} %get-tuple-element.258) | copy-start | bytes 580
  10.7 264.1 %copy-start.165 = (f32[48]{0:T(128)}, f32[48]{0:T(128)S(1)}, u32[]{:S(2)}) copy-start(f32[48]{0:T(128)S(1)} %get-tuple-element.262) | copy-start | bytes 580
  12.9 51.0 %copy-start.169 = (f32[4,2,1,48]{3,2,1,0:T(1,128)S(1)}, f32[4,2,1,48]{3,2,1,0:T(1,128)}, u32[]{:S(2)}) copy-start(f32[4,2,1,48]{3,2,1,0:T(1,128)} %param.21) | copy-start | bytes 4612
  12.9 51.6 %copy-start.170 = (f32[4,2,1,48]{3,2,1,0:T(1,128)S(1)}, f32[4,2,1,48]{3,2,1,0:T(1,128)}, u32[]{:S(2)}) copy-start(f32[4,2,1,48]{3,2,1,0:T(1,128)} %param.23) | copy-start | bytes 4612
  12.9 52.2 %copy-start.171 = (f32[4,192]{1,0:T(4,128)S(1)}, f32[4,192]{1,0:T(4,128)}, u32[]{:S(2)}) copy-start(f32[4,192]{1,0:T(4,128)} %param.27) | copy-start | bytes 9220
  49.8 41.9 %copy-start.109 = (f32[5,180]{1,0:T(8,128)}, f32[5,180]{1,0:T(8,128)S(1)}, u32[]{:S(2)}) copy-start(f32[5,180]{1,0:T(8,128)S(1)} %get-tuple-element.223) | copy-start | bytes 10804
  49.8 41.9 %copy-start.111 = (f32[5,180]{1,0:T(8,128)}, f32[5,180]{1,0:T(8,128)S(1)}, u32[]{:S(2)}) copy-start(f32[5,180]{1,0:T(8,128)S(1)} %get-tuple-element.224) | copy-start | bytes 10804
  51.5 18.4 all-to-all-start
  66.5 56.2 %copy-start.159 = (f32[48]{0:T(128)}, f32[48]{0:T(128)S(1)}, u32[]{:S(2)}) copy-start(f32[48]{0:T(128)S(1)} %get-tuple-element.251) | copy-start | bytes 580
  80.6 10.1 all-to-all-start.1
  84.5 156.6 %reduce-scatter.9.cloned.1.call-start = ((), (), s32[]{:S(2)}) async-start(), calls=%async_computation.24 | async-start | bytes 1769472 | tf_op jit(solution)/shard_map/reduce_scatter | solution.py:188
  92.5 148.7 %copy-start.2 = (f32[48,5,180]{2,0,1:T(8,128)}, f32[48,5,180]{2,0,1:T(8,128)S(1)}, u32[]{:S(2)}) copy-start(f32[48,5,180]{2,0,1:T(8,128)S(1)} %get-tuple-element.273) | copy-start | bytes 518404
  122.6 34.7 %copy-start.129 = (f32[5,180]{1,0:T(8,128)}, f32[5,180]{1,0:T(8,128)S(1)}, u32[]{:S(2)}) copy-start(f32[5,180]{1,0:T(8,128)S(1)} %get-tuple-element.221) | copy-start | bytes 10804
  122.6 34.7 %copy-start.131 = (f32[5,180]{1,0:T(8,128)}, f32[5,180]{1,0:T(8,128)S(1)}, u32[]{:S(2)}) copy-start(f32[5,180]{1,0:T(8,128)S(1)} %get-tuple-element.222) | copy-start | bytes 10804
  161.5 304.9 %reduce-scatter.11.cloned.1.call-start = ((), (), s32[]{:S(2)}) async-start(), calls=%async_computation.25 | async-start | bytes 1769472 | tf_op jit(solution)/shard_map/reduce_scatter | solution.py:188
  242.2 73.2 %copy-start.4 = (f32[48,5,180]{2,0,1:T(8,128)}, f32[48,5,180]{2,0,1:T(8,128)S(1)}, u32[]{:S(2)}) copy-start(f32[48,5,180]{2,0,1:T(8,128)S(1)} %get-tuple-element.188) | copy-start | bytes 518404
  274.8 40.6 %copy-start.113 = (f32[5,180]{1,0:T(8,128)}, f32[5,180]{1,0:T(8,128)S(1)}, u32[]{:S(2)}) copy-start(f32[5,180]{1,0:T(8,128)S(1)} %get-tuple-element.219) | copy-start | bytes 10804
  274.8 40.6 %copy-start.115 = (f32[5,180]{1,0:T(8,128)}, f32[5,180]{1,0:T(8,128)S(1)}, u32[]{:S(2)}) copy-start(f32[5,180]{1,0:T(8,128)S(1)} %get-tuple-element.220) | copy-start | bytes 10804
  304.8 41.5 %copy-start.161 = (f32[48]{0:T(128)S(1)}, f32[48]{0:T(128)}, u32[]{:S(2)}) copy-start(f32[48]{0:T(128)} %get-tuple-element.250) | copy-start | bytes 580
  304.8 41.5 %copy-start.197 = (f32[48]{0:T(128)S(1)}, f32[48]{0:T(128)}, u32[]{:S(2)}) copy-start(f32[48]{0:T(128)} %get-tuple-element.254) | copy-start | bytes 580
  315.4 63.3 %copy-start.168 = (f32[1,192]{1,0:T(1,128)S(1)}, f32[1,192]{1,0:T(1,128)}, u32[]{:S(2)}) copy-start(f32[1,192]{1,0:T(1,128)} %get-tuple-element.226) | copy-start | bytes 2308
  316.2 150.2 %copy-start.6 = (f32[48,5,180]{2,0,1:T(8,128)}, f32[48,5,180]{2,0,1:T(8,128)S(1)}, u32[]{:S(2)}) copy-start(f32[48,5,180]{2,0,1:T(8,128)S(1)} %get-tuple-element.280) | copy-start | bytes 518404
  346.3 34.7 %copy-start.133 = (f32[5,180]{1,0:T(8,128)}, f32[5,180]{1,0:T(8,128)S(1)}, u32[]{:S(2)}) copy-start(f32[5,180]{1,0:T(8,128)S(1)} %get-tuple-element.217) | copy-start | bytes 10804
  346.3 34.7 %copy-start.135 = (f32[5,180]{1,0:T(8,128)}, f32[5,180]{1,0:T(8,128)S(1)}, u32[]{:S(2)}) copy-start(f32[5,180]{1,0:T(8,128)S(1)} %get-tuple-element.218) | copy-start | bytes 10804
  386.8 79.6 %copy-start.198 = (f32[48]{0:T(128)S(1)}, f32[48]{0:T(128)}, u32[]{:S(2)}) copy-start(f32[48]{0:T(128)} %get-tuple-element.246) | copy-start | bytes 580
  386.8 112.9 %copy-start.156 = (f32[48]{0:T(128)S(1)}, f32[48]{0:T(128)}, u32[]{:S(2)}) copy-start(f32[48]{0:T(128)} %get-tuple-element.260) | copy-start | bytes 580
  386.8 112.9 %copy-start.164 = (f32[48]{0:T(128)S(1)}, f32[48]{0:T(128)}, u32[]{:S(2)}) copy-start(f32[48]{0:T(128)} %get-tuple-element.264) | copy-start | bytes 580
  386.8 314.2 %reduce-scatter.13.cloned.1.call-start = ((), (), s32[]{:S(2)}) async-start(), calls=%async_computation.26 | async-start | bytes 1769472 | tf_op jit(solution)/shard_map/reduce_scatter | solution.py:188
  467.5 81.3 %copy-start.8 = (f32[48,5,180]{2,0,1:T(8,128)}, f32[48,5,180]{2,0,1:T(8,128)S(1)}, u32[]{:S(2)}) copy-start(f32[48,5,180]{2,0,1:T(8,128)S(1)} %get-tuple-element.187) | copy-start | bytes 518404
  538.2 42.8 %copy-start.163 = (f32[48]{0:T(128)S(1)}, f32[48]{0:T(128)}, u32[]{:S(2)}) copy-start(f32[48]{0:T(128)} %get-tuple-element.252) | copy-start | bytes 580
  538.2 42.8 %copy-start.196 = (f32[48]{0:T(128)S(1)}, f32[48]{0:T(128)}, u32[]{:S(2)}) copy-start(f32[48]{0:T(128)} %get-tuple-element.256) | copy-start | bytes 580
  792.2 38.4 %all-to-all-start.7 = ((f32[16,1,1920]{2,1,0:T(1,128)}), f32[16,1,1920]{2,1,0:T(1,128)}, u32[]{:S(2)}, u32[]{:S(2)}) async-start(f32[16,1,1920]{2,1,0:T(1,128)} %reshape.1495), calls=%async_computation.10 | async-start | bytes 245760 | tf_op jit(solution)/shard_map/all_to_all | solution.py:124
  796.7 204.7 %reduce-scatter.17.cloned.1.call-start = ((), (), s32[]{:S(2)}) async-start(), calls=%async_computation.28 | async-start | bytes 1769472 | tf_op jit(solution)/shard_map/reduce_scatter | solution.py:239
  871.6 34.9 %copy-start.54 = (bf16[4,384,192]{1,2,0:T(8,128)(2,1)S(1)}, bf16[4,384,192]{1,2,0:T(8,128)(2,1)}, u32[]{:S(2)}) copy-start(bf16[4,384,192]{1,2,0:T(8,128)(2,1)} %param.26) | copy-start | bytes 1769476
  871.6 34.9 %copy-start.167 = (f32[1,192]{1,0:T(1,128)S(1)}, f32[1,192]{1,0:T(1,128)}, u32[]{:S(2)}) copy-start(f32[1,192]{1,0:T(1,128)} %get-tuple-element.225) | copy-start | bytes 2308
  872.4 34.1 %copy-start.139 = (f32[5,180]{1,0:T(8,128)}, f32[5,180]{1,0:T(8,128)S(1)}, u32[]{:S(2)}) copy-start(f32[5,180]{1,0:T(8,128)S(1)} %get-tuple-element.209) | copy-start | bytes 10804
  872.4 34.1 %copy-start.140 = (f32[5,180]{1,0:T(8,128)}, f32[5,180]{1,0:T(8,128)S(1)}, u32[]{:S(2)}) copy-start(f32[5,180]{1,0:T(8,128)S(1)} %get-tuple-element.210) | copy-start | bytes 10804
  915.3 161.7 %reduce-scatter.15.cloned.1.call-start = ((), (), s32[]{:S(2)}) async-start(), calls=%async_computation.27 | async-start | bytes 1769472 | tf_op jit(solution)/shard_map/reduce_scatter | solution.py:188
  1084.8 12.5 all-to-all-start.8
  1127.6 10.8 all-to-all-start.9
  1132.1 172.2 %reduce-scatter.19.cloned.1.call-start = ((), (), s32[]{:S(2)}) async-start(), calls=%async_computation.29 | async-start | bytes 1769472 | tf_op jit(solution)/shard_map/reduce_scatter | solution.py:239
  1181.3 33.3 %copy-start.99 = (f32[192,5,180]{0,2,1:T(8,128)S(1)}, f32[192,5,180]{0,2,1:T(8,128)}, u32[]{:S(2)}) copy-start(f32[192,5,180]{0,2,1:T(8,128)} %get-tuple-element.289) | copy-start | bytes 2073604
  1348.1 20.5 %all-to-all-start.10 = ((f32[16,1,1920]{2,1,0:T(1,128)}), f32[16,1,1920]{2,1,0:T(1,128)}, u32[]{:S(2)}, u32[]{:S(2)}) async-start(f32[16,1,1920]{2,1,0:T(1,128)} %reshape.1501), calls=%async_computation.16 | async-start | bytes 245760 | tf_op jit(solution)/shard_map/all_to_all | solution.py:120
  1386.5 10.8 all-to-all-start.11
  1391.0 165.7 %reduce-scatter.21.cloned.1.call-start = ((), (), s32[]{:S(2)}) async-start(), calls=%async_computation.30 | async-start | bytes 1769472 | tf_op jit(solution)/shard_map/reduce_scatter | solution.py:239
  1434.7 34.1 %copy-start.98 = (f32[192,5,180]{0,2,1:T(8,128)S(1)}, f32[192,5,180]{0,2,1:T(8,128)}, u32[]{:S(2)}) copy-start(f32[192,5,180]{0,2,1:T(8,128)} %get-tuple-element.282) | copy-start | bytes 2073604
  1481.3 75.4 %copy-start.7 = (f32[48,5,180]{2,0,1:T(8,128)S(1)}, f32[48,5,180]{2,0,1:T(8,128)}, u32[]{:S(2)}) copy-start(f32[48,5,180]{2,0,1:T(8,128)} %copy-done.6) | copy-start | bytes 518404
  1481.3 75.4 %copy-start.134 = (f32[5,180]{1,0:T(8,128)S(1)}, f32[5,180]{1,0:T(8,128)}, u32[]{:S(2)}) copy-start(f32[5,180]{1,0:T(8,128)} %copy-done.133) | copy-start | bytes 10804
  1481.3 75.4 %copy-start.136 = (f32[5,180]{1,0:T(8,128)S(1)}, f32[5,180]{1,0:T(8,128)}, u32[]{:S(2)}) copy-start(f32[5,180]{1,0:T(8,128)} %copy-done.135) | copy-start | bytes 10804
  1481.4 75.4 %copy-start.162 = (f32[48]{0:T(128)S(1)}, f32[48]{0:T(128)}, u32[]{:S(2)}) copy-start(f32[48]{0:T(128)} %get-tuple-element.250) | copy-start | bytes 580
  1484.3 106.9 %copy-start.57 = (f32[48,5,180]{2,0,1:T(8,128)S(1)}, f32[48,5,180]{2,0,1:T(8,128)}, u32[]{:S(2)}) copy-start(f32[48,5,180]{2,0,1:T(8,128)} %copy-done.56) | copy-start | bytes 518404
  1595.6 20.1 %all-to-all-start.12 = ((f32[16,1,1920]{2,1,0:T(1,128)}), f32[16,1,1920]{2,1,0:T(1,128)S(1)}, u32[]{:S(2)}, u32[]{:S(2)}) async-start(f32[16,1,1920]{2,1,0:T(1,128)} %reshape.1505), calls=%async_computation.19 | async-start | bytes 245760 | tf_op jit(solution)/shard_map/all_to_all | solution.py:120
  1629.2 10.1 all-to-all-start.13
  1633.1 159.2 %reduce-scatter.23.cloned.1.call-start = ((), (), s32[]{:S(2)}) async-start(), calls=%async_computation.31 | async-start | bytes 1769472 | tf_op jit(solution)/shard_map/reduce_scatter | solution.py:239
  1671.8 32.2 %copy-start.97 = (f32[192,5,180]{0,2,1:T(8,128)S(1)}, f32[192,5,180]{0,2,1:T(8,128)}, u32[]{:S(2)}) copy-start(f32[192,5,180]{0,2,1:T(8,128)} %get-tuple-element.275) | copy-start | bytes 2073604
  1721.3 71.0 %copy-start.3 = (f32[48,5,180]{2,0,1:T(8,128)S(1)}, f32[48,5,180]{2,0,1:T(8,128)}, u32[]{:S(2)}) copy-start(f32[48,5,180]{2,0,1:T(8,128)} %copy-done.2) | copy-start | bytes 518404
  1721.3 71.0 %copy-start.130 = (f32[5,180]{1,0:T(8,128)S(1)}, f32[5,180]{1,0:T(8,128)}, u32[]{:S(2)}) copy-start(f32[5,180]{1,0:T(8,128)} %copy-done.129) | copy-start | bytes 10804
  1721.3 71.0 %copy-start.132 = (f32[5,180]{1,0:T(8,128)S(1)}, f32[5,180]{1,0:T(8,128)}, u32[]{:S(2)}) copy-start(f32[5,180]{1,0:T(8,128)} %copy-done.131) | copy-start | bytes 10804
  1721.3 71.0 %copy-start.160 = (f32[48]{0:T(128)S(1)}, f32[48]{0:T(128)}, u32[]{:S(2)}) copy-start(f32[48]{0:T(128)} %copy-done.159) | copy-start | bytes 580
  1827.4 20.1 %all-to-all-start.14 = ((f32[16,1,1920]{2,1,0:T(1,128)}), f32[16,1,1920]{2,1,0:T(1,128)S(1)}, u32[]{:S(2)}, u32[]{:S(2)}) async-start(f32[16,1,1920]{2,1,0:T(1,128)} %reshape.1509), calls=%async_computation.22 | async-start | bytes 245760 | tf_op jit(solution)/shard_map/all_to_all | solution.py:120
  1841.5 138.1 %all-reduce.76.cloned.1.call-start = ((), (), s32[]{:S(2)}) async-start(), calls=%async_computation.32 | async-start | bytes 5505024 | tf_op jit(solution)/shard_map/psum | solution.py:299
  1860.0 10.0 all-to-all-start.15
  (164 other events, 953.6 us)
Sparse Core Ops, SparseCore 0:
  161.6 79.4 reduce-scatter.8
  386.9 79.3 reduce-scatter.10
  620.8 80.2 reduce-scatter.12
  915.5 85.8 reduce-scatter.16
  1004.9 72.0 reduce-scatter.14
  1222.8 81.4 reduce-scatter.18
  1476.3 80.3 reduce-scatter.20
  1712.0 80.2 reduce-scatter.22
  1856.8 122.7 all-reduce.75
where the time goes:
time: 2010 us; the launch traced here: 1990 us
  blocking collectives  898 us (45%)
  waiting for transfers between devices  635 us (32%)
  matrix products  166 us (8%)
  local copies, waits for them, and re-layouts  114 us (6%)
  starting transfers between devices  87.3 us (4%)
  other arithmetic  73.9 us (4%)
    reduce_scatter x4, waiting for transfers between devices, body(): lax.psum_scatter(jnp.einsum('frw,cf->crw', pre_round, up_layer, preferred...  288 us
    reduce_scatter x4, waiting for transfers between devices, body(): lax.psum_scatter(jnp.einsum('frw,fc->crw', hidden_act, down_layer, prefer...  276 us
    psum x8, blocking collectives, norm_sums(): lax.psum((jnp.sum(values, axis=0), jnp.sum(values * values, axis=0)), 'ch')  258 us
    psum x8, blocking collectives, norm_back_sums(): lax.psum((jnp.sum(scaled_grad, axis=0), jnp.sum(scaled_grad * normed, axi...  254 us
    all_gather x4, blocking collectives, body(): lifted = lax.all_gather(lifted_part, 'ch', axis=0, tiled=True)  129 us
    all_gather x4, blocking collectives, body(): lax.all_gather(grad_now.astype(jnp.bfloat16), 'ch', axis=0, tiled=True)  127 us
    all_to_all x5, starting transfers between devices, to_modes(): lax.all_to_all(values, 'lat', split_axis=2, concat_axis=1, tiled=True)  61.1 us
    all_to_all x3, blocking collectives, to_modes(): lax.all_to_all(values, 'lat', split_axis=2, concat_axis=1, tiled=True)  60.7 us
  transfers between devices with their start and end apart: 20, of which 19 were waited for; matrix products, arithmetic and copies ran while one was open for 3% of the time, Pallas kernels for 0%

commit v1 on v0

v1 whole, which is shorter than its diff:
```python
import functools
import math

import jax
import jax.numpy as jnp
from jax import lax
from jax.experimental import pallas as pl
from jax.experimental.pallas import tpu as pltpu
from jax.sharding import PartitionSpec as P

shrink_level = 0.01
norm_eps = 1e-05
highest = lax.Precision.HIGHEST
MESH = pl.DeviceIdType.MESH


def gelu_exact(values):
    return 0.5 * values * (1.0 + lax.erf(values * 0.7071067811865476))


def gelu_slope(values):
    return (
        0.5 * (1.0 + lax.erf(values * 0.7071067811865476))
        + values * jnp.exp(-0.5 * values * values) * 0.3989422804014327
    )


def soft_shrink(values):
    return values - shrink_level * jnp.tanh(values / shrink_level)


def push_kernel(axis, n, scatters, *refs):
    count = len(scatters)
    sources, targets = refs[:count], refs[count : 2 * count]
    send_sem, recv_sem, own_sem = refs[2 * count :]
    me = lax.axis_index(axis)
    barrier = pltpu.get_barrier_semaphore()
    for step in range(1, n):
        pl.semaphore_signal(
            barrier, inc=1, device_id={axis: lax.rem(me + step, n)}, device_id_type=MESH
        )
    own = []
    for at, scatter in enumerate(scatters):
        block = sources[at].at[me] if scatter else sources[at]
        copy = pltpu.make_async_copy(block, targets[at].at[me], own_sem.at[at])
        copy.start()
        own.append(copy)
    pl.semaphore_wait(barrier, n - 1)
    copies = []
    for step in range(1, n):
        peer = lax.rem(me + step, n)
        for at, scatter in enumerate(scatters):
            block = sources[at].at[peer] if scatter else sources[at]
            copy = pltpu.make_async_remote_copy(
                src_ref=block,
                dst_ref=targets[at].at[me],
                send_sem=send_sem.at[at, step],
                recv_sem=recv_sem.at[at, step],
                device_id={axis: peer},
                device_id_type=MESH,
            )
            copy.start()
            copies.append(copy)
    for copy in own + copies:
        copy.wait()


def push(axis, ident, arrays, scatters):
    n = lax.axis_size(axis)
    shapes = [
        jax.ShapeDtypeStruct(a.shape if s else (n,) + a.shape, a.dtype)
        for a, s in zip(arrays, scatters)
    ]
    count = len(arrays)
    return pl.pallas_call(
        functools.partial(push_kernel, axis, n, scatters),
        out_shape=shapes,
        in_specs=[pl.BlockSpec(memory_space=pltpu.VMEM)] * count,
        out_specs=[pl.BlockSpec(memory_space=pltpu.VMEM)] * count,
        scratch_shapes=[
            pltpu.SemaphoreType.DMA((count, n)),
            pltpu.SemaphoreType.DMA((count, n)),
            pltpu.SemaphoreType.DMA((count,)),
        ],
        compiler_params=pltpu.CompilerParams(collective_id=ident, has_side_effects=True),
    )(*arrays)


def block_mlp(values, weight_in, bias_in, weight_out, bias_out):
    def mix(part, weight, bias_pair):
        re, im = part[:, 0], part[:, 1]
        out_re = jnp.einsum("kim,ij->kjm", re, weight[0], precision=highest) - jnp.einsum(
            "kim,ij->kjm", im, weight[1], precision=highest
        )
        out_im = jnp.einsum("kim,ij->kjm", im, weight[0], precision=highest) + jnp.einsum(
            "kim,ij->kjm", re, weight[1], precision=highest
        )
        return jnp.stack(
            [out_re + bias_pair[0][:, None], out_im + bias_pair[1][:, None]], axis=1
        )

    inner = gelu_exact(mix(values, weight_in, bias_in))
    return soft_shrink(mix(inner, weight_out, bias_out))


def spectral_local(spectrum, weight_in, bias_in, weight_out, bias_out, lat_matrix):
    groups, pairs, _ = spectrum.shape
    modes = lat_matrix.shape[1]
    rows = lat_matrix.shape[4]
    paired = spectrum.reshape(groups, pairs // 2, 2, -1, rows)
    mode = jnp.einsum("xmsyr,skycr->kxcm", lat_matrix, paired, precision=highest)
    out = block_mlp(mode, weight_in[:, 0], bias_in[:, 0], weight_out[:, 0], bias_out[:, 0])
    back = jnp.einsum("xmsyr,kxcm->skycr", lat_matrix, out, precision=highest)
    return back.reshape(spectrum.shape)


def lat_matrix_of(cos_lat, sin_lat, groups):
    modes, cells = cos_lat.shape
    rows = cells // groups
    both = jnp.stack(
        [jnp.stack([cos_lat, sin_lat], axis=1), jnp.stack([-sin_lat, cos_lat], axis=1)], axis=0
    )
    return jnp.transpose(both.reshape(2, modes, 2, groups, rows), (0, 1, 3, 2, 4))


def block_sums(values):
    return jnp.stack([jnp.sum(values, axis=0), jnp.sum(values * values, axis=0)])


def to_modes(values, table, groups):
    moved = jnp.einsum("crw,wp->pcr", values, table, precision=highest)
    pairs = table.shape[1] // groups
    return push("lat", 0, [moved.reshape(groups, pairs, -1)], [True])[0]


def to_rows(values, table, shape):
    moved = push("lat", 0, [values], [True])[0]
    chan_count, row_count, _ = shape
    return jnp.einsum(
        "pcr,pw->crw", moved.reshape(-1, chan_count, row_count), table, precision=highest
    )


def lat_tables(kept_lat, lat_cells):
    cell_index = jnp.arange(lat_cells, dtype=jnp.int32)
    phase_index = kept_lat[:, None] * cell_index[None, :] % lat_cells
    angles = phase_index.astype(jnp.float32) * (2.0 * math.pi / lat_cells)
    norm_scale = 1.0 / math.sqrt(lat_cells)
    return (jnp.cos(angles) * norm_scale, jnp.sin(angles) * norm_scale)


def lon_tables(kept_lon, lon_cells):
    cell_index = jnp.arange(lon_cells, dtype=jnp.int32)
    phase_index = kept_lon[:, None] * cell_index[None, :] % lon_cells
    angles = phase_index.astype(jnp.float32) * (2.0 * math.pi / lon_cells)
    norm_scale = 1.0 / math.sqrt(lon_cells)
    mode_weight = jnp.where((kept_lon == 0) | (2 * kept_lon == lon_cells), 1.0, 2.0).astype(
        jnp.float32
    )[:, None]
    forward_table = (
        jnp.stack([jnp.cos(angles), -jnp.sin(angles)], axis=1).reshape(-1, lon_cells).T * norm_scale
    )
    inverse_table = (
        jnp.stack([jnp.cos(angles) * mode_weight, -jnp.sin(angles) * mode_weight], axis=1).reshape(
            -1, lon_cells
        )
        * norm_scale
    )
    return (forward_table, inverse_table)


def body(
    inputs,
    cotangent,
    first_gain,
    first_shift,
    filter_inner,
    filter_inner_bias,
    filter_outer,
    filter_outer_bias,
    second_gain,
    second_shift,
    up_weight,
    up_bias,
    down_weight,
    down_bias,
    kept_lat,
    kept_lon,
):
    shape = inputs.shape
    chan_count, row_count, lon_cells = shape
    cells = row_count * lon_cells
    groups = lax.axis_size("lat")
    blocks = lax.axis_size("ch")
    lat_cells = row_count * groups
    channel_total = chan_count * blocks
    layer_count = first_gain.shape[0]
    lon_forward, lon_inverse = lon_tables(kept_lon, lon_cells)
    cos_lat, sin_lat = lat_tables(kept_lat, lat_cells)
    lat_matrix = lat_matrix_of(cos_lat, sin_lat, groups)
    gathered_gain = push(
        "ch", 1, [jnp.stack([second_gain, second_shift])], [False]
    )[0]
    full_gain = gathered_gain[:, 0].transpose(1, 0, 2)
    full_shift = gathered_gain[:, 1].transpose(1, 0, 2)

    current = inputs
    saved_layers = []
    for layer in range(layer_count):
        sums = push("ch", 2, [block_sums(current).reshape(2, cells)], [False])[0]
        sums = jnp.sum(sums, axis=0).reshape(2, row_count, lon_cells) / channel_total
        mean_one = sums[0]
        rstd_one = lax.rsqrt(sums[1] - mean_one * mean_one + norm_eps)
        normed_one = (current - mean_one) * rstd_one
        mixed_one = (
            normed_one * first_gain[layer][:, None, None] + first_shift[layer][:, None, None]
        )
        spectrum = to_modes(mixed_one, lon_forward, groups)
        filtered = spectral_local(
            spectrum,
            filter_inner[layer],
            filter_inner_bias[layer],
            filter_outer[layer],
            filter_outer_bias[layer],
            lat_matrix,
        )
        inner_field = current + mixed_one + to_rows(filtered, lon_inverse, shape)
        flat = inner_field.reshape(chan_count, cells)
        block_mean = jnp.mean(flat, axis=0)
        centered = flat - block_mean
        round_part = centered.astype(jnp.bfloat16)
        own_sums = jnp.stack([block_mean, jnp.sum(centered * centered, axis=0)])
        parts, sums = push("ch", 3, [round_part, own_sums], [False, False])
        means = sums[:, 0]
        mean_two = jnp.mean(means, axis=0)
        offsets = means - mean_two
        spread = jnp.mean(offsets * offsets, axis=0) + jnp.sum(sums[:, 1], axis=0) / channel_total
        rstd_two = lax.rsqrt(spread + norm_eps)
        full_normed = (parts.astype(jnp.float32) + offsets[:, None, :]) * rstd_two
        normed_two = (flat - mean_two) * rstd_two
        lifted = (
            (full_normed * full_gain[layer][:, :, None] + full_shift[layer][:, :, None])
            .astype(jnp.bfloat16)
            .reshape(channel_total, cells)
        )
        pre_act = (
            jnp.einsum("cn,cf->fn", lifted, up_weight[layer], preferred_element_type=jnp.float32)
            + up_bias[layer][:, None]
        )
        hidden_act = gelu_exact(pre_act).astype(jnp.bfloat16)
        partial = jnp.einsum(
            "fn,fc->cn", hidden_act, down_weight[layer], preferred_element_type=jnp.float32
        ).astype(jnp.bfloat16)
        pieces = push("ch", 4, [partial.reshape(blocks, chan_count, cells)], [True])[0]
        summed = jnp.sum(pieces.astype(jnp.float32), axis=0)
        current = (flat + summed + down_bias[layer][:, None]).reshape(shape)
        saved_layers.append(
            (
                normed_one,
                rstd_one,
                spectrum,
                normed_two,
                rstd_two,
                full_normed,
                lifted,
                pre_act,
                hidden_act,
            )
        )
    grad_now = cotangent
    collected = []
    for layer in reversed(range(layer_count)):
        (
            normed_one,
            rstd_one,
            spectrum,
            normed_two,
            rstd_two,
            full_normed,
            lifted,
            pre_act,
            hidden_act,
        ) = saved_layers[layer]
        flat_grad = grad_now.reshape(chan_count, cells)
        down_shift_grad = jnp.sum(flat_grad, axis=1)
        full_cot = push("ch", 5, [flat_grad.astype(jnp.bfloat16)], [False])[0]
        full_cot = full_cot.reshape(channel_total, cells)
        hidden_grad = jnp.einsum(
            "cn,fc->fn", full_cot, down_weight[layer], preferred_element_type=jnp.float32
        )
        down_grad = jnp.einsum(
            "fn,cn->fc", hidden_act, full_cot, preferred_element_type=jnp.float32
        )
        pre_grad = hidden_grad * gelu_slope(pre_act)
        pre_round = pre_grad.astype(jnp.bfloat16)
        up_shift_grad = jnp.sum(pre_grad, axis=1)
        up_grad = jnp.einsum("cn,fn->cf", lifted, pre_round, preferred_element_type=jnp.float32)
        partial = jnp.einsum(
            "fn,cf->cn", pre_round, up_weight[layer], preferred_element_type=jnp.float32
        ).reshape(blocks, chan_count, cells)
        scaled_part = partial * full_gain[layer][:, :, None]
        own_sums = jnp.stack(
            [
                jnp.sum(scaled_part, axis=(0, 1)),
                jnp.sum(scaled_part * full_normed, axis=(0, 1)),
            ]
        )
        pieces, sums = push("ch", 6, [partial.astype(jnp.bfloat16), own_sums], [True, False])
        lift_grad = jnp.sum(pieces.astype(jnp.float32), axis=0)
        gain_two_grad = jnp.sum(lift_grad * normed_two, axis=1)
        shift_two_grad = jnp.sum(lift_grad, axis=1)
        scaled_two = lift_grad * second_gain[layer][:, None]
        sums = jnp.sum(sums, axis=0) / channel_total
        inner_grad = (
            flat_grad + rstd_two * (scaled_two - sums[0] - normed_two * sums[1])
        ).reshape(shape)
        mode_grad = to_modes(inner_grad, lon_inverse.T, groups)

        def local_filter(spec_in, weight_in, bias_in, weight_out, bias_out):
            return spectral_local(spec_in, weight_in, bias_in, weight_out, bias_out, lat_matrix)

        _, filter_vjp = jax.vjp(
            local_filter,
            spectrum,
            filter_inner[layer],
            filter_inner_bias[layer],
            filter_outer[layer],
            filter_outer_bias[layer],
        )
        spectrum_grad, first_w_grad, first_b_grad, second_w_grad, second_b_grad = filter_vjp(
            mode_grad
        )
        mixed_grad = inner_grad + to_rows(spectrum_grad, lon_forward.T, shape)
        gain_one_grad = jnp.sum(mixed_grad * normed_one, axis=(1, 2))
        shift_one_grad = jnp.sum(mixed_grad, axis=(1, 2))
        scaled_one = mixed_grad * first_gain[layer][:, None, None]
        own_sums = jnp.stack([jnp.sum(scaled_one, axis=0), jnp.sum(scaled_one * normed_one, axis=0)])
        sums = push("ch", 2, [own_sums.reshape(2, cells)], [False])[0]
        sums = jnp.sum(sums, axis=0).reshape(2, row_count, lon_cells) / channel_total
        grad_now = inner_grad + rstd_one * (scaled_one - sums[0] - normed_one * sums[1])
        layer_terms = (
            gain_one_grad,
            shift_one_grad,
            first_w_grad,
            first_b_grad,
            second_w_grad,
            second_b_grad,
            gain_two_grad,
            shift_two_grad,
            lax.psum(up_grad, "lat"),
            up_shift_grad,
            lax.psum(down_grad, "lat"),
            down_shift_grad,
        )
        collected.append(layer_terms)
    collected = collected[::-1]
    stacked = [jnp.stack([terms[position] for terms in collected]) for position in range(12)]
    small = [at for at in range(12) if at not in (8, 10)]
    packed = jnp.concatenate([stacked[at].reshape(-1) for at in small])
    packed = jnp.pad(packed, (0, -packed.size % 1024)).reshape(-1, 128)
    packed = jnp.sum(push("lat", 7, [packed], [False])[0], axis=0).reshape(-1)
    begin = 0
    for at in small:
        size = stacked[at].size
        stacked[at] = packed[begin : begin + size].reshape(stacked[at].shape)
        begin += size
    return (current, grad_now) + tuple(stacked)


def solution(mesh):
    placed = (
        P("ch", "lat", None),
        P("ch", "lat", None),
        P(None, "ch"),
        P(None, "ch"),
        P(None, None, "ch", None, None),
        P(None, None, "ch", None),
        P(None, None, "ch", None, None),
        P(None, None, "ch", None),
        P(None, "ch"),
        P(None, "ch"),
        P(None, None, "ch"),
        P(None, "ch"),
        P(None, "ch", None),
        P(None, "ch"),
        P(),
        P(),
    )
    return jax.shard_map(
        body,
        mesh=mesh,
        in_specs=placed,
        out_specs=(
            P("ch", "lat", None),
            P("ch", "lat", None),
            P(None, "ch"),
            P(None, "ch"),
            P(None, None, "ch", None, None),
            P(None, None, "ch", None),
            P(None, None, "ch", None, None),
            P(None, None, "ch", None),
            P(None, "ch"),
            P(None, "ch"),
            P(None, None, "ch"),
            P(None, "ch"),
            P(None, "ch", None),
            P(None, "ch"),
        ),
        check_vma=False,
    )
```

time: 2010 us -> 872 us (0.43)
  blocking collectives: 898 us -> 0 us
  waiting for transfers between devices: 635 us -> 0.02 us
  Pallas kernels: 0 us -> 537 us
  starting transfers between devices: 87.3 us -> 0.04 us
  matrix products: 166 us -> 110 us
    reduce_scatter x8 -> x0, waiting for transfers between devices: 564 us -> none  [the longest x4 288 us: body(): lax.psum_scatter(jnp.einsum('frw,cf->crw', pre_round, up_layer, preferred...]
    psum x17 -> x0, blocking collectives: 563 us -> none  [the longest x8 258 us: norm_sums(): lax.psum((jnp.sum(values, axis=0), jnp.sum(values * values, axis=0)), 'ch')]
    pallas_call x0 -> x42, Pallas kernels: none -> 537 us  [push(): pl.pallas_call(functools.partial(push_kernel, axis, n, scatters), out_sha...]
    all_gather x8 -> x0, blocking collectives: 256 us -> none  [the longest x4 129 us: body(): lifted = lax.all_gather(lifted_part, 'ch', axis=0, tiled=True)]
    all_to_all x11 -> x0, starting transfers between devices: 86.5 us -> none  [the longest x5 61.1 us: to_modes(): lax.all_to_all(values, 'lat', split_axis=2, concat_axis=1, tiled=True)]
    all_to_all x5 -> x0, blocking collectives: 79.1 us -> none  [the longest x3 60.7 us: to_modes(): lax.all_to_all(values, 'lat', split_axis=2, concat_axis=1, tiled=True)]
    dot_general x200 -> x152, matrix products: 166 us -> 110 us  [the longest x8 11.6 us: to_rows(): jnp.einsum('pcr,pw->crw', moved.reshape(-1, chan_count, row_count), table...]
    unnamed x468 -> x516, local copies, waits for them, and re-layouts: 60.3 us -> 11.2 us
  transfers between devices with their start and end apart: 20 -> 1, of which waited for: 19 -> 0; matrix products, arithmetic and copies ran while one was open for 3% -> 7% of each run, Pallas kernels for 0% -> 12%
where the time goes in v1:
time: 872 us; the launch traced here: 859 us
  Pallas kernels  537 us (62%)
  matrix products  110 us (13%)
  local copies, waits for them, and re-layouts  109 us (12%)
  other arithmetic  82.4 us (9%)
  between operations  19.8 us (2%)
    pallas_call x42, Pallas kernels, push(): pl.pallas_call(functools.partial(push_kernel, axis, n, scatters), out_sha...  537 us
    pallas_call x16, local copies, waits for them, and re-layouts, push(): pl.pallas_call(functools.partial(push_kernel, axis, n, scatters), out_sha...  26.4 us
  transfers between devices with their start and end apart: 1, of which 0 were waited for; matrix products, arithmetic and copies ran while one was open for 7% of the time, Pallas kernels for 12%

profile of v1, /device:TPU:1, one launch (start us, length us, event | category | flops | bytes accessed | tf_op | source)
XLA Modules:
  0.0 858.9 jit_solution(17561199133956890088)
XLA Ops:
  11.2 11.3 %shard_map.263 = f32[8,2,900]{2,1,0:T(2,128)} custom-call(f32[2,900]{1,0:T(2,128)} %pad_maximum_fusion.12.refs_0_), custom_call_target="tpu_custom_call" | custom-call | tf_op jit(solution)/shard_map/pallas_call | solution.py:75
  27.3 10.5 %shard_map.264 = f32[16,8,240]{2,1,0:T(8,128)} custom-call(f32[16,8,240]{2,1,0:T(8,128)} %copy.496.refs_0_), custom_call_target="tpu_custom_call" | custom-call | tf_op jit(solution)/shard_map/pallas_call | solution.py:75
  47.8 8.6 shard_map.265
  56.3 2.0 copy.507
  61.9 8.0 shard_map.267
  72.2 17.2 %shard_map.266 = (bf16[8,48,900]{2,1,0:T(8,128)(2,1)}, f32[8,2,900]{2,1,0:T(2,128)}) custom-call(bf16[48,900]{1,0:T(8,128)(2,1)} %subtract_convert_fusion.3.refs_0_, f32[2,900]{1,0:T(2,128)} %pad_maximum_fusion.13.refs_1_), custom_call_target="tpu_custom_call" | custom-call | tf_op jit(solution)/shard_map/pallas_call | solution.py:75
  95.0 2.2 multiply_convert_fusion.3
  100.5 15.0 %shard_map.268 = bf16[8,48,900]{2,1,0:T(8,128)(2,1)} custom-call(bf16[8,48,900]{2,1,0:T(8,128)(2,1)} %bitcast.1575), custom_call_target="tpu_custom_call" | custom-call | tf_op jit(solution)/shard_map/pallas_call | solution.py:75
  117.9 8.0 shard_map.269
  128.4 10.8 %shard_map.270 = f32[16,8,240]{2,1,0:T(8,128)} custom-call(f32[16,8,240]{2,1,0:T(8,128)} %fusion.95.refs_0_), custom_call_target="tpu_custom_call" | custom-call | tf_op jit(solution)/shard_map/pallas_call | solution.py:75
  146.2 8.3 shard_map.271
  161.3 16.4 %shard_map.272 = (bf16[8,48,900]{2,1,0:T(8,128)(2,1)}, f32[8,2,900]{2,1,0:T(2,128)}) custom-call(bf16[48,900]{1,0:T(8,128)(2,1)} %subtract_convert_fusion.2.refs_0_, f32[2,900]{1,0:T(2,128)} %pad_maximum_fusion.15.refs_1_), custom_call_target="tpu_custom_call" | custom-call | tf_op jit(solution)/shard_map/pallas_call | solution.py:75
  183.4 2.2 multiply_convert_fusion.2
  188.9 16.2 %shard_map.273 = bf16[8,48,900]{2,1,0:T(8,128)(2,1)} custom-call(bf16[8,48,900]{2,1,0:T(8,128)(2,1)} %bitcast.1576), custom_call_target="tpu_custom_call" | custom-call | tf_op jit(solution)/shard_map/pallas_call | solution.py:75
  207.6 8.0 shard_map.274
  218.1 10.2 %shard_map.275 = f32[16,8,240]{2,1,0:T(8,128)} custom-call(f32[16,8,240]{2,1,0:T(8,128)} %fusion.93.refs_0_), custom_call_target="tpu_custom_call" | custom-call | tf_op jit(solution)/shard_map/pallas_call | solution.py:75
  235.5 8.3 shard_map.276
  243.7 2.0 copy.545
  250.6 18.0 %shard_map.277 = (bf16[8,48,900]{2,1,0:T(8,128)(2,1)}, f32[8,2,900]{2,1,0:T(2,128)}) custom-call(bf16[48,900]{1,0:T(8,128)(2,1)} %subtract_convert_fusion.1.refs_0_, f32[2,900]{1,0:T(2,128)} %pad_maximum_fusion.17.refs_1_), custom_call_target="tpu_custom_call" | custom-call | tf_op jit(solution)/shard_map/pallas_call | solution.py:75
  273.4 2.3 multiply_convert_fusion.1
  279.0 15.4 %shard_map.278 = bf16[8,48,900]{2,1,0:T(8,128)(2,1)} custom-call(bf16[8,48,900]{2,1,0:T(8,128)(2,1)} %bitcast.1577), custom_call_target="tpu_custom_call" | custom-call | tf_op jit(solution)/shard_map/pallas_call | solution.py:75
  296.9 8.0 shard_map.279
  307.9 10.4 %shard_map.280 = f32[16,8,240]{2,1,0:T(8,128)} custom-call(f32[16,8,240]{2,1,0:T(8,128)} %fusion.91.refs_0_), custom_call_target="tpu_custom_call" | custom-call | tf_op jit(solution)/shard_map/pallas_call | solution.py:75
  326.4 8.3 shard_map.281
  341.6 18.0 %shard_map.282 = (bf16[8,48,900]{2,1,0:T(8,128)(2,1)}, f32[8,2,900]{2,1,0:T(2,128)}) custom-call(bf16[48,900]{1,0:T(8,128)(2,1)} %subtract_convert_fusion.refs_0_, f32[2,900]{1,0:T(2,128)} %pad_maximum_fusion.19.refs_1_), custom_call_target="tpu_custom_call" | custom-call | tf_op jit(solution)/shard_map/pallas_call | solution.py:75
  362.6 15.1 %shard_map.284 = bf16[8,48,900]{2,1,0:T(8,128)(2,1)} custom-call(bf16[48,900]{1,0:T(8,128)(2,1)} %convert_element_type.217.refs_0_), custom_call_target="tpu_custom_call" | custom-call | tf_op jit(solution)/shard_map/pallas_call | solution.py:75
  384.6 2.5 multiply_reduce_fusion.7
  391.4 2.3 copy.567
  393.6 13.6 %shard_map.283 = bf16[8,48,900]{2,1,0:T(8,128)(2,1)} custom-call(bf16[8,48,900]{2,1,0:T(8,128)(2,1)} %bitcast.1578), custom_call_target="tpu_custom_call" | custom-call | tf_op jit(solution)/shard_map/pallas_call | solution.py:75
  409.4 14.5 %shard_map.285 = (bf16[8,48,900]{2,1,0:T(8,128)(2,1)}, f32[8,2,900]{2,1,0:T(2,128)}) custom-call(bf16[8,48,900]{2,1,0:T(8,128)(2,1)} %convert_element_type.219.refs_0_, f32[2,900]{1,0:T(2,128)} %pad_maximum_fusion.20.refs_1_), custom_call_target="tpu_custom_call" | custom-call | tf_op jit(solution)/shard_map/pallas_call | solution.py:75
  430.1 11.1 %shard_map.286 = f32[16,8,240]{2,1,0:T(8,128)} custom-call(f32[16,8,240]{2,1,0:T(8,128)} %fusion.89.refs_0_), custom_call_target="tpu_custom_call" | custom-call | tf_op jit(solution)/shard_map/pallas_call | solution.py:75
  448.9 8.3 shard_map.287
  460.8 2.3 multiply_reduce_fusion.12
  463.9 8.0 shard_map.288
  475.8 14.9 %shard_map.289 = bf16[8,48,900]{2,1,0:T(8,128)(2,1)} custom-call(bf16[48,900]{1,0:T(8,128)(2,1)} %convert_element_type.222.refs_0_), custom_call_target="tpu_custom_call" | custom-call | tf_op jit(solution)/shard_map/pallas_call | solution.py:75
  490.7 2.3 convolution_bitcast_fusion.16
  493.0 2.4 fusion.537
  496.6 2.5 multiply_reduce_fusion.6
  503.0 16.2 %shard_map.290 = (bf16[8,48,900]{2,1,0:T(8,128)(2,1)}, f32[8,2,900]{2,1,0:T(2,128)}) custom-call(bf16[8,48,900]{2,1,0:T(8,128)(2,1)} %convert_element_type.224.refs_0_, f32[2,900]{1,0:T(2,128)} %pad_maximum_fusion.22.refs_1_), custom_call_target="tpu_custom_call" | custom-call | tf_op jit(solution)/shard_map/pallas_call | solution.py:75
  519.2 2.0 convert_reduce_fusion.4
  525.3 9.8 %shard_map.291 = f32[16,8,240]{2,1,0:T(8,128)} custom-call(f32[16,8,240]{2,1,0:T(8,128)} %fusion.87.refs_0_), custom_call_target="tpu_custom_call" | custom-call | tf_op jit(solution)/shard_map/pallas_call | solution.py:75
  542.8 8.3 shard_map.292
  551.1 2.0 copy.615
  554.7 2.2 multiply_reduce_fusion.13
  557.7 8.1 shard_map.293
  570.2 14.9 %shard_map.294 = bf16[8,48,900]{2,1,0:T(8,128)(2,1)} custom-call(bf16[48,900]{1,0:T(8,128)(2,1)} %convert_element_type.227.refs_0_), custom_call_target="tpu_custom_call" | custom-call | tf_op jit(solution)/shard_map/pallas_call | solution.py:75
  585.2 2.3 convolution_bitcast_fusion.17
  587.5 2.4 fusion.538
  591.1 3.1 multiply_reduce_fusion.5
  598.8 16.4 %shard_map.295 = (bf16[8,48,900]{2,1,0:T(8,128)(2,1)}, f32[8,2,900]{2,1,0:T(2,128)}) custom-call(bf16[8,48,900]{2,1,0:T(8,128)(2,1)} %convert_element_type.229.refs_0_, f32[2,900]{1,0:T(2,128)} %pad_maximum_fusion.24.refs_1_), custom_call_target="tpu_custom_call" | custom-call | tf_op jit(solution)/shard_map/pallas_call | solution.py:75
  621.3 9.7 %shard_map.296 = f32[16,8,240]{2,1,0:T(8,128)} custom-call(f32[16,8,240]{2,1,0:T(8,128)} %fusion.85.refs_0_), custom_call_target="tpu_custom_call" | custom-call | tf_op jit(solution)/shard_map/pallas_call | solution.py:75
  638.0 8.3 shard_map.297
  649.9 2.3 multiply_reduce_fusion.14
  653.0 8.0 shard_map.298
  665.5 14.9 %shard_map.299 = bf16[8,48,900]{2,1,0:T(8,128)(2,1)} custom-call(bf16[48,900]{1,0:T(8,128)(2,1)} %convert_element_type.232.refs_0_), custom_call_target="tpu_custom_call" | custom-call | tf_op jit(solution)/shard_map/pallas_call | solution.py:75
  680.5 2.3 convolution_bitcast_fusion.18
  682.8 2.4 fusion.539
  709.3 2.1 multiply_reduce_fusion.4
  715.3 21.7 %shard_map.300 = (bf16[8,48,900]{2,1,0:T(8,128)(2,1)}, f32[8,2,900]{2,1,0:T(2,128)}) custom-call(bf16[8,48,900]{2,1,0:T(8,128)(2,1)} %convert_element_type.234.refs_0_, f32[2,900]{1,0:T(2,128)} %pad_maximum_fusion.26.refs_1_), custom_call_target="tpu_custom_call" | custom-call | tf_op jit(solution)/shard_map/pallas_call | solution.py:75
  741.3 11.6 %shard_map.301 = f32[16,8,240]{2,1,0:T(8,128)} custom-call(f32[16,8,240]{2,1,0:T(8,128)} %fusion.83.refs_0_), custom_call_target="tpu_custom_call" | custom-call | tf_op jit(solution)/shard_map/pallas_call | solution.py:75
  765.6 9.0 %shard_map.302 = f32[16,8,240]{2,1,0:T(8,128)} custom-call(f32[16,8,240]{2,1,0:T(8,128)} %copy.662.refs_0_), custom_call_target="tpu_custom_call" | custom-call | tf_op jit(solution)/shard_map/pallas_call | solution.py:75
  779.1 51.1 %shard_map.304 = f32[16,312,128]{2,1,0:T(8,128)} custom-call(f32[312,128]{1,0:T(8,128)} %pad_bitcast_fusion.refs_0_), custom_call_target="tpu_custom_call" | custom-call | tf_op jit(solution)/shard_map/pallas_call | solution.py:75
  833.1 9.1 %shard_map.303 = f32[8,2,900]{2,1,0:T(2,128)} custom-call(f32[2,900]{1,0:T(2,128)} %pad_maximum_fusion.27.refs_0_), custom_call_target="tpu_custom_call" | custom-call | tf_op jit(solution)/shard_map/pallas_call | solution.py:75
  848.3 2.4 pad_maximum_fusion
  (1016 shorter events, 251.2 us)
Async XLA Ops:
  7.2 16.4 %copy-start.251 = (f32[4,48]{1,0:T(4,128)S(1)}, f32[4,48]{1,0:T(4,128)}, u32[]{:S(2)}) copy-start(f32[4,48]{1,0:T(4,128)} %param.19) | copy-start | bytes 2308
  7.2 16.4 %copy-start.252 = (f32[4,48]{1,0:T(4,128)S(1)}, f32[4,48]{1,0:T(4,128)}, u32[]{:S(2)}) copy-start(f32[4,48]{1,0:T(4,128)} %param.18) | copy-start | bytes 2308
  7.2 841.1 %all-reduce.68.cloned.1.call-start = ((), (), s32[]{:S(2)}) async-start(), calls=%async_computation | async-start | bytes 4718592 | tf_op jit(solution)/shard_map/psum | solution.py:350
  9.3 16.5 %copy-start.32 = (f32[128,180]{1,0:T(8,128)}, f32[128,180]{1,0:T(8,128)S(1)}, u32[]{:S(2)}) copy-start(f32[128,180]{1,0:T(8,128)S(1)} %mul.1112) | copy-start | bytes 276484
  10.3 237.0 %copy-start.52 = (f32[128,180]{1,0:T(8,128)}, f32[128,180]{1,0:T(8,128)S(1)}, u32[]{:S(2)}) copy-start(f32[128,180]{1,0:T(8,128)S(1)} %mul.1135) | copy-start | bytes 276484
  23.5 35.8 %copy-start.130 = (f32[5,180]{1,0:T(8,128)}, f32[5,180]{1,0:T(8,128)S(1)}, u32[]{:S(2)}) copy-start(f32[5,180]{1,0:T(8,128)S(1)} %sub.380) | copy-start | bytes 10804
  23.6 35.8 %copy-start.132 = (f32[5,180]{1,0:T(8,128)}, f32[5,180]{1,0:T(8,128)S(1)}, u32[]{:S(2)}) copy-start(f32[5,180]{1,0:T(8,128)S(1)} %mul.1099) | copy-start | bytes 10804
  24.2 35.1 %copy-start.187 = (f32[48]{0:T(128)}, f32[48]{0:T(128)S(1)}, u32[]{:S(2)}) copy-start(f32[48]{0:T(128)S(1)} %get-tuple-element.268) | copy-start | bytes 580
  24.2 102.8 %copy-start.189 = (f32[48]{0:T(128)}, f32[48]{0:T(128)S(1)}, u32[]{:S(2)}) copy-start(f32[48]{0:T(128)S(1)} %get-tuple-element.269) | copy-start | bytes 580
  24.2 102.8 %copy-start.198 = (f32[48]{0:T(128)}, f32[48]{0:T(128)S(1)}, u32[]{:S(2)}) copy-start(f32[48]{0:T(128)S(1)} %get-tuple-element.222) | copy-start | bytes 580
  39.4 101.0 %copy-start.74 = (f32[1,60,1,16,5]{1,3,2,4,0:T(8,128)}, f32[1,60,1,16,5]{1,3,2,4,0:T(8,128)S(1)}, u32[]{:S(2)}) copy-start(f32[1,60,1,16,5]{1,3,2,4,0:T(8,128)S(1)} %get-tuple-element.186) | copy-start | bytes 57604
  39.5 101.0 %copy-start.77 = (f32[1,60,1,16,5]{1,3,2,4,0:T(8,128)}, f32[1,60,1,16,5]{1,3,2,4,0:T(8,128)S(1)}, u32[]{:S(2)}) copy-start(f32[1,60,1,16,5]{1,3,2,4,0:T(8,128)S(1)} %get-tuple-element.187) | copy-start | bytes 57604
  39.5 101.0 %copy-start.80 = (f32[1,60,1,16,5]{1,3,2,4,0:T(8,128)}, f32[1,60,1,16,5]{1,3,2,4,0:T(8,128)S(1)}, u32[]{:S(2)}) copy-start(f32[1,60,1,16,5]{1,3,2,4,0:T(8,128)S(1)} %get-tuple-element.188) | copy-start | bytes 57604
  59.7 57.2 %copy-start.5 = (f32[48,5,180]{2,0,1:T(8,128)}, f32[48,5,180]{2,0,1:T(8,128)S(1)}, u32[]{:S(2)}) copy-start(f32[48,5,180]{2,0,1:T(8,128)S(1)} %get-tuple-element.230) | copy-start | bytes 518404
  92.5 88.5 %copy-start.170 = (f32[1,8,48]{2,0,1:T(1,128)}, f32[1,8,48]{2,0,1:T(1,128)S(1)}, u32[]{:S(2)}) copy-start(f32[1,8,48]{2,0,1:T(1,128)S(1)} %get-tuple-element.180) | copy-start | bytes 4612
  92.5 179.3 %copy-start.171 = (f32[1,8,48]{2,0,1:T(1,128)}, f32[1,8,48]{2,0,1:T(1,128)S(1)}, u32[]{:S(2)}) copy-start(f32[1,8,48]{2,0,1:T(1,128)S(1)} %get-tuple-element.179) | copy-start | bytes 4612
  117.1 41.0 %copy-start.7 = (f32[48,5,180]{2,0,1:T(8,128)}, f32[48,5,180]{2,0,1:T(8,128)S(1)}, u32[]{:S(2)}) copy-start(f32[48,5,180]{2,0,1:T(8,128)S(1)} %get-tuple-element.146) | copy-start | bytes 518404
  126.9 31.3 %copy-start.134 = (f32[5,180]{1,0:T(8,128)}, f32[5,180]{1,0:T(8,128)S(1)}, u32[]{:S(2)}) copy-start(f32[5,180]{1,0:T(8,128)S(1)} %sub.395) | copy-start | bytes 10804
  127.0 31.2 %copy-start.135 = (f32[5,180]{1,0:T(8,128)}, f32[5,180]{1,0:T(8,128)S(1)}, u32[]{:S(2)}) copy-start(f32[5,180]{1,0:T(8,128)S(1)} %mul.1148) | copy-start | bytes 10804
  159.4 47.2 %copy-start.8 = (f32[48,5,180]{2,0,1:T(8,128)}, f32[48,5,180]{2,0,1:T(8,128)S(1)}, u32[]{:S(2)}) copy-start(f32[48,5,180]{2,0,1:T(8,128)S(1)} %get-tuple-element.234) | copy-start | bytes 518404
  159.8 23.5 %copy-start.201 = (f32[1,192]{1,0:T(1,128)S(1)}, f32[1,192]{1,0:T(1,128)}, u32[]{:S(2)}) copy-start(f32[1,192]{1,0:T(1,128)} %get-tuple-element.190) | copy-start | bytes 2308
  188.9 17.7 %copy-start.222 = (f32[48]{0:T(128)S(1)}, f32[48]{0:T(128)}, u32[]{:S(2)}) copy-start(f32[48]{0:T(128)} %get-tuple-element.277) | copy-start | bytes 580
  206.8 40.5 %copy-start.10 = (f32[48,5,180]{2,0,1:T(8,128)}, f32[48,5,180]{2,0,1:T(8,128)S(1)}, u32[]{:S(2)}) copy-start(f32[48,5,180]{2,0,1:T(8,128)S(1)} %get-tuple-element.145) | copy-start | bytes 518404
  216.6 30.7 %copy-start.136 = (f32[5,180]{1,0:T(8,128)}, f32[5,180]{1,0:T(8,128)S(1)}, u32[]{:S(2)}) copy-start(f32[5,180]{1,0:T(8,128)S(1)} %sub.410) | copy-start | bytes 10804
  216.7 30.7 %copy-start.138 = (f32[5,180]{1,0:T(8,128)}, f32[5,180]{1,0:T(8,128)S(1)}, u32[]{:S(2)}) copy-start(f32[5,180]{1,0:T(8,128)S(1)} %mul.1171) | copy-start | bytes 10804
  248.7 47.2 %copy-start.12 = (f32[48,5,180]{2,0,1:T(8,128)}, f32[48,5,180]{2,0,1:T(8,128)S(1)}, u32[]{:S(2)}) copy-start(f32[48,5,180]{2,0,1:T(8,128)S(1)} %get-tuple-element.238) | copy-start | bytes 518404
  249.1 24.3 %copy-start.200 = (f32[1,192]{1,0:T(1,128)S(1)}, f32[1,192]{1,0:T(1,128)}, u32[]{:S(2)}) copy-start(f32[1,192]{1,0:T(1,128)} %get-tuple-element.192) | copy-start | bytes 2308
  279.0 16.9 %copy-start.217 = (f32[48]{0:T(128)S(1)}, f32[48]{0:T(128)}, u32[]{:S(2)}) copy-start(f32[48]{0:T(128)} %get-tuple-element.275) | copy-start | bytes 580
  296.1 23.6 %copy-start.14 = (f32[48,5,180]{2,0,1:T(8,128)}, f32[48,5,180]{2,0,1:T(8,128)S(1)}, u32[]{:S(2)}) copy-start(f32[48,5,180]{2,0,1:T(8,128)S(1)} %get-tuple-element.144) | copy-start | bytes 518404
  338.3 23.3 %copy-start.186 = (f32[8,48]{1,0:T(8,128)S(1)}, f32[8,48]{1,0:T(8,128)}, u32[]{:S(2)}) copy-start(f32[8,48]{1,0:T(8,128)} %get-tuple-element.105) | copy-start | bytes 4612
  338.3 23.4 %copy-start.83 = (f32[48,5,180]{2,0,1:T(8,128)S(1)}, f32[48,5,180]{2,0,1:T(8,128)}, u32[]{:S(2)}) copy-start(f32[48,5,180]{2,0,1:T(8,128)} %param.17) | copy-start | bytes 518404
  340.2 37.8 %copy-start.173 = (f32[1,8,48]{2,0,1:T(1,128)S(1)}, f32[1,8,48]{2,0,1:T(1,128)}, u32[]{:S(2)}) copy-start(f32[1,8,48]{2,0,1:T(1,128)} %get-tuple-element.178) | copy-start | bytes 4612
  340.2 37.8 %copy-start.180 = (f32[1,8,48]{2,0,1:T(1,128)S(1)}, f32[1,8,48]{2,0,1:T(1,128)}, u32[]{:S(2)}) copy-start(f32[1,8,48]{2,0,1:T(1,128)} %get-tuple-element.274) | copy-start | bytes 4612
  359.6 18.3 %copy-start.67 = (bf16[8,48,900]{2,1,0:T(8,128)(2,1)S(1)}, bf16[8,48,900]{2,1,0:T(8,128)(2,1)}, u32[]{:S(2)}) copy-start(bf16[8,48,900]{2,1,0:T(8,128)(2,1)} %get-tuple-element.36) | copy-start | bytes 2073604
  361.7 16.6 %copy-start.199 = (f32[1,192]{1,0:T(1,128)S(1)}, f32[1,192]{1,0:T(1,128)}, u32[]{:S(2)}) copy-start(f32[1,192]{1,0:T(1,128)} %get-tuple-element.189) | copy-start | bytes 2308
  408.6 18.6 %copy-start.84 = (f32[48,5,180]{2,0,1:T(8,128)S(1)}, f32[48,5,180]{2,0,1:T(8,128)}, u32[]{:S(2)}) copy-start(f32[48,5,180]{2,0,1:T(8,128)} %param.17) | copy-start | bytes 518404
  408.6 18.6 %copy-start.211 = (f32[48]{0:T(128)S(1)}, f32[48]{0:T(128)}, u32[]{:S(2)}) copy-start(f32[48]{0:T(128)} %get-tuple-element.211) | copy-start | bytes 580
  408.6 18.6 %copy-start.212 = (f32[48]{0:T(128)S(1)}, f32[48]{0:T(128)}, u32[]{:S(2)}) copy-start(f32[48]{0:T(128)} %get-tuple-element.278) | copy-start | bytes 580
  429.0 14.2 %copy-start.35 = (f32[2,60,16,2,5,1]{1,2,3,4,0,5:T(8,128)S(1)}, f32[2,60,16,2,5,1]{1,2,3,4,0,5:T(8,128)}, u32[]{:S(2)}) copy-start(f32[2,60,16,2,5,1]{1,2,3,4,0,5:T(8,128)} %get-tuple-element.166) | copy-start | bytes 230404
  429.0 14.2 %copy-start.114 = (f32[4,1,48,60]{3,2,0,1:T(8,128)S(1)}, f32[4,1,48,60]{3,2,0,1:T(8,128)}, u32[]{:S(2)}) copy-start(f32[4,1,48,60]{3,2,0,1:T(8,128)} %copy-done.113) | copy-start | bytes 138244
  429.0 14.2 %copy-start.116 = (f32[4,1,48,60]{3,2,0,1:T(8,128)S(1)}, f32[4,1,48,60]{3,2,0,1:T(8,128)}, u32[]{:S(2)}) copy-start(f32[4,1,48,60]{3,2,0,1:T(8,128)} %copy-done.115) | copy-start | bytes 138244
  463.2 27.5 %copy-start.47 = (bf16[192,900]{1,0:T(8,128)(2,1)S(1)}, bf16[192,900]{1,0:T(8,128)(2,1)}, u32[]{:S(2)}) copy-start(bf16[192,900]{1,0:T(8,128)(2,1)} %copy-done.46) | copy-start | bytes 1036804
  474.9 18.1 %copy-start.119 = (f32[192,900]{1,0:T(8,128)S(1)}, f32[192,900]{1,0:T(8,128)}, u32[]{:S(2)}) copy-start(f32[192,900]{1,0:T(8,128)} %get-tuple-element.240) | copy-start | bytes 2073604
  502.3 20.2 %copy-start.13 = (f32[48,5,180]{2,0,1:T(8,128)S(1)}, f32[48,5,180]{2,0,1:T(8,128)}, u32[]{:S(2)}) copy-start(f32[48,5,180]{2,0,1:T(8,128)} %copy-done.12) | copy-start | bytes 518404
  502.3 20.2 %copy-start.176 = (f32[5,180]{1,0:T(8,128)S(1)}, f32[5,180]{1,0:T(8,128)}, u32[]{:S(2)}) copy-start(f32[5,180]{1,0:T(8,128)} %div.173) | copy-start | bytes 10804
  502.3 20.2 %copy-start.177 = (f32[5,180]{1,0:T(8,128)S(1)}, f32[5,180]{1,0:T(8,128)}, u32[]{:S(2)}) copy-start(f32[5,180]{1,0:T(8,128)} %rsqrt.81) | copy-start | bytes 10804
  502.4 20.2 %copy-start.210 = (f32[48]{0:T(128)S(1)}, f32[48]{0:T(128)}, u32[]{:S(2)}) copy-start(f32[48]{0:T(128)} %get-tuple-element.210) | copy-start | bytes 580
  556.9 28.2 %copy-start.45 = (bf16[192,900]{1,0:T(8,128)(2,1)S(1)}, bf16[192,900]{1,0:T(8,128)(2,1)}, u32[]{:S(2)}) copy-start(bf16[192,900]{1,0:T(8,128)(2,1)} %copy-done.44) | copy-start | bytes 1036804
  569.3 18.1 %copy-start.118 = (f32[192,900]{1,0:T(8,128)S(1)}, f32[192,900]{1,0:T(8,128)}, u32[]{:S(2)}) copy-start(f32[192,900]{1,0:T(8,128)} %get-tuple-element.236) | copy-start | bytes 2073604
  598.2 20.3 %copy-start.9 = (f32[48,5,180]{2,0,1:T(8,128)S(1)}, f32[48,5,180]{2,0,1:T(8,128)}, u32[]{:S(2)}) copy-start(f32[48,5,180]{2,0,1:T(8,128)} %copy-done.8) | copy-start | bytes 518404
  598.2 20.3 %copy-start.71 = (f32[48,5,180]{2,0,1:T(8,128)S(1)}, f32[48,5,180]{2,0,1:T(8,128)}, u32[]{:S(2)}) copy-start(f32[48,5,180]{2,0,1:T(8,128)} %copy-done.70) | copy-start | bytes 518404
  598.2 20.3 %copy-start.174 = (f32[5,180]{1,0:T(8,128)S(1)}, f32[5,180]{1,0:T(8,128)}, u32[]{:S(2)}) copy-start(f32[5,180]{1,0:T(8,128)} %div.177) | copy-start | bytes 10804
  598.2 20.3 %copy-start.175 = (f32[5,180]{1,0:T(8,128)S(1)}, f32[5,180]{1,0:T(8,128)}, u32[]{:S(2)}) copy-start(f32[5,180]{1,0:T(8,128)} %rsqrt.82) | copy-start | bytes 10804
  598.2 20.3 %copy-start.209 = (f32[48]{0:T(128)S(1)}, f32[48]{0:T(128)}, u32[]{:S(2)}) copy-start(f32[48]{0:T(128)} %get-tuple-element.212) | copy-start | bytes 580
  652.2 28.2 %copy-start.43 = (bf16[192,900]{1,0:T(8,128)(2,1)S(1)}, bf16[192,900]{1,0:T(8,128)(2,1)}, u32[]{:S(2)}) copy-start(bf16[192,900]{1,0:T(8,128)(2,1)} %copy-done.42) | copy-start | bytes 1036804
  664.6 18.1 %copy-start.117 = (f32[192,900]{1,0:T(8,128)S(1)}, f32[192,900]{1,0:T(8,128)}, u32[]{:S(2)}) copy-start(f32[192,900]{1,0:T(8,128)} %get-tuple-element.232) | copy-start | bytes 2073604
  714.7 25.1 %copy-start.6 = (f32[48,5,180]{2,0,1:T(8,128)S(1)}, f32[48,5,180]{2,0,1:T(8,128)}, u32[]{:S(2)}) copy-start(f32[48,5,180]{2,0,1:T(8,128)} %copy-done.5) | copy-start | bytes 518404
  714.7 25.1 %copy-start.69 = (f32[48,5,180]{2,0,1:T(8,128)S(1)}, f32[48,5,180]{2,0,1:T(8,128)}, u32[]{:S(2)}) copy-start(f32[48,5,180]{2,0,1:T(8,128)} %copy-done.68) | copy-start | bytes 518404
  714.7 25.1 %copy-start.178 = (f32[5,180]{1,0:T(8,128)S(1)}, f32[5,180]{1,0:T(8,128)}, u32[]{:S(2)}) copy-start(f32[5,180]{1,0:T(8,128)} %div.181) | copy-start | bytes 10804
  714.7 25.1 %copy-start.179 = (f32[5,180]{1,0:T(8,128)S(1)}, f32[5,180]{1,0:T(8,128)}, u32[]{:S(2)}) copy-start(f32[5,180]{1,0:T(8,128)} %rsqrt.83) | copy-start | bytes 10804
  714.7 25.1 %copy-start.208 = (f32[48]{0:T(128)S(1)}, f32[48]{0:T(128)}, u32[]{:S(2)}) copy-start(f32[48]{0:T(128)} %get-tuple-element.209) | copy-start | bytes 580
  740.2 14.8 %copy-start.38 = (f32[2,60,16,2,5,1]{1,2,3,4,0,5:T(8,128)S(1)}, f32[2,60,16,2,5,1]{1,2,3,4,0,5:T(8,128)}, u32[]{:S(2)}) copy-start(f32[2,60,16,2,5,1]{1,2,3,4,0,5:T(8,128)} %get-tuple-element.166) | copy-start | bytes 230404
  740.2 14.8 %copy-start.102 = (f32[4,1,48,60]{3,2,0,1:T(8,128)S(1)}, f32[4,1,48,60]{3,2,0,1:T(8,128)}, u32[]{:S(2)}) copy-start(f32[4,1,48,60]{3,2,0,1:T(8,128)} %copy-done.101) | copy-start | bytes 138244
  740.2 14.8 %copy-start.104 = (f32[4,1,48,60]{3,2,0,1:T(8,128)S(1)}, f32[4,1,48,60]{3,2,0,1:T(8,128)}, u32[]{:S(2)}) copy-start(f32[4,1,48,60]{3,2,0,1:T(8,128)} %copy-done.103) | copy-start | bytes 138244
  (193 other events, 717.1 us)
Sparse Core Ops, SparseCore 0:
  687.3 133.7 all-reduce.67

commit v2 on v0

v2 whole, which is shorter than its diff:
```python
import functools
import math

import jax
import jax.numpy as jnp
from jax import lax
from jax.experimental import pallas as pl
from jax.experimental.pallas import tpu as pltpu
from jax.sharding import PartitionSpec as P

shrink_level = 0.01
norm_eps = 1e-05
highest = lax.Precision.HIGHEST
MESH = pl.DeviceIdType.MESH
F32 = jnp.float32
BF16 = jnp.bfloat16

LAYERS = 4
NCH = 8
NLAT = 16
CB = 48
CP = 64
D = NCH * CB
ROWS = 5
LON = 180
TILE = 128
FB = 192
FF = NCH * FB
CHUNK = 384
TILE_FROM = [r * LON // TILE for r in range(ROWS)]
TILE_TO = [-(-(r + 1) * LON // TILE) for r in range(ROWS)]
SPAN = max(b - a for a, b in zip(TILE_FROM, TILE_TO)) * TILE


def gelu_exact(values):
    return 0.5 * values * (1.0 + lax.erf(values * 0.7071067811865476))


def gelu_slope(values):
    return (
        0.5 * (1.0 + lax.erf(values * 0.7071067811865476))
        + values * jnp.exp(-0.5 * values * values) * 0.3989422804014327
    )


def mm(a, b, dims=((1,), (0,)), precision=highest):
    return lax.dot_general(a, b, (dims, ((), ())), precision=precision, preferred_element_type=F32)


def mb(a, b, dims=((1,), (0,))):
    return lax.dot_general(a, b, (dims, ((), ())), preferred_element_type=F32)


NT = ((1,), (1,))


def stack_kernel(
    x0, ct, prm, wsh, bdw, bdt, fb, lat_a, lat_t, lon,
    out_h, out_g, gw, gp, gf, gfb,
    h_s, g_s, xin, pbuf, pcol, bcol, mbuf, fbuf, sbuf, xbuf, zbuf, cbuf, bbuf,
    wall, wT, n1_s, n2_s, r1_s, r2_s, lifted_s, pre_s, hid_s, y_s, hh_s, t_s,
    xs, prs, gr, psend, pget, gsend, gget, prow, pin, ig_s,
    bsem_s, bsem_r, asem_s, asem_r, psem_s, psem_r, gsem_s, gsem_r, qsem_s, qsem_r,
    c_s, c_r, l_s, l_r,
):
    ch = lax.axis_index("ch")
    lat = lax.axis_index("lat")
    core = lax.rem(lat, 2)
    partner = lat + 1 - 2 * core
    flip = lat + 2 - 4 * lax.rem(lat // 2, 2)
    ch_peer = [lax.rem(ch + s, NCH) for s in range(NCH)]
    lat_peer = [lax.rem(lat + s, NLAT) for s in range(NLAT)]

    barrier = pltpu.get_barrier_semaphore()
    for s in range(1, NCH):
        pl.semaphore_signal(barrier, inc=1, device_id={"ch": ch_peer[s]}, device_id_type=MESH)
        if s % 2:
            pl.semaphore_signal(
                barrier, inc=1, device_id={"lat": flip, "ch": ch_peer[s]}, device_id_type=MESH
            )
    for s in range(1, NLAT):
        pl.semaphore_signal(barrier, inc=1, device_id={"lat": lat_peer[s]}, device_id_type=MESH)

    def remote(src, dst, send, recv, where):
        return pltpu.make_async_remote_copy(
            src_ref=src, dst_ref=dst, send_sem=send, recv_sem=recv,
            device_id=where, device_id_type=MESH,
        )

    def over_ch(src, dst, send, recv):
        copies = [
            remote(src(ch_peer[s]), dst, send.at[s], recv.at[s], {"ch": ch_peer[s]})
            for s in range(1, NCH)
        ]
        for copy in copies:
            copy.start()
        return copies

    def over_near(src, dst, send, recv):
        copies = []
        for s in range(1, NCH):
            where = {"lat": flip, "ch": ch_peer[s]} if s % 2 else {"ch": ch_peer[s]}
            copies.append(remote(src(ch_peer[s]), dst, send.at[s], recv.at[s], where))
        return copies

    def over_lat(src, dst, at):
        copies = [
            remote(
                src.at[lat_peer[s]], dst.at[lat], l_s.at[at, s], l_r.at[at, s], {"lat": lat_peer[s]}
            )
            for s in range(1, NLAT)
        ]
        for copy in copies:
            copy.start()
        return copies

    def done(copies):
        for copy in copies:
            copy.wait()

    def weights_near(layer):
        mine = wall.at[layer, core, pl.ds(pl.multiple_of(ch * FB, FB), FB)]
        return over_near(
            lambda p: wsh.at[layer, core], mine, asem_s.at[layer], asem_r.at[layer]
        )

    def weights_pair(layer):
        block = wall.at[layer, core]
        return remote(block, block, psem_s.at[layer], psem_r.at[layer], {"lat": partner})

    def weights_start(layer):
        for copy in weights_near(layer):
            copy.start()

    def weights_pass(layer):
        wall[layer, core, pl.ds(pl.multiple_of(ch * FB, FB), FB)] = wsh[layer, core]
        done(weights_near(layer))
        weights_pair(layer).start()

    def weights_done(layer):
        weights_pair(layer).wait()

    fbuf[...] = jnp.zeros(fbuf.shape, F32)
    sbuf[...] = jnp.zeros(sbuf.shape, F32)
    prow[...] = jnp.zeros(prow.shape, F32)
    gfb[...] = jnp.zeros(gfb.shape, F32)
    xin[0, ch] = x0[ch]
    xin[1, ch] = ct[ch]
    pbuf[ch] = prm[...]
    pl.semaphore_wait(barrier, 2 * (NCH - 1) + NLAT - 1 - 3)
    first = over_ch(lambda p: x0.at[p], xin.at[0, ch], bsem_s.at[0], bsem_r.at[0])
    first += over_ch(lambda p: prm, pbuf.at[ch], bsem_s.at[1], bsem_r.at[1])
    second = over_ch(lambda p: ct.at[p], xin.at[1, ch], bsem_s.at[2], bsem_r.at[2])
    weights_start(0)
    done(first)
    for j in range(NCH):
        turned = jnp.transpose(pbuf[j])
        for layer in range(LAYERS):
            part = turned[:, layer * 8 : layer * 8 + 8]
            pcol[layer, j * CB : (j + 1) * CB, 0:8] = part[:CB]
            bcol[layer, j * FB : (j + 1) * FB, 0:8] = part[:FB]
    h_s[...] = xin[0]

    low = lax.broadcasted_iota(jnp.int32, (NLAT, TILE), 1) < CP

    def swap(v):
        return pltpu.roll(v, CP, 1)

    def lon_to_modes(which):
        for r in range(ROWS):
            a, b = TILE_FROM[r], TILE_TO[r]
            field = jnp.concatenate([fbuf[t] for t in range(a, b)], axis=1)
            part = mm(lon[which, r, :, : (b - a) * TILE], field, NT)
            sbuf[:, :, r * CP : (r + 1) * CP] = part.reshape(NLAT, 8, CP)

    def gather_lat():
        for ri in range(2):
            for kt in range(2):
                even = xbuf[:, 4 * kt + ri, :]
                odd = xbuf[:, 4 * kt + 2 + ri, :]
                for r in range(ROWS):
                    cut = slice(r // 2 * TILE, (r // 2 + 1) * TILE)
                    a, b = even[:, cut], odd[:, cut]
                    tile = jnp.where(low, swap(a), b) if r % 2 else jnp.where(low, a, swap(b))
                    at = ri * ROWS * NLAT + r * NLAT
                    xs[at : at + NLAT, kt * TILE : (kt + 1) * TILE] = tile

    def scatter_lat(z):
        for ri in range(2):
            for k in range(4):
                for t in range(3):
                    at = ri * ROWS * NLAT + 2 * t * NLAT
                    lanes = slice(k // 2 * TILE, (k // 2 + 1) * TILE)
                    a = z[at : at + NLAT, lanes]
                    if t == 2:
                        b = jnp.zeros_like(a)
                    else:
                        b = z[at + NLAT : at + 2 * NLAT, lanes]
                    tile = jnp.where(low, swap(a), b) if k % 2 else jnp.where(low, a, swap(b))
                    sbuf[:, 2 * k + ri, t * TILE : (t + 1) * TILE] = tile

    def lon_to_cells(which):
        tiles = [None] * NCH
        for r in range(ROWS):
            if r % 2 == 0:
                turned = jnp.transpose(
                    zbuf[:, :, r // 2 * TILE : (r // 2 + 1) * TILE].reshape(TILE, TILE)
                )
            a, b = TILE_FROM[r], TILE_TO[r]
            rows = turned[(r % 2) * CP : (r % 2) * CP + CB]
            part = mm(rows, lon[which, r, :, : (b - a) * TILE])
            for t in range(a, b):
                piece = part[:, (t - a) * TILE : (t - a + 1) * TILE]
                tiles[t] = piece if tiles[t] is None else tiles[t] + piece
        for t in range(NCH):
            cbuf[t] = tiles[t]

    def mix(v, table, sign):
        out = []
        for t in range(2):
            q = mm(v[:, t * TILE : (t + 1) * TILE], table)
            re = q[:64, :TILE] - sign * q[64:, TILE:]
            im = q[64:, :TILE] + sign * q[:64, TILE:]
            out.append(jnp.concatenate([re, im], axis=0))
        return jnp.concatenate(out, axis=1)

    def bias_rows(layer, at):
        re = jnp.broadcast_to(fb[layer, at : at + 1, :], (64, 2 * TILE))
        im = jnp.broadcast_to(fb[layer, at + 1 : at + 2, :], (64, 2 * TILE))
        return jnp.concatenate([re, im], axis=0)

    def exchange_one(value):
        mbuf[...] = value.reshape(NCH, CB, TILE)
        copies = over_ch(lambda p: mbuf.at[p], fbuf.at[ch, pl.ds(0, CB)], c_s.at[0], c_r.at[0])
        fbuf[ch, 0:CB] = mbuf[ch]
        return copies

    def exchange_four():
        copies = over_ch(lambda p: cbuf.at[p], bbuf.at[ch], c_s.at[1], c_r.at[1])
        bbuf[ch] = cbuf[ch]
        return copies

    def exchange_lat(dst, at):
        copies = over_lat(sbuf, dst, at)
        dst[lat] = sbuf[lat]
        return copies

    def col(layer, at):
        return pcol[layer, :, at : at + 1]

    def forward(layer, carry):
        h = h_s[...].reshape(D, TILE)
        mean = jnp.sum(h, axis=0, keepdims=True) * (1.0 / D)
        spread = jnp.sum(h * h, axis=0, keepdims=True) * (1.0 / D) - mean * mean
        rstd = lax.rsqrt(spread + norm_eps)
        n1 = (h - mean) * rstd
        n1_s[layer] = n1
        r1_s[layer] = jnp.broadcast_to(rstd, (8, TILE))
        mixed = n1 * col(layer, 0) + col(layer, 1)
        copies = exchange_one(mixed)
        ig_s[...] = h + mixed

        @pl.when(layer < LAYERS - 1)
        def _():
            weights_start(layer + 1)

        done(copies)
        lon_to_modes(0)
        copies = exchange_lat(xbuf, 0)
        weights_pass(layer)
        done(copies)
        gather_lat()
        y = mm(lat_a[...], xs[...])
        y_s[layer] = y
        hh = mix(y, bdw[layer, 0], 1.0) + bias_rows(layer, 0)
        hh_s[layer] = hh
        b = mix(gelu_exact(hh), bdw[layer, 1], 1.0) + bias_rows(layer, 2)
        t = jnp.tanh(b / shrink_level)
        t_s[layer] = t
        scatter_lat(mm(lat_t[...], b - shrink_level * t))
        copies = exchange_lat(zbuf, 1)
        weights_done(layer)
        for at in range(0, FF, CHUNK):
            wT[:, at : at + CHUNK] = jnp.transpose(wall[layer, 1, at : at + CHUNK, :])
        done(copies)
        lon_to_cells(1)
        copies = exchange_four()
        done(copies)
        inner = ig_s[...] + bbuf[...].reshape(D, TILE)
        mean = jnp.sum(inner, axis=0, keepdims=True) * (1.0 / D)
        spread = jnp.sum(inner * inner, axis=0, keepdims=True) * (1.0 / D) - mean * mean
        rstd = lax.rsqrt(spread + norm_eps)
        n2 = (inner - mean) * rstd
        n2_s[layer] = n2
        r2_s[layer] = jnp.broadcast_to(rstd, (8, TILE))
        lifted = (n2 * col(layer, 2) + col(layer, 3)).astype(BF16)
        lifted_s[layer] = lifted
        total = inner + col(layer, 4)
        for at in range(0, FF, CHUNK):
            pre = mb(wall[layer, 0, at : at + CHUNK, :], lifted) + bcol[layer, at : at + CHUNK, 5:6]
            pre_s[layer, at : at + CHUNK] = pre
            hidden = gelu_exact(pre).astype(BF16)
            hid_s[layer, at : at + CHUNK] = hidden
            total = total + mb(wT[:, at : at + CHUNK], hidden)
        h_s[...] = total.reshape(NCH, CB, TILE)
        return carry

    lax.fori_loop(0, LAYERS, forward, 0)
    last_h = over_ch(lambda p: h_s.at[p], out_h.at[ch], bsem_s.at[3], bsem_r.at[3])
    out_h[ch] = h_s[ch]
    done(second)
    g_s[...] = xin[1]
    ones = jnp.ones((8, TILE), F32)

    def turn_up(layer):
        for at in range(0, FF, CHUNK):
            wT[:, at : at + CHUNK] = jnp.transpose(wall[layer, 0, at : at + CHUNK, :])

    turn_up(LAYERS - 1)

    def row_sums(layer, at, value, width):
        for j in range(NCH):
            part = mm(ones, value[j * width : (j + 1) * width], NT)
            prow[j, layer, at : at + 1, 0:width] = part[0:1]

    def grads_pair(layer):
        return remote(
            psend.at[layer], pget.at[layer], qsem_s.at[layer], qsem_r.at[layer], {"lat": partner}
        )

    def grads_near(layer):
        return over_near(
            lambda p: gsend.at[layer, p], gget.at[layer, ch], gsem_s.at[layer], gsem_r.at[layer]
        )

    def grads_done(layer):
        gget[layer, ch] = gsend[layer, ch]
        done(grads_near(layer))
        total = gget[layer, 0].astype(F32)
        for j in range(1, NCH):
            total = total + gget[layer, j].astype(F32)
        gw[layer] = total

    def backward(step, carry):
        layer = LAYERS - 1 - step
        g = g_s[...].reshape(D, TILE)
        g_round = g.astype(BF16)
        lift = jnp.zeros((D, TILE), F32)
        for at in range(0, FF, CHUNK):
            hidden_grad = mb(wall[layer, 1, at : at + CHUNK, :], g_round)
            pre_grad = hidden_grad * gelu_slope(pre_s[layer, at : at + CHUNK])
            pre_s[layer, at : at + CHUNK] = pre_grad
            pre_round = pre_grad.astype(BF16)
            prs[at : at + CHUNK] = pre_round
            lift = lift + mb(wT[:, at : at + CHUNK], pre_round)
        n2 = n2_s[layer]
        q2 = lift * col(layer, 2)
        m1 = jnp.sum(q2, axis=0, keepdims=True) * (1.0 / D)
        m2 = jnp.sum(q2 * n2, axis=0, keepdims=True) * (1.0 / D)
        inner_grad = g + r2_s[layer, 0:1, :] * (q2 - m1 - n2 * m2)
        copies = exchange_one(inner_grad)
        ig_s[...] = inner_grad
        lifted = lifted_s[layer]
        for at in range(0, FF, CHUNK):
            gr[1, at : at + CHUNK] = mb(hid_s[layer, at : at + CHUNK], g_round, NT)
            gr[0, at : at + CHUNK] = mb(prs[at : at + CHUNK], lifted, NT)
        psend[layer] = gr[1 - core].astype(BF16)
        grads_pair(layer).start()
        row_sums(layer, 4, g, CB)
        row_sums(layer, 2, lift * n2, CB)
        row_sums(layer, 3, lift, CB)
        done(copies)
        lon_to_modes(1)
        copies = exchange_lat(xbuf, 0)
        row_sums(layer, 5, pre_s[layer], FB)
        grads_pair(layer).wait()
        gsend[layer] = (
            (gr[core] + pget[layer].astype(F32)).astype(BF16).reshape(NCH, FB, D)
        )
        for copy in grads_near(layer):
            copy.start()
        done(copies)
        gather_lat()
        t = t_s[layer]
        db = mm(lat_a[...], xs[...]) * (t * t)
        hh = hh_s[layer]
        dh = mix(db, bdt[layer, 1], -1.0) * gelu_slope(hh)
        dy = mix(dh, bdt[layer, 0], -1.0)
        scatter_lat(mm(lat_t[...], dy))
        copies = exchange_lat(zbuf, 1)

        def filter_grads(at, left, right):
            turned = jnp.concatenate([right[64:], -right[:64]], axis=0)
            total = jnp.zeros((TILE, 2 * TILE), F32)
            for tt in range(2):
                lanes = slice(tt * TILE, (tt + 1) * TILE)
                pair = jnp.concatenate([right[:, lanes], turned[:, lanes]], axis=1)
                total = total + mm(jnp.transpose(left[:, lanes]), pair)
            re = total[:64, :TILE] + swap(total[64:, :TILE])
            im = total[:64, TILE:] + swap(total[64:, TILE:])
            keep = lax.broadcasted_iota(jnp.int32, (64, TILE), 1) < CP
            gf[layer, at] = jnp.where(keep, re, swap(im))
            gfb[layer, 2 * at : 2 * at + 1] = jnp.sum(right[:64], axis=0, keepdims=True)
            gfb[layer, 2 * at + 1 : 2 * at + 2] = jnp.sum(right[64:], axis=0, keepdims=True)

        filter_grads(1, gelu_exact(hh), db)
        filter_grads(0, y_s[layer], dh)

        @pl.when(layer > 0)
        def _():
            turn_up(layer - 1)

        done(copies)
        lon_to_cells(0)
        copies = exchange_four()

        @pl.when(layer < LAYERS - 1)
        def _():
            grads_done(layer + 1)

        done(copies)
        inner_grad = ig_s[...]
        mixed_grad = inner_grad + bbuf[...].reshape(D, TILE)
        n1 = n1_s[layer]
        q1 = mixed_grad * col(layer, 0)
        m1 = jnp.sum(q1, axis=0, keepdims=True) * (1.0 / D)
        m2 = jnp.sum(q1 * n1, axis=0, keepdims=True) * (1.0 / D)
        g = inner_grad + r1_s[layer, 0:1, :] * (q1 - m1 - n1 * m2)
        g_s[...] = g.reshape(NCH, CB, TILE)
        row_sums(layer, 0, mixed_grad * n1, CB)
        row_sums(layer, 1, mixed_grad, CB)
        return carry

    lax.fori_loop(0, LAYERS, backward, 0)
    final = over_ch(lambda p: g_s.at[p], out_g.at[ch], bsem_s.at[4], bsem_r.at[4])
    final += over_ch(lambda p: prow.at[p], pin.at[ch], bsem_s.at[5], bsem_r.at[5])
    out_g[ch] = g_s[ch]
    pin[ch] = prow[ch]
    grads_done(0)
    done(last_h)
    done(final)
    total = pin[0]
    for j in range(1, NCH):
        total = total + pin[j]
    gp[...] = total


def run_stack(*args):
    shapes = [
        jax.ShapeDtypeStruct((NCH, CB, TILE), F32),
        jax.ShapeDtypeStruct((NCH, CB, TILE), F32),
        jax.ShapeDtypeStruct((LAYERS, FB, D), F32),
        jax.ShapeDtypeStruct((LAYERS, 8, 256), F32),
        jax.ShapeDtypeStruct((LAYERS, 2, 64, TILE), F32),
        jax.ShapeDtypeStruct((LAYERS, 8, 256), F32),
    ]
    v = pltpu.VMEM
    dma = pltpu.SemaphoreType.DMA
    scratch = [
        v((NCH, CB, TILE), F32),
        v((NCH, CB, TILE), F32),
        v((2, NCH, CB, TILE), F32),
        v((NCH, 32, 256), F32),
        v((LAYERS, D, TILE), F32),
        v((LAYERS, FF, TILE), F32),
        v((NCH, CB, TILE), F32),
        v((NCH, CP, TILE), F32),
        v((NLAT, 8, 3 * TILE), F32),
        v((NLAT, 8, 3 * TILE), F32),
        v((NLAT, 8, 3 * TILE), F32),
        v((NCH, CB, TILE), F32),
        v((NCH, CB, TILE), F32),
        v((LAYERS, 2, FF, D), BF16),
        v((D, FF), BF16),
        v((LAYERS, D, TILE), F32),
        v((LAYERS, D, TILE), F32),
        v((LAYERS, 8, TILE), F32),
        v((LAYERS, 8, TILE), F32),
        v((LAYERS, D, TILE), BF16),
        v((LAYERS, FF, TILE), F32),
        v((LAYERS, FF, TILE), BF16),
        v((LAYERS, TILE, 256), F32),
        v((LAYERS, TILE, 256), F32),
        v((LAYERS, TILE, 256), F32),
        v((2 * ROWS * NLAT, 256), F32),
        v((FF, TILE), BF16),
        v((2, FF, D), F32),
        v((LAYERS, FF, D), BF16),
        v((LAYERS, FF, D), BF16),
        v((LAYERS, NCH, FB, D), BF16),
        v((LAYERS, NCH, FB, D), BF16),
        v((NCH, LAYERS, 8, 256), F32),
        v((NCH, LAYERS, 8, 256), F32),
        v((D, TILE), F32),
        dma((6, NCH)),
        dma((6, NCH)),
        dma((LAYERS, NCH)),
        dma((LAYERS, NCH)),
        dma((LAYERS,)),
        dma((LAYERS,)),
        dma((LAYERS, NCH)),
        dma((LAYERS, NCH)),
        dma((LAYERS,)),
        dma((LAYERS,)),
        dma((2, NCH)),
        dma((2, NCH)),
        dma((2, NLAT)),
        dma((2, NLAT)),
    ]
    return pl.pallas_call(
        stack_kernel,
        out_shape=shapes,
        in_specs=[pl.BlockSpec(memory_space=pltpu.VMEM)] * len(args),
        out_specs=[pl.BlockSpec(memory_space=pltpu.VMEM)] * len(shapes),
        scratch_shapes=scratch,
        compiler_params=pltpu.CompilerParams(
            collective_id=0, has_side_effects=True, vmem_limit_bytes=60 << 20
        ),
        name="stack",
    )(*args)


SMALL = 640
WROWS = LAYERS * FB // 8


def finish_kernel(gw, small, wout, sout, wget, sget, wsum, ssum, s1, r1, s2, r2, s3, r3, s4, r4):
    lat = lax.axis_index("lat")
    core = lax.rem(lat, 2)
    near = lat // 2
    peer = [lax.rem(lat + s, NLAT) for s in range(NLAT)]
    barrier = pltpu.get_barrier_semaphore()
    for s in range(1, NLAT):
        pl.semaphore_signal(barrier, inc=1, device_id={"lat": peer[s]}, device_id_type=MESH)

    def remote(src, dst, send, recv, where):
        copy = pltpu.make_async_remote_copy(
            src_ref=src, dst_ref=dst, send_sem=send, recv_sem=recv,
            device_id={"lat": where}, device_id_type=MESH,
        )
        copy.start()
        return copy

    pl.semaphore_wait(barrier, NLAT - 1)
    copies = [
        remote(gw.at[peer[s] // 2], wget.at[near], s1.at[s], r1.at[s], peer[s])
        for s in range(2, NLAT, 2)
    ]
    copies += [
        remote(small.at[peer[s]], sget.at[lat], s2.at[s], r2.at[s], peer[s])
        for s in range(1, NLAT)
    ]
    wget[near] = gw[near]
    sget[lat] = small[lat]
    for copy in copies:
        copy.wait()
    total = wget[0]
    for j in range(1, 8):
        total = total + wget[j]
    wsum[...] = total.astype(BF16)
    copies = [
        remote(wsum, wout.at[core, near], s3.at[s], r3.at[s], peer[s]) for s in range(1, NLAT)
    ]
    part = sget[0]
    for j in range(1, NLAT):
        part = part + sget[j]
    ssum[...] = part
    copies += [
        remote(ssum, sout.at[lat], s4.at[s], r4.at[s], peer[s]) for s in range(1, NLAT)
    ]
    wout[core, near] = wsum[...]
    sout[lat] = ssum[...]
    for copy in copies:
        copy.wait()


def run_finish(gw, small):
    v = pltpu.VMEM
    dma = pltpu.SemaphoreType.DMA
    return pl.pallas_call(
        finish_kernel,
        out_shape=[
            jax.ShapeDtypeStruct((2, 8, WROWS, D), BF16),
            jax.ShapeDtypeStruct((NLAT, SMALL // NLAT, TILE), F32),
        ],
        in_specs=[pl.BlockSpec(memory_space=pltpu.VMEM)] * 2,
        out_specs=[pl.BlockSpec(memory_space=pltpu.VMEM)] * 2,
        scratch_shapes=[
            v((8, WROWS, D), F32),
            v((NLAT, SMALL // NLAT, TILE), F32),
            v((WROWS, D), BF16),
            v((SMALL // NLAT, TILE), F32),
        ]
        + [dma((NLAT,))] * 8,
        compiler_params=pltpu.CompilerParams(
            collective_id=1, has_side_effects=True, vmem_limit_bytes=40 << 20
        ),
        name="finish",
    )(gw.reshape(8, WROWS, D), small.reshape(NLAT, SMALL // NLAT, TILE))


def lat_table(kept_lat, lat_cells):
    cell_index = jnp.arange(lat_cells, dtype=jnp.int32)
    phase_index = kept_lat[:, None] * cell_index[None, :] % lat_cells
    angles = phase_index.astype(F32) * (2.0 * math.pi / lat_cells)
    scale = 1.0 / math.sqrt(lat_cells)
    modes = kept_lat.shape[0]

    def place(table):
        table = table.reshape(modes, NLAT, ROWS).transpose(0, 2, 1).reshape(modes, lat_cells)
        return jnp.pad(table, ((0, 64 - modes), (0, 0)))

    cos, sin = place(jnp.cos(angles) * scale), place(jnp.sin(angles) * scale)
    return jnp.concatenate(
        [jnp.concatenate([cos, sin], axis=1), jnp.concatenate([-sin, cos], axis=1)], axis=0
    )


def lon_tables(kept_lon, lon_cells):
    cell_index = jnp.arange(lon_cells, dtype=jnp.int32)
    phase_index = kept_lon[:, None] * cell_index[None, :] % lon_cells
    angles = phase_index.astype(F32) * (2.0 * math.pi / lon_cells)
    scale = 1.0 / math.sqrt(lon_cells)
    weight = jnp.where((kept_lon == 0) | (2 * kept_lon == lon_cells), 1.0, 2.0).astype(F32)
    table = jnp.stack([jnp.cos(angles), -jnp.sin(angles)], axis=1) * scale
    both = jnp.stack([table, table * weight[:, None, None]]).reshape(2, -1, lon_cells)
    rows = []
    for r in range(ROWS):
        before = r * LON - TILE_FROM[r] * TILE
        rows.append(jnp.pad(both, ((0, 0), (0, 0), (before, SPAN - LON - before))))
    return jnp.stack(rows, axis=1)


def pair_table(weight):
    padded = jnp.pad(weight, ((0, 0), (0, 0), (0, CP - CB), (0, CP - CB)))
    zero = jnp.zeros_like(padded)
    top = jnp.concatenate([padded, zero], axis=3)
    bottom = jnp.concatenate([zero, padded], axis=3)
    both = jnp.concatenate([top, bottom], axis=2)
    return jnp.concatenate([both[:, 0], both[:, 1]], axis=2)


def body(
    inputs,
    cotangent,
    first_gain,
    first_shift,
    filter_inner,
    filter_inner_bias,
    filter_outer,
    filter_outer_bias,
    second_gain,
    second_shift,
    up_weight,
    up_bias,
    down_weight,
    down_bias,
    kept_lat,
    kept_lon,
):
    shape = inputs.shape
    cells = ROWS * LON

    def to_tiles(field):
        flat = jnp.pad(field.reshape(CB, cells), ((0, 0), (0, NCH * TILE - cells)))
        return flat.reshape(CB, NCH, TILE).transpose(1, 0, 2)

    def from_tiles(tiles):
        return tiles.transpose(1, 0, 2).reshape(CB, NCH * TILE)[:, :cells].reshape(shape)

    vectors = jnp.stack([first_gain, first_shift, second_gain, second_shift, down_bias], axis=1)
    prm = jnp.concatenate(
        [
            jnp.pad(vectors, ((0, 0), (0, 0), (0, 256 - CB))),
            jnp.pad(up_bias[:, None, :], ((0, 0), (0, 2), (0, 256 - FB))),
        ],
        axis=1,
    ).reshape(32, 256)
    shards = jnp.stack([up_weight.transpose(0, 2, 1), down_weight], axis=1)
    inner_w, outer_w = filter_inner[:, :, 0], filter_outer[:, :, 0]
    bdw = jnp.stack([pair_table(inner_w), pair_table(outer_w)], axis=1)
    bdt = jnp.stack(
        [pair_table(inner_w.transpose(0, 1, 3, 2)), pair_table(outer_w.transpose(0, 1, 3, 2))],
        axis=1,
    )
    biases = jnp.concatenate([filter_inner_bias[:, :, 0], filter_outer_bias[:, :, 0]], axis=1)
    biases = jnp.tile(jnp.pad(biases, ((0, 0), (0, 4), (0, CP - CB))), (1, 1, 4))
    lat_a = lat_table(kept_lat, ROWS * NLAT)
    lon = lon_tables(kept_lon, LON)
    out_h, out_g, gw, gp, gf, gfb = run_stack(
        to_tiles(inputs), to_tiles(cotangent), prm, shards, bdw, bdt, biases,
        lat_a, lat_a.T, lon,
    )
    small = jnp.concatenate(
        [gf.reshape(-1, TILE), gfb.reshape(-1, TILE), gp.reshape(-1, TILE)], axis=0
    )
    wout, sout = run_finish(gw, small)
    wout = wout.reshape(2, LAYERS, FB, D).astype(F32)
    sout = sout.reshape(SMALL, TILE)
    filters = sout[:512].reshape(LAYERS, 2, CP, 2, CP)[:, :, :CB, :, :CB].transpose(1, 0, 3, 2, 4)
    fbias = sout[512:576].reshape(LAYERS, 8, 4, CP)[:, :4, :, :CB].sum(axis=2)
    fbias = fbias.reshape(LAYERS, 2, 2, 1, CB)
    rows = sout[576:].reshape(LAYERS, 8, 256)
    return (
        from_tiles(out_h),
        from_tiles(out_g),
        rows[:, 0, :CB],
        rows[:, 1, :CB],
        filters[0][:, :, None],
        fbias[:, 0],
        filters[1][:, :, None],
        fbias[:, 1],
        rows[:, 2, :CB],
        rows[:, 3, :CB],
        wout[0].transpose(0, 2, 1),
        rows[:, 5, :FB],
        wout[1],
        rows[:, 4, :CB],
    )


def solution(mesh):
    placed = (
        P("ch", "lat", None),
        P("ch", "lat", None),
        P(None, "ch"),
        P(None, "ch"),
        P(None, None, "ch", None, None),
        P(None, None, "ch", None),
        P(None, None, "ch", None, None),
        P(None, None, "ch", None),
        P(None, "ch"),
        P(None, "ch"),
        P(None, None, "ch"),
        P(None, "ch"),
        P(None, "ch", None),
        P(None, "ch"),
        P(),
        P(),
    )
    return jax.shard_map(
        body,
        mesh=mesh,
        in_specs=placed,
        out_specs=(
            P("ch", "lat", None),
            P("ch", "lat", None),
            P(None, "ch"),
            P(None, "ch"),
            P(None, None, "ch", None, None),
            P(None, None, "ch", None),
            P(None, None, "ch", None, None),
            P(None, None, "ch", None),
            P(None, "ch"),
            P(None, "ch"),
            P(None, None, "ch"),
            P(None, "ch"),
            P(None, "ch", None),
            P(None, "ch"),
        ),
        check_vma=False,
    )
```

time: 2010 us -> 328 us (0.16)
  blocking collectives: 898 us -> 0 us
  waiting for transfers between devices: 635 us -> 0 us
  Pallas kernels: 0 us -> 303 us
  matrix products: 166 us -> 0 us
  local copies, waits for them, and re-layouts: 114 us -> 17.4 us
  starting transfers between devices: 87.3 us -> 0 us
  other arithmetic: 73.9 us -> 6.84 us
    reduce_scatter x8 -> x0, waiting for transfers between devices: 564 us -> none  [the longest x4 288 us: body(): lax.psum_scatter(jnp.einsum('frw,cf->crw', pre_round, up_layer, preferred...]
    psum x17 -> x0, blocking collectives: 563 us -> none  [the longest x8 258 us: norm_sums(): lax.psum((jnp.sum(values, axis=0), jnp.sum(values * values, axis=0)), 'ch')]
    pallas_call x0 -> x2, Pallas kernels: none -> 303 us  [the longest x1 259 us: run_stack(): pl.pallas_call(stack_kernel, out_shape=shapes, in_specs=[pl.BlockSpec(mem...]
    all_gather x8 -> x0, blocking collectives: 256 us -> none  [the longest x4 129 us: body(): lifted = lax.all_gather(lifted_part, 'ch', axis=0, tiled=True)]
    dot_general x200 -> x0, matrix products: 166 us -> none  [the longest x24 17 us: complex_mix(): jnp.einsum('bimk,bij->bjmk', imag_part, weight[1], precision=highest)]
    all_to_all x11 -> x0, starting transfers between devices: 86.5 us -> none  [the longest x5 61.1 us: to_modes(): lax.all_to_all(values, 'lat', split_axis=2, concat_axis=1, tiled=True)]
    all_to_all x5 -> x0, blocking collectives: 79.1 us -> none  [the longest x3 60.7 us: to_modes(): lax.all_to_all(values, 'lat', split_axis=2, concat_axis=1, tiled=True)]
    unnamed x468 -> x55, local copies, waits for them, and re-layouts: 60.3 us -> 6.8 us
  transfers between devices with their start and end apart: 20 -> 0, of which waited for: 19 -> 0; matrix products, arithmetic and copies ran while one was open for 3% -> 0% of each run, Pallas kernels for 0% -> 0%
where the time goes in v2:
time: 328 us
  Pallas kernels  303 us (92%)
  local copies, waits for them, and re-layouts  17.4 us (5%)
  other arithmetic  6.84 us (2%)
    pallas_call x1, Pallas kernels, run_stack(): pl.pallas_call(stack_kernel, out_shape=shapes, in_specs=[pl.BlockSpec(mem...  259 us
    pallas_call x1, Pallas kernels, run_finish(): pl.pallas_call(finish_kernel, out_shape=[jax.ShapeDtypeStruct((2, 8, WROW...  43.2 us
    unnamed x55, local copies, waits for them, and re-layouts  6.8 us

profile of v2, /device:TPU:1, one launch (start us, length us, event | category | flops | bytes accessed | tf_op | source)
XLA Modules:
  0.0 327.9 jit_solution(4158889259272328815)
XLA Ops:
  0.6 1.0 fusion.4
  1.7 0.1 copy.72
  1.8 0.7 fusion.11
  2.5 0.1 mul.162
  2.6 0.1 mul.163
  2.7 0.1 copy_multiply_fusion.1
  2.8 0.0 copy-start.6
  2.9 0.2 bitcast_dynamic-update-slice_fusion.2
  3.0 0.2 bitcast_dynamic-update-slice_fusion.1
  3.2 0.0 copy-start.7
  3.2 0.2 bitcast_dynamic-update-slice_fusion
  3.4 0.2 bitcast_dynamic-update-slice_fusion.4.lon
  3.6 0.2 copy-done.6
  3.7 0.1 copy.69
  3.9 0.1 select_maximum_fusion.1
  4.1 0.1 copy-done.7
  4.2 0.1 copy.70
  4.3 0.1 select_maximum_fusion
  4.4 0.6 copy-done.1
  5.1 0.1 maximum_bitcast_fusion.2
  5.1 1.1 pad_maximum_fusion.2.bdt
  6.2 0.1 select_maximum_fusion.3
  6.4 0.1 select_maximum_fusion.2
  6.6 0.1 maximum_bitcast_fusion
  6.7 0.0 copy-start.18
  6.7 0.1 pad_maximum_fusion.1
  6.8 0.0 copy-start.5
  6.8 1.3 copy.79.bdw
  8.1 0.1 mul.144
  8.2 0.3 sine_multiply_fusion
  8.5 0.0 copy-start.3
  8.5 0.1 maximum_maximum_fusion
  8.6 0.8 copy.80.lat_a
  9.4 0.7 fusion.17.lat_t
  10.1 0.2 copy.64
  10.3 0.1 reshape.261
  10.4 0.2 copy.66
  10.6 0.0 copy-start.15
  10.6 0.0 copy-start.16
  10.6 0.0 copy-start.10
  10.6 0.0 copy-start.11
  10.7 0.1 reshape.263
  10.8 0.8 bitcast_bitcast_fusion
  11.6 1.1 pad_maximum_fusion.wsh
  12.8 0.6 copy.102
  13.5 0.7 tile.10.fb
  14.2 259.3 %stack.100 = (f32[8,48,128]{2,1,0:T(8,128)}, f32[8,48,128]{2,1,0:T(8,128)}, f32[4,192,384]{2,1,0:T(8,128)}, f32[4,8,256]{2,1,0:T(8,128)}, f32[4,2,64,128]{3,2,1,0:T(8,128)}, /*index=5*/f32[4,8,256]{2,1,0:T(8,128)}) custom-call(f32[8,48,128]{2,1,0:T(8,128)} %get-tuple-element.92.x0, f32[8,48,128]{2,1,0:T(8,128)} %get-tuple-element.91.ct, ...), custom_call_target="tpu_custom_call" | custom-call | tf_op jit(solution)/shard_map/stack/pallas_call | solution.py:510
  273.6 0.8 reshape.272
  274.3 0.8 reshape.273
  275.1 1.0 pad_maximum_fusion.3
  276.1 1.3 copy-done
  277.3 43.2 %finish.1 = (bf16[2,8,96,384]{3,2,1,0:T(8,128)(2,1)S(1)}, f32[16,40,128]{2,1,0:T(8,128)S(1)}) custom-call(f32[8,96,384]{2,1,0:T(8,128)S(1)} %bitcast.131, f32[16,40,128]{2,1,0:T(8,128)S(1)} %bitcast.130), custom_call_target="tpu_custom_call" | custom-call | tf_op jit(solution)/shard_map/finish/pallas_call | solution.py:580
  320.5 1.6 fusion.12
  322.2 0.3 reshape.277
  322.6 0.7 copy.85
  323.3 0.7 copy.87
  324.0 0.1 reshape.278
  324.1 0.6 fusion.16
  324.7 0.6 fusion.15
  325.3 0.6 copy.103
  326.0 0.2 reshape.267
  326.1 0.8 copy.83
  326.9 0.2 reshape.269
  327.1 0.8 copy.84
  (56 shorter events, 0.6 us)
Async XLA Ops:
  2.8 0.9 copy-start.6
  3.2 1.0 copy-start.7
  3.7 1.3 copy-start.1
  6.7 1.5 copy-start.18
  6.8 3.3 %copy-start.4 = (f32[48,5,180]{2,0,1:T(8,128)S(1)}, f32[48,5,180]{2,0,1:T(8,128)}, u32[]{:S(2)}) copy-start(f32[48,5,180]{2,0,1:T(8,128)} %param.16) | copy-start | bytes 518404
  6.8 3.6 %copy-start.5 = (f32[48,5,180]{2,0,1:T(8,128)S(1)}, f32[48,5,180]{2,0,1:T(8,128)}, u32[]{:S(2)}) copy-start(f32[48,5,180]{2,0,1:T(8,128)} %param.17) | copy-start | bytes 518404
  8.5 3.1 copy-start.2
  8.5 3.1 copy-start.3
  10.6 2.2 copy-start.13
  10.6 2.2 copy-start.14
  10.6 2.2 copy-start.15
  10.6 2.2 copy-start.16
  10.6 2.2 copy-start.17
  10.6 2.2 copy-start.10
  10.6 2.8 copy-start.11
  10.7 2.8 copy-start.12
  276.1 1.3 copy-start
  322.2 3.8 %copy-start.9 = (f32[8,48,128]{2,1,0:T(8,128)S(1)}, f32[8,48,128]{2,1,0:T(8,128)}, u32[]{:S(2)}) copy-start(f32[8,48,128]{2,1,0:T(8,128)} %get-tuple-element.22) | copy-start | bytes 589828
  322.6 4.4 %copy-start.8 = (f32[8,48,128]{2,1,0:T(8,128)S(1)}, f32[8,48,128]{2,1,0:T(8,128)}, u32[]{:S(2)}) copy-start(f32[8,48,128]{2,1,0:T(8,128)} %get-tuple-element.23) | copy-start | bytes 589828

commit v3 on v2

v3 whole, which is shorter than its diff:
```python
import functools
import math

import jax
import jax.numpy as jnp
import ml_dtypes
import numpy as np
from jax import lax
from jax.experimental import pallas as pl
from jax.experimental.pallas import tpu as pltpu
from jax.sharding import PartitionSpec as P

shrink_level = 0.01
norm_eps = 1e-05
highest = lax.Precision.HIGHEST
MESH = pl.DeviceIdType.MESH
F32 = jnp.float32
BF16 = jnp.bfloat16

LAYERS = 4
NCH = 8
NLAT = 16
CB = 48
CP = 64
D = NCH * CB
ROWS = 5
LON = 180
TILE = 128
FB = 192
FF = NCH * FB
CHUNK = 384
WROWS = FB // 8
TILE_FROM = [r * LON // TILE for r in range(ROWS)]
TILE_TO = [-(-(r + 1) * LON // TILE) for r in range(ROWS)]
SPAN = max(b - a for a, b in zip(TILE_FROM, TILE_TO)) * TILE


def gelu_exact(values):
    return 0.5 * values * (1.0 + lax.erf(values * 0.7071067811865476))


def gelu_slope(values):
    return (
        0.5 * (1.0 + lax.erf(values * 0.7071067811865476))
        + values * jnp.exp(-0.5 * values * values) * 0.3989422804014327
    )


def mm(a, b, dims=((1,), (0,)), precision=highest):
    return lax.dot_general(a, b, (dims, ((), ())), precision=precision, preferred_element_type=F32)


def mb(a, b, dims=((1,), (0,))):
    return lax.dot_general(a, b, (dims, ((), ())), preferred_element_type=F32)


NT = ((1,), (1,))


def split(value):
    high = value.astype(BF16)
    return high, (value - high.astype(F32)).astype(BF16)


def rows_times(value, high, low):
    vh, vl = split(value)
    n = value.shape[0]
    both = mb(jnp.concatenate([vh, vl], axis=0), high)
    return both[:n] + both[n:] + mb(vh, low)


def table_times(high, low, value):
    vh, vl = split(value)
    n = value.shape[1]
    both = mb(high, jnp.concatenate([vh, vl], axis=1))
    return both[:, :n] + both[:, n:] + mb(low, vh)


def stack_kernel(
    x0, ct, prm, wsh, fi, fo, fb, idx, all_a, all_t, all_k, all_v,
    out_h, out_g, wout, sout, rout, eout,
    h_s, g_s, xin, pbuf, pcol, bcol, mbuf, fbuf, sbuf, sbuf2, xbuf, zbuf, cbuf, bbuf,
    wall, wT, n1_s, n2_s, r1_s, r2_s, lifted_s, pre_s, hid_s, y_s, hh_s, t_s,
    xs, prs, gr, psend, pget, gsend, gget, pc, pin, bc, brow, bin_s, ig_s, mg_s, bwf,
    bw, bt, la, lt, lk, lv,
    gw, wget, wsum, gf, fget, fsum, gpsum, gpget, late, lin, lsum, lget,
    bsem_s, bsem_r, asem_s, asem_r, psem_s, psem_r, gsem_s, gsem_r, qsem_s, qsem_r,
    c_s, c_r, l_s, l_r, w1_s, w1_r, w2_s, w2_r, f_s, f_r,
):
    ch = lax.axis_index("ch")
    lat = lax.axis_index("lat")
    core = lax.rem(lat, 2)
    partner = lat + 1 - 2 * core
    flip = lat + 2 - 4 * lax.rem(lat // 2, 2)
    ch_peer = [lax.rem(ch + s, NCH) for s in range(NCH)]
    lat_peer = [lax.rem(lat + s, NLAT) for s in range(NLAT)]

    barrier = pltpu.get_barrier_semaphore()
    for s in range(1, NCH):
        pl.semaphore_signal(barrier, inc=1, device_id={"ch": ch_peer[s]}, device_id_type=MESH)
        if s % 2:
            pl.semaphore_signal(
                barrier, inc=1, device_id={"lat": flip, "ch": ch_peer[s]}, device_id_type=MESH
            )
    for s in range(1, NLAT):
        pl.semaphore_signal(barrier, inc=1, device_id={"lat": lat_peer[s]}, device_id_type=MESH)

    def remote(src, dst, send, recv, where):
        return pltpu.make_async_remote_copy(
            src_ref=src, dst_ref=dst, send_sem=send, recv_sem=recv,
            device_id=where, device_id_type=MESH,
        )

    def over_ch(src, dst, send, recv):
        copies = [
            remote(src(ch_peer[s]), dst, send.at[s], recv.at[s], {"ch": ch_peer[s]})
            for s in range(1, NCH)
        ]
        for copy in copies:
            copy.start()
        return copies

    def over_near(src, dst, send, recv):
        copies = []
        for s in range(1, NCH):
            where = {"lat": flip, "ch": ch_peer[s]} if s % 2 else {"ch": ch_peer[s]}
            copies.append(remote(src(ch_peer[s]), dst, send.at[s], recv.at[s], where))
        return copies

    def to_lat(src, dst, send, recv):
        return [
            remote(src(lat_peer[s]), dst, send.at[s], recv.at[s], {"lat": lat_peer[s]})
            for s in range(1, NLAT)
        ]

    def start(copies):
        for copy in copies:
            copy.start()
        return copies

    def arrived(copies):
        for copy in copies:
            copy.wait_recv()

    def sent(copies):
        for copy in copies:
            copy.wait_send()

    def done(copies):
        for copy in copies:
            copy.wait()

    def weights_near(layer):
        mine = wall.at[layer, core, pl.ds(pl.multiple_of(ch * FB, FB), FB)]
        return over_near(
            lambda p: wsh.at[layer, core], mine, asem_s.at[layer], asem_r.at[layer]
        )

    def weights_pair(layer):
        block = wall.at[layer, core]
        return remote(block, block, psem_s.at[layer], psem_r.at[layer], {"lat": partner})

    def weights_start(layer):
        for copy in weights_near(layer):
            copy.start()

    def weights_pass(layer):
        wall[layer, core, pl.ds(pl.multiple_of(ch * FB, FB), FB)] = wsh[layer, core]
        done(weights_near(layer))
        weights_pair(layer).start()

    def weights_done(layer):
        weights_pair(layer).wait()

    xin[0, ch] = x0[ch]
    xin[1, ch] = ct[ch]
    pbuf[ch] = prm[...]
    pl.semaphore_wait(barrier, 2 * (NCH - 1) + NLAT - 1 - 3)
    first = over_ch(lambda p: x0.at[p], xin.at[0, ch], bsem_s.at[0], bsem_r.at[0])
    first += over_ch(lambda p: prm, pbuf.at[ch], bsem_s.at[1], bsem_r.at[1])
    weights_start(0)
    pc[...] = jnp.zeros(pc.shape, F32)
    bc[...] = jnp.zeros(bc.shape, F32)
    late[...] = jnp.zeros(late.shape, F32)
    bwf[...] = jnp.zeros(bwf.shape, F32)

    def picker(at):
        rows = lax.broadcasted_iota(jnp.int32, (2 * TILE, TILE), 0)
        return jnp.where(rows == idx[at : at + 1, :], 1.0, 0.0)

    def turn(pick):
        return jnp.concatenate([jnp.transpose(pick[:TILE]), jnp.transpose(pick[TILE:])], axis=1)

    ends = (idx[0:1, :] < 2) | (idx[0:1, :] >= 180)
    mode_weight = jnp.where(ends, 1.0, 2.0)
    pick = picker(0)
    pick_t = jnp.concatenate([turn(pick), turn(pick * mode_weight)], axis=0).astype(BF16)
    pick = pick.astype(BF16)
    for part in range(2):
        for r in range(ROWS):
            table = mb(all_k[part, r], pick)
            lk[part, 0, r] = table.astype(BF16)
            lk[part, 1, r] = (table * mode_weight).astype(BF16)
            table = mb(pick_t, all_v[part, r]).astype(BF16)
            lv[part, 0, r] = table[:TILE]
            lv[part, 1, r] = table[TILE:]
    pick = picker(1)
    pick_t = turn(pick).astype(BF16)
    pick = pick.astype(BF16)
    for part in range(2):
        la[part] = mb(pick_t, all_a[part]).astype(BF16)
        lt[part] = mb(all_t[part], pick).astype(BF16)
    done(first)
    second = over_ch(lambda p: ct.at[p], xin.at[1, ch], bsem_s.at[2], bsem_r.at[2])
    for j in range(NCH):
        turned = jnp.transpose(pbuf[j])
        for layer in range(LAYERS):
            part = turned[:, layer * 8 : layer * 8 + 8]
            pcol[layer, j * CB : (j + 1) * CB, 0:8] = part[:CB]
            bcol[layer, j * FB : (j + 1) * FB, 0:8] = part[:FB]
    h_s[...] = xin[0]

    lane = lax.broadcasted_iota(jnp.int32, (NLAT, TILE), 1)

    def filter_tables(layer):
        for at, weight in enumerate((fi, fo)):
            for part in range(2):
                for k in range(2):
                    lanes = part * TILE + k * CP
                    bwf[k * CP : k * CP + CB, lanes : lanes + CB] = weight[layer, part]
            table = bwf[...]
            bw[0, layer, at], bw[1, layer, at] = split(table)
            bt[0, layer, at], bt[1, layer, at] = split(
                jnp.concatenate(
                    [jnp.transpose(table[:, :TILE]), jnp.transpose(table[:, TILE:])], axis=1
                )
            )

    def swap(v):
        return pltpu.roll(v, CP, 1)

    def lon_to_modes(which):
        parts = []
        for r in range(ROWS):
            a, b = TILE_FROM[r], TILE_TO[r]
            field = jnp.concatenate([fbuf[t] for t in range(a, b)], axis=1)
            span = (b - a) * TILE
            parts.append(rows_times(field, lk[0, which, r, :span], lk[1, which, r, :span]))
        parts.append(jnp.zeros((2 * TILE - ROWS * CB, TILE), F32))
        both = jnp.concatenate(parts, axis=0)
        for t in range(2):
            turned = jnp.transpose(both[t * TILE : (t + 1) * TILE])
            sbuf[:, :, t * TILE : (t + 1) * TILE] = turned.reshape(NLAT, 8, TILE)

    def gather_lat():
        for ri in range(2):
            for kt in range(2):
                sides = []
                for side in range(2):
                    q = 4 * kt + 2 * side + ri
                    left, right = xbuf[:, q, :TILE], xbuf[:, q, TILE:]
                    middle = jnp.where(lane >= 2 * CB, left, right)
                    sides.append([left, left, middle, right, right])
                for r in range(ROWS):
                    a = pltpu.roll(sides[0][r], (-r * CB) % TILE, 1) if r else sides[0][r]
                    b = pltpu.roll(sides[1][r], (CP - r * CB) % TILE, 1)
                    at = ri * ROWS * NLAT + r * NLAT
                    xs[at : at + NLAT, kt * TILE : (kt + 1) * TILE] = jnp.where(lane < CP, a, b)

    def scatter_lat(z):
        for ri in range(2):
            for k in range(4):
                lanes = slice(k // 2 * TILE, (k // 2 + 1) * TILE)
                p = []
                for r in range(ROWS):
                    at = ri * ROWS * NLAT + r * NLAT
                    piece = z[at : at + NLAT, lanes]
                    move = (r * CB - k % 2 * CP) % TILE
                    p.append(pltpu.roll(piece, move, 1) if move else piece)
                left = jnp.where(lane < CB, p[0], jnp.where(lane < 2 * CB, p[1], p[2]))
                right = jnp.where(lane < 16, p[2], jnp.where(lane < 64, p[3], p[4]))
                sbuf2[:, 2 * k + ri, :TILE] = left
                sbuf2[:, 2 * k + ri, TILE:] = jnp.where(lane < 112, right, 0.0)

    def lon_to_cells(which):
        both = jnp.concatenate(
            [
                jnp.transpose(zbuf[:, :, t * TILE : (t + 1) * TILE].reshape(TILE, TILE))
                for t in range(2)
            ],
            axis=0,
        )
        tiles = [None] * NCH
        for r in range(ROWS):
            a, b = TILE_FROM[r], TILE_TO[r]
            span = (b - a) * TILE
            rows = both[r * CB : (r + 1) * CB]
            part = rows_times(rows, lv[0, which, r, :, :span], lv[1, which, r, :, :span])
            for t in range(a, b):
                piece = part[:, (t - a) * TILE : (t - a + 1) * TILE]
                tiles[t] = piece if tiles[t] is None else tiles[t] + piece
        for t in range(NCH):
            cbuf[t] = tiles[t]

    def mix(v, table, layer, at, sign):
        out = []
        for t in range(2):
            q = rows_times(v[:, t * TILE : (t + 1) * TILE], table[0, layer, at], table[1, layer, at])
            re = q[:64, :TILE] - sign * q[64:, TILE:]
            im = q[64:, :TILE] + sign * q[:64, TILE:]
            out.append(jnp.concatenate([re, im], axis=0))
        return jnp.concatenate(out, axis=1)

    def bias_rows(layer, at):
        rows = [jnp.broadcast_to(fb[layer, at + ri : at + ri + 1, :], (64, TILE)) for ri in range(2)]
        both = jnp.concatenate(rows, axis=0)
        return jnp.concatenate([both, both], axis=1)

    def exchange_one(value):
        mbuf[...] = value.reshape(NCH, CB, TILE)
        copies = over_ch(lambda p: mbuf.at[p], fbuf.at[ch], c_s.at[0], c_r.at[0])
        fbuf[ch] = mbuf[ch]
        return copies

    def exchange_four():
        copies = over_ch(lambda p: cbuf.at[p], bbuf.at[ch], c_s.at[1], c_r.at[1])
        bbuf[ch] = cbuf[ch]
        return copies

    def exchange_lat(src, dst, at):
        copies = start(to_lat(lambda p: src.at[p], dst.at[lat], l_s.at[at], l_r.at[at]))
        dst[lat] = src[lat]
        return copies

    def col(layer, at):
        return pcol[layer, :, at : at + 1]

    def forward(layer, carry):
        h = h_s[...].reshape(D, TILE)
        mean = jnp.sum(h, axis=0, keepdims=True) * (1.0 / D)
        spread = jnp.sum(h * h, axis=0, keepdims=True) * (1.0 / D) - mean * mean
        rstd = lax.rsqrt(spread + norm_eps)
        n1 = (h - mean) * rstd
        n1_s[layer] = n1
        r1_s[layer] = jnp.broadcast_to(rstd, (8, TILE))
        mixed = n1 * col(layer, 0) + col(layer, 1)
        one = exchange_one(mixed)
        ig_s[...] = h + mixed
        filter_tables(layer)
        arrived(one)
        lon_to_modes(0)
        two = exchange_lat(sbuf, xbuf, 0)
        sent(one)

        @pl.when(layer < LAYERS - 1)
        def _():
            weights_start(layer + 1)

        arrived(two)
        gather_lat()
        y = table_times(la[0], la[1], xs[...])
        y_s[layer] = y
        hh = mix(y, bw, layer, 0, 1.0) + bias_rows(layer, 0)
        hh_s[layer] = hh
        b = mix(gelu_exact(hh), bw, layer, 1, 1.0) + bias_rows(layer, 2)
        t = jnp.tanh(b / shrink_level)
        t_s[layer] = t
        scatter_lat(table_times(lt[0], lt[1], b - shrink_level * t))
        three = exchange_lat(sbuf2, zbuf, 1)
        sent(two)
        weights_pass(layer)
        arrived(three)
        lon_to_cells(1)
        four = exchange_four()
        sent(three)
        weights_done(layer)
        for at in range(0, FF, CHUNK):
            wT[:, at : at + CHUNK] = jnp.transpose(wall[layer, 1, at : at + CHUNK, :])
        arrived(four)
        inner = ig_s[...] + bbuf[...].reshape(D, TILE)
        mean = jnp.sum(inner, axis=0, keepdims=True) * (1.0 / D)
        spread = jnp.sum(inner * inner, axis=0, keepdims=True) * (1.0 / D) - mean * mean
        rstd = lax.rsqrt(spread + norm_eps)
        n2 = (inner - mean) * rstd
        n2_s[layer] = n2
        r2_s[layer] = jnp.broadcast_to(rstd, (8, TILE))
        lifted = (n2 * col(layer, 2) + col(layer, 3)).astype(BF16)
        lifted_s[layer] = lifted
        total = inner + col(layer, 4)
        for at in range(0, FF, CHUNK):
            pre = mb(wall[layer, 0, at : at + CHUNK, :], lifted) + bcol[layer, at : at + CHUNK, 5:6]
            pre_s[layer, at : at + CHUNK] = pre
            hidden = gelu_exact(pre).astype(BF16)
            hid_s[layer, at : at + CHUNK] = hidden
            total = total + mb(wT[:, at : at + CHUNK], hidden)
        h_s[...] = total.reshape(NCH, CB, TILE)
        sent(four)
        return carry

    lax.fori_loop(0, LAYERS, forward, 0)
    last_h = over_ch(lambda p: h_s.at[p], out_h.at[ch], bsem_s.at[3], bsem_r.at[3])
    out_h[ch] = h_s[ch]
    done(second)
    g_s[...] = xin[1]
    ones = jnp.ones((8, TILE), F32)

    def turn_up(layer):
        for at in range(0, FF, CHUNK):
            wT[:, at : at + CHUNK] = jnp.transpose(wall[layer, 0, at : at + CHUNK, :])

    turn_up(LAYERS - 1)

    lanes_d = lax.broadcasted_iota(jnp.int32, (D, TILE), 1)
    lanes_f = lax.broadcasted_iota(jnp.int32, (CHUNK, TILE), 1)

    def cell_sums(layer, at, value):
        total = jnp.sum(value, axis=1, keepdims=True)
        held = pc[...].reshape(D, TILE)
        held = jnp.where(lanes_d == layer * 8 + at, total, held)
        pc[...] = held.reshape(NCH, CB, TILE)

    def hidden_sums(layer):
        for at in range(0, FF, CHUNK):
            total = jnp.sum(pre_s[layer, at : at + CHUNK], axis=1, keepdims=True)
            held = bc[at : at + CHUNK]
            bc[at : at + CHUNK] = jnp.where(lanes_f == layer, total, held)

    def turn_hidden_sums():
        blank = jnp.zeros((2 * TILE - FB, TILE), F32)
        for j in range(NCH):
            tall = jnp.concatenate([bc[j * FB : (j + 1) * FB], blank], axis=0)
            for t in range(2):
                turned = jnp.transpose(tall[t * TILE : (t + 1) * TILE])
                brow[j, :, t * TILE : (t + 1) * TILE] = turned[:8]

    def grads_pair(layer):
        return remote(
            psend, pget, qsem_s.at[layer], qsem_r.at[layer], {"lat": partner}
        )

    def grads_near(layer):
        return over_near(
            lambda p: gsend.at[p], gget.at[lax.rem(layer, 2), ch], gsem_s.at[layer], gsem_r.at[layer]
        )

    def grads_done(layer):
        slot = lax.rem(layer, 2)
        gget[slot, ch] = gsend[ch]
        done(grads_near(layer))
        total = gget[slot, 0].astype(F32)
        for j in range(1, NCH):
            total = total + gget[slot, j].astype(F32)
        gw[layer] = total.reshape(8, WROWS, D)

    near = lat // 2

    def sum_share(layer):
        return [
            remote(
                gw.at[layer, lat_peer[s] // 2], wget.at[layer, near],
                w1_s.at[layer, s], w1_r.at[layer, s], {"lat": lat_peer[s]},
            )
            for s in range(2, NLAT, 2)
        ]

    def sum_give(layer):
        return to_lat(
            lambda p: wsum.at[layer], wout.at[layer, core, near], w2_s.at[layer], w2_r.at[layer]
        )

    def sum_pass(layer):
        wget[layer, near] = gw[layer, near]
        done(sum_share(layer))
        total = wget[layer, 0]
        for j in range(1, 8):
            total = total + wget[layer, j]
        wsum[layer] = total
        wout[layer, core, near] = total
        start(sum_give(layer))

    def filters_share():
        return to_lat(lambda p: gf.at[p], fget.at[lat], f_s.at[0], f_r.at[0])

    def filters_give():
        return to_lat(lambda p: fsum, sout.at[lat], f_s.at[1], f_r.at[1])

    def rows_share():
        copies = []
        for s in range(1, NCH):
            p, where = ch_peer[s], {"ch": ch_peer[s]}
            copies.append(remote(pc.at[p], pin.at[ch], bsem_s.at[5, s], bsem_r.at[5, s], where))
            copies.append(
                remote(brow.at[p], bin_s.at[ch], bsem_s.at[7, s], bsem_r.at[7, s], where)
            )
        return copies

    def rows_give():
        return to_lat(lambda p: gpsum, gpget.at[lat], f_s.at[2], f_r.at[2])

    def rows_pass():
        pin[ch] = pc[ch]
        bin_s[ch] = brow[ch]
        done(rows_share())
        total, hidden = pin[0], bin_s[0]
        for j in range(1, NCH):
            total, hidden = total + pin[j], hidden + bin_s[j]
        tall = jnp.concatenate([total, jnp.zeros((TILE - CB, TILE), F32)], axis=0)
        gpsum[:32] = jnp.transpose(tall)[:32]
        gpsum[32:40] = hidden[:, :TILE]
        gpsum[40:48] = hidden[:, TILE:]
        gpget[lat] = gpsum[...]
        start(rows_give())

    def backward(step, carry):
        layer = LAYERS - 1 - step
        g = g_s[...].reshape(D, TILE)
        g_round = g.astype(BF16)
        lift = jnp.zeros((D, TILE), F32)
        for at in range(0, FF, CHUNK):
            hidden_grad = mb(wall[layer, 1, at : at + CHUNK, :], g_round)
            pre_grad = hidden_grad * gelu_slope(pre_s[layer, at : at + CHUNK])
            pre_s[layer, at : at + CHUNK] = pre_grad
            pre_round = pre_grad.astype(BF16)
            prs[at : at + CHUNK] = pre_round
            lift = lift + mb(wT[:, at : at + CHUNK], pre_round)
        n2 = n2_s[layer]
        q2 = lift * col(layer, 2)
        m1 = jnp.sum(q2, axis=0, keepdims=True) * (1.0 / D)
        m2 = jnp.sum(q2 * n2, axis=0, keepdims=True) * (1.0 / D)
        inner_grad = g + r2_s[layer, 0:1, :] * (q2 - m1 - n2 * m2)
        one = exchange_one(inner_grad)
        ig_s[...] = inner_grad
        lifted = lifted_s[layer]
        for at in range(0, FF, CHUNK):
            gr[1, at : at + CHUNK] = mb(hid_s[layer, at : at + CHUNK], g_round, NT)
            gr[0, at : at + CHUNK] = mb(prs[at : at + CHUNK], lifted, NT)
        psend[...] = gr[1 - core].astype(BF16)
        grads_pair(layer).start()
        cell_sums(layer, 4, g)
        cell_sums(layer, 2, lift * n2)
        cell_sums(layer, 3, lift)
        arrived(one)
        lon_to_modes(1)
        two = exchange_lat(sbuf, xbuf, 0)
        sent(one)

        @pl.when(layer < LAYERS - 1)
        def _():
            grads_done(layer + 1)
            start(sum_share(layer + 1))

        grads_pair(layer).wait()
        gsend[...] = (gr[core] + pget[...].astype(F32)).astype(BF16).reshape(NCH, FB, D)
        start(grads_near(layer))
        hidden_sums(layer)
        arrived(two)
        gather_lat()
        t = t_s[layer]
        db = table_times(la[0], la[1], xs[...]) * (t * t)
        hh = hh_s[layer]
        dh = mix(db, bt, layer, 1, -1.0) * gelu_slope(hh)
        dy = mix(dh, bt, layer, 0, -1.0)
        scatter_lat(table_times(lt[0], lt[1], dy))
        three = exchange_lat(sbuf2, zbuf, 1)
        sent(two)

        def filter_grads(at, left, right):
            turned = jnp.concatenate([right[64:], -right[:64]], axis=0)
            total = jnp.zeros((TILE, 2 * TILE), F32)
            for tt in range(2):
                lanes = slice(tt * TILE, (tt + 1) * TILE)
                pair = jnp.concatenate([right[:, lanes], turned[:, lanes]], axis=1)
                total = total + mm(jnp.transpose(left[:, lanes]), pair)
            re = total[:64, :TILE] + swap(total[64:, :TILE])
            im = total[:64, TILE:] + swap(total[64:, TILE:])
            keep = lax.broadcasted_iota(jnp.int32, (64, TILE), 1) < CP
            value = jnp.where(keep, re, swap(im))
            base = (layer * 2 + at) * 2
            gf[base] = value[:32]
            gf[base + 1] = value[32:]
            sums = []
            for part in (right[:64], right[64:]):
                row = jnp.sum(part, axis=0, keepdims=True)
                row = row[:, :TILE] + row[:, TILE:]
                sums.append(row + swap(row))
            gf[base + 1, 16:17, :] = jnp.where(keep[:1], sums[0], sums[1])

        filter_grads(1, gelu_exact(hh), db)
        filter_grads(0, y_s[layer], dh)

        @pl.when(layer > 0)
        def _():
            turn_up(layer - 1)

        @pl.when(layer == 0)
        def _():
            start(filters_share())
            turn_hidden_sums()
            start(rows_share())

        arrived(three)
        lon_to_cells(0)
        four = exchange_four()
        sent(three)

        @pl.when(layer < LAYERS - 1)
        def _():
            sum_pass(layer + 1)

        @pl.when(layer == 0)
        def _():
            fget[lat] = gf[lat]
            done(filters_share())
            total = fget[0]
            for j in range(1, NLAT):
                total = total + fget[j]
            fsum[...] = total
            sout[lat] = total
            start(filters_give())
            rows_pass()
            grads_done(0)
            start(sum_share(0))

        arrived(four)
        inner_grad = ig_s[...]
        mixed_grad = inner_grad + bbuf[...].reshape(D, TILE)
        n1 = n1_s[layer]
        q1 = mixed_grad * col(layer, 0)
        m1 = jnp.sum(q1, axis=0, keepdims=True) * (1.0 / D)
        m2 = jnp.sum(q1 * n1, axis=0, keepdims=True) * (1.0 / D)
        g = inner_grad + r1_s[layer, 0:1, :] * (q1 - m1 - n1 * m2)
        g_s[...] = g.reshape(NCH, CB, TILE)
        mg_s[...] = mixed_grad

        @pl.when(layer > 0)
        def _():
            cell_sums(layer, 0, mixed_grad * n1)
            cell_sums(layer, 1, mixed_grad)

        sent(four)
        return carry

    lax.fori_loop(0, LAYERS, backward, 0)
    final = over_ch(lambda p: g_s.at[p], out_g.at[ch], bsem_s.at[4], bsem_r.at[4])
    out_g[ch] = g_s[ch]
    mixed_grad = mg_s[...]
    for at, value in enumerate((mixed_grad * n1_s[0], mixed_grad)):
        for j in range(NCH):
            part = mm(ones, value[j * CB : (j + 1) * CB], NT)
            late[j, at : at + 1, 0:CB] = part[0:1]
    late_copies = over_ch(lambda p: late.at[p], lin.at[ch], bsem_s.at[6], bsem_r.at[6])
    lin[ch] = late[ch]
    sum_pass(0)
    done(late_copies)
    total = lin[0]
    for j in range(1, NCH):
        total = total + lin[j]
    lsum[...] = total
    lget[lat] = total
    give_late = start(to_lat(lambda p: lsum, lget.at[lat], f_s.at[3], f_r.at[3]))
    done(last_h)
    done(final)
    done(filters_give())
    for layer in range(LAYERS):
        done(sum_give(layer))
    done(rows_give())
    total = gpget[0]
    for j in range(1, NLAT):
        total = total + gpget[j]
    rout[...] = total
    done(give_late)
    total = lget[0]
    for j in range(1, NLAT):
        total = total + lget[j]
    eout[...] = total


def run_stack(*args):
    shapes = [
        jax.ShapeDtypeStruct((NCH, CB, TILE), F32),
        jax.ShapeDtypeStruct((NCH, CB, TILE), F32),
        jax.ShapeDtypeStruct((LAYERS, 2, 8, WROWS, D), F32),
        jax.ShapeDtypeStruct((NLAT, 32, TILE), F32),
        jax.ShapeDtypeStruct((48, TILE), F32),
        jax.ShapeDtypeStruct((8, TILE), F32),
    ]
    v = pltpu.VMEM
    dma = pltpu.SemaphoreType.DMA
    scratch = [
        v((NCH, CB, TILE), F32),
        v((NCH, CB, TILE), F32),
        v((2, NCH, CB, TILE), F32),
        v((NCH, 32, 256), F32),
        v((LAYERS, D, TILE), F32),
        v((LAYERS, FF, TILE), F32),
        v((NCH, CB, TILE), F32),
        v((NCH, CB, TILE), F32),
        v((NLAT, 8, 2 * TILE), F32),
        v((NLAT, 8, 2 * TILE), F32),
        v((NLAT, 8, 2 * TILE), F32),
        v((NLAT, 8, 2 * TILE), F32),
        v((NCH, CB, TILE), F32),
        v((NCH, CB, TILE), F32),
        v((LAYERS, 2, FF, D), BF16),
        v((D, FF), BF16),
        v((LAYERS, D, TILE), F32),
        v((LAYERS, D, TILE), F32),
        v((LAYERS, 8, TILE), F32),
        v((LAYERS, 8, TILE), F32),
        v((LAYERS, D, TILE), BF16),
        v((LAYERS, FF, TILE), F32),
        v((LAYERS, FF, TILE), BF16),
        v((LAYERS, TILE, 256), F32),
        v((LAYERS, TILE, 256), F32),
        v((LAYERS, TILE, 256), F32),
        v((2 * ROWS * NLAT, 256), F32),
        v((FF, TILE), BF16),
        v((2, FF, D), F32),
        v((FF, D), BF16),
        v((FF, D), BF16),
        v((NCH, FB, D), BF16),
        v((2, NCH, FB, D), BF16),
        v((NCH, CB, TILE), F32),
        v((NCH, CB, TILE), F32),
        v((FF, TILE), F32),
        v((NCH, 8, 256), F32),
        v((NCH, 8, 256), F32),
        v((D, TILE), F32),
        v((D, TILE), F32),
        v((TILE, 256), F32),
        v((2, LAYERS, 2, TILE, 256), BF16),
        v((2, LAYERS, 2, TILE, 256), BF16),
        v((2, TILE, 2 * ROWS * NLAT), BF16),
        v((2, 2 * ROWS * NLAT, TILE), BF16),
        v((2, 2, ROWS, SPAN, TILE), BF16),
        v((2, 2, ROWS, TILE, SPAN), BF16),
        v((LAYERS, 8, WROWS, D), F32),
        v((LAYERS, 8, WROWS, D), F32),
        v((LAYERS, WROWS, D), F32),
        v((NLAT, 32, TILE), F32),
        v((NLAT, 32, TILE), F32),
        v((32, TILE), F32),
        v((48, TILE), F32),
        v((NLAT, 48, TILE), F32),
        v((NCH, 8, TILE), F32),
        v((NCH, 8, TILE), F32),
        v((8, TILE), F32),
        v((NLAT, 8, TILE), F32),
        dma((8, NCH)),
        dma((8, NCH)),
        dma((LAYERS, NCH)),
        dma((LAYERS, NCH)),
        dma((LAYERS,)),
        dma((LAYERS,)),
        dma((LAYERS, NCH)),
        dma((LAYERS, NCH)),
        dma((LAYERS,)),
        dma((LAYERS,)),
        dma((2, NCH)),
        dma((2, NCH)),
        dma((2, NLAT)),
        dma((2, NLAT)),
        dma((LAYERS, NLAT)),
        dma((LAYERS, NLAT)),
        dma((LAYERS, NLAT)),
        dma((LAYERS, NLAT)),
        dma((4, NLAT)),
        dma((4, NLAT)),
    ]
    return pl.pallas_call(
        stack_kernel,
        out_shape=shapes,
        in_specs=[pl.BlockSpec(memory_space=pltpu.VMEM)] * len(args),
        out_specs=[pl.BlockSpec(memory_space=pltpu.VMEM)] * len(shapes),
        scratch_shapes=scratch,
        compiler_params=pltpu.CompilerParams(
            collective_id=0, has_side_effects=True, vmem_limit_bytes=60 << 20
        ),
        name="stack",
    )(*args)


def two_parts(table):
    high = table.astype(ml_dtypes.bfloat16)
    return np.stack([high, (table - high.astype(np.float64)).astype(ml_dtypes.bfloat16)])


def lat_all():
    lat_cells = ROWS * NLAT
    phase = np.outer(np.arange(lat_cells), np.arange(lat_cells)) % lat_cells
    angles = phase * (2.0 * math.pi / lat_cells)

    def place(table):
        return table.reshape(lat_cells, NLAT, ROWS).transpose(0, 2, 1).reshape(lat_cells, -1)

    cos, sin = place(np.cos(angles)), place(np.sin(angles))
    table = np.block([[cos, sin], [-sin, cos]]) / math.sqrt(lat_cells)
    table = np.pad(table, ((0, 2 * TILE - 2 * lat_cells), (0, 0)))
    return two_parts(table), two_parts(np.ascontiguousarray(table.T))


def lon_all():
    modes = LON // 2 + 1
    phase = np.outer(np.arange(modes), np.arange(LON)) % LON
    angles = phase * (2.0 * math.pi / LON)
    table = np.stack([np.cos(angles), -np.sin(angles)], axis=1).reshape(2 * modes, LON)
    table = table / math.sqrt(LON)
    rows = []
    for r in range(ROWS):
        before = r * LON - TILE_FROM[r] * TILE
        rows.append(
            np.pad(table, ((0, 2 * TILE - 2 * modes), (before, SPAN - LON - before)))
        )
    cells = np.stack(rows)
    return two_parts(np.ascontiguousarray(cells.transpose(0, 2, 1))), two_parts(cells)


def body(
    inputs,
    cotangent,
    first_gain,
    first_shift,
    filter_inner,
    filter_inner_bias,
    filter_outer,
    filter_outer_bias,
    second_gain,
    second_shift,
    up_weight,
    up_bias,
    down_weight,
    down_bias,
    kept_lat,
    kept_lon,
):
    shape = inputs.shape
    cells = ROWS * LON

    def to_tiles(field):
        flat = jnp.pad(field.reshape(CB, cells), ((0, 0), (0, NCH * TILE - cells)))
        return flat.reshape(CB, NCH, TILE).transpose(1, 0, 2)

    def from_tiles(tiles):
        return tiles.transpose(1, 0, 2).reshape(CB, NCH * TILE)[:, :cells].reshape(shape)

    vectors = jnp.stack([first_gain, first_shift, second_gain, second_shift, down_bias], axis=1)
    prm = jnp.concatenate(
        [
            jnp.pad(vectors, ((0, 0), (0, 0), (0, 256 - CB))),
            jnp.pad(up_bias[:, None, :], ((0, 0), (0, 2), (0, 256 - FB))),
        ],
        axis=1,
    ).reshape(32, 256)
    shards = jnp.stack([up_weight.transpose(0, 2, 1), down_weight], axis=1)
    biases = jnp.concatenate([filter_inner_bias[:, :, 0], filter_outer_bias[:, :, 0]], axis=1)
    biases = jnp.tile(jnp.pad(biases, ((0, 0), (0, 4), (0, CP - CB))), (1, 1, 2))
    lon_index = (kept_lon[:, None] * 2 + jnp.arange(2, dtype=jnp.int32)).reshape(1, TILE)
    lat_index = jnp.pad(kept_lat, (0, 64 - kept_lat.shape[0]), constant_values=-4 * LON)
    lat_index = (jnp.arange(2, dtype=jnp.int32)[:, None] * (ROWS * NLAT) + lat_index).reshape(1, TILE)
    index = jnp.concatenate([lon_index, lat_index, jnp.zeros((6, TILE), jnp.int32)], axis=0)
    all_a, all_t = lat_all()
    all_k, all_v = lon_all()
    out_h, out_g, wout, sout, sums, edge = run_stack(
        to_tiles(inputs), to_tiles(cotangent), prm, shards,
        filter_inner.reshape(LAYERS, 2, CB, CB), filter_outer.reshape(LAYERS, 2, CB, CB),
        biases, index, all_a, all_t, all_k, all_v,
    )
    rows = sums[:32].reshape(LAYERS, 8, TILE)
    up_shift_grad = jnp.concatenate([sums[32:36], sums[40:44]], axis=1)[:, :FB]
    wout = wout.reshape(LAYERS, 2, FB, D)
    filters = sout.reshape(LAYERS, 2, CP, 2, CP).transpose(1, 0, 3, 2, 4)
    fbias = filters[:, :, :, CB, :CB]
    filters = filters[:, :, :, :CB, :CB]
    first_rows = jnp.concatenate([edge[None, :2, :CB], rows[1:, :2, :CB]], axis=0)
    return (
        from_tiles(out_h),
        from_tiles(out_g),
        first_rows[:, 0],
        first_rows[:, 1],
        filters[0][:, :, None],
        fbias[0][:, :, None],
        filters[1][:, :, None],
        fbias[1][:, :, None],
        rows[:, 2, :CB],
        rows[:, 3, :CB],
        wout[:, 0].transpose(0, 2, 1),
        up_shift_grad,
        wout[:, 1],
        rows[:, 4, :CB],
    )


def solution(mesh):
    placed = (
        P("ch", "lat", None),
        P("ch", "lat", None),
        P(None, "ch"),
        P(None, "ch"),
        P(None, None, "ch", None, None),
        P(None, None, "ch", None),
        P(None, None, "ch", None, None),
        P(None, None, "ch", None),
        P(None, "ch"),
        P(None, "ch"),
        P(None, None, "ch"),
        P(None, "ch"),
        P(None, "ch", None),
        P(None, "ch"),
        P(),
        P(),
    )
    return jax.shard_map(
        body,
        mesh=mesh,
        in_specs=placed,
        out_specs=(
            P("ch", "lat", None),
            P("ch", "lat", None),
            P(None, "ch"),
            P(None, "ch"),
            P(None, None, "ch", None, None),
            P(None, None, "ch", None),
            P(None, None, "ch", None, None),
            P(None, None, "ch", None),
            P(None, "ch"),
            P(None, "ch"),
            P(None, None, "ch"),
            P(None, "ch"),
            P(None, "ch", None),
            P(None, "ch"),
        ),
        check_vma=False,
    )
```

time: 328 us -> 279 us (0.85)
  Pallas kernels: 303 us -> 262 us
  local copies, waits for them, and re-layouts: 17.4 us -> 13.1 us
  other arithmetic: 6.84 us -> 3.17 us
    pallas_call x1 -> x0, Pallas kernels: 43.2 us -> none  [run_finish(): pl.pallas_call(finish_kernel, out_shape=[jax.ShapeDtypeStruct((2, 8, WROW...]
    unnamed x55 -> x43, local copies, waits for them, and re-layouts: 6.8 us -> 4.34 us
where the time goes in v3:
time: 279 us
  Pallas kernels  262 us (94%)
  local copies, waits for them, and re-layouts  13.1 us (5%)
  other arithmetic  3.17 us (1%)
    pallas_call x1, Pallas kernels, run_stack(): pl.pallas_call(stack_kernel, out_shape=shapes, in_specs=[pl.BlockSpec(mem...  262 us

profile of v3, /device:TPU:1, one launch (start us, length us, event | category | flops | bytes accessed | tf_op | source)
XLA Modules:
  0.0 279.1 jit_solution(174067039466785821)
XLA Ops:
  0.6 0.0 copy-start.3
  0.7 1.1 copy.43
  1.8 0.0 copy-start.1
  1.8 0.0 copy-start.2
  1.8 0.1 reshape.132
  2.0 0.0 copy-done.3
  2.0 0.2 copy.45
  2.1 0.1 reshape.134
  2.3 0.8 bitcast_bitcast_fusion
  3.0 0.0 copy-done.1
  3.1 0.0 copy-done.2
  3.1 0.0 copy-start.9
  3.1 0.0 copy-start.10
  3.1 0.0 copy-start.11
  3.1 0.0 copy-start.12
  3.1 0.0 copy-start.13
  3.1 0.0 copy-start.6
  3.1 0.0 copy-start.7
  3.1 0.0 copy-start.8
  3.1 0.0 copy-start.14
  3.1 0.0 copy-start.15
  3.2 1.1 pad_maximum_fusion.wsh
  4.3 0.0 copy-done.9
  4.3 0.0 copy-done.10
  4.3 0.0 copy-done.11
  4.3 0.0 copy-done.12
  4.4 0.0 copy-done.13
  4.4 0.0 copy-done.6
  4.4 0.6 copy.81
  5.0 0.0 copy-done.7
  5.0 0.0 copy-done.8
  5.1 0.7 tile.10.fb
  5.8 0.0 copy-done.14
  5.8 0.1 iota_add_fusion
  5.9 0.1 add.61
  6.0 0.0 copy-done.15
  6.0 0.1 broadcast_add_fusion
  6.1 0.1 add.65
  6.2 0.1 pad.35.clone
  6.3 0.7 add_add_fusion.idx
  6.9 261.9 %stack.37 = (f32[8,48,128]{2,1,0:T(8,128)}, f32[8,48,128]{2,1,0:T(8,128)}, f32[4,2,8,24,384]{4,3,2,1,0:T(8,128)}, f32[16,32,128]{2,1,0:T(8,128)}, f32[48,128]{1,0:T(8,128)}, /*index=5*/f32[8,128]{1,0:T(8,128)}) custom-call(f32[8,48,128]{2,1,0:T(8,128)} %get-tuple-element.54.x0, f32[8,48,128]{2,1,0:T(8,128)} %get-tuple-element.53.ct, f32[32,256]{1,0:T(8,128)} %bitcast.107, ...), custom_call_target="tpu_custom_call" | custom-call | tf_op jit(solution)/shard_map/stack/pallas_call | solution.py:770
  268.8 0.7 fusion.3
  269.5 0.6 pad_maximum_fusion.1
  270.1 0.7 slice_bitcast_fusion.4
  270.8 0.7 slice.67
  271.5 0.6 fusion.2
  272.1 0.6 fusion.4
  272.7 0.0 copy-start
  272.7 1.4 reshape.144
  274.2 0.8 slice_bitcast_fusion.2
  275.0 0.6 slice_bitcast_fusion.5
  275.6 0.0 copy-done
  275.6 0.0 copy-start.5
  275.6 1.6 slice_bitcast_fusion
  277.1 0.0 copy-start.4
  277.1 0.0 copy-done.5
  277.2 0.2 reshape.140
  277.4 0.8 copy.58
  278.1 0.0 copy-done.4
  278.1 0.2 reshape.142
  278.3 0.8 copy.59
  (17 shorter events, 0.2 us)
Async XLA Ops:
  0.6 1.3 copy-start.3
  1.8 1.3 copy-start.1
  1.8 1.2 copy-start.2
  3.1 1.3 copy-start.9
  3.1 1.3 copy-start.10
  3.1 1.3 copy-start.11
  3.1 1.3 copy-start.12
  3.1 1.3 copy-start.13
  3.1 1.3 copy-start.6
  3.1 1.9 copy-start.7
  3.1 1.9 copy-start.8
  3.1 2.6 copy-start.14
  3.1 2.9 %copy-start.15 = (s32[60]{0:T(128)S(1)}, s32[60]{0:T(128)}, u32[]{:S(2)}) copy-start(s32[60]{0:T(128)} %param.34) | copy-start | bytes 724
  272.7 2.9 %copy-start = (f32[4,2,8,24,384]{4,3,2,1,0:T(8,128)S(1)}, f32[4,2,8,24,384]{4,3,2,1,0:T(8,128)}, u32[]{:S(2)}) copy-start(f32[4,2,8,24,384]{4,3,2,1,0:T(8,128)} %get-tuple-element.25) | copy-start | bytes 7077892
  275.6 1.6 copy-start.5
  277.1 1.0 copy-start.4

commit v4 on v3

--- a/solution.py
+++ b/solution.py
@@ -29,7 +29,8 @@
 FB = 192
 FF = NCH * FB
 CHUNK = 384
-WROWS = FB // 8
+WROWS = 32
+SHARES = FB // WROWS
 TILE_FROM = [r * LON // TILE for r in range(ROWS)]
 TILE_TO = [-(-(r + 1) * LON // TILE) for r in range(ROWS)]
 SPAN = max(b - a for a, b in zip(TILE_FROM, TILE_TO)) * TILE
@@ -78,30 +79,36 @@
 
 def stack_kernel(
     x0, ct, prm, wsh, fi, fo, fb, idx, all_a, all_t, all_k, all_v,
-    out_h, out_g, wout, sout, rout, eout,
+    out_h, out_g, wout, sout, rout,
     h_s, g_s, xin, pbuf, pcol, bcol, mbuf, fbuf, sbuf, sbuf2, xbuf, zbuf, cbuf, bbuf,
     wall, wT, n1_s, n2_s, r1_s, r2_s, lifted_s, pre_s, hid_s, y_s, hh_s, t_s,
-    xs, prs, gr, psend, pget, gsend, gget, pc, pin, bc, brow, bin_s, ig_s, mg_s, bwf,
+    xs, prs, gr, psend, pget, gsend, gget, pc, pin, bc, brow, bin_s, pr, ig_s, igr, mixr_s, bwf, k_s, v_s,
     bw, bt, la, lt, lk, lv,
-    gw, wget, wsum, gf, fget, fsum, gpsum, gpget, late, lin, lsum, lget,
+    gw, wget, wsum, gf, fget, fsum, gpsum, gpget,
     bsem_s, bsem_r, asem_s, asem_r, psem_s, psem_r, gsem_s, gsem_r, qsem_s, qsem_r,
-    c_s, c_r, l_s, l_r, w1_s, w1_r, w2_s, w2_r, f_s, f_r,
+    c_s, c_r, l_s, l_r, t_sem, w1_s, w1_r, w2_s, w2_r, f_s, f_r,
 ):
     ch = lax.axis_index("ch")
     lat = lax.axis_index("lat")
     core = lax.rem(lat, 2)
     partner = lat + 1 - 2 * core
-    flip = lat + 2 - 4 * lax.rem(lat // 2, 2)
+
+
+    def flipped(at):
+        return at + 2 - 4 * lax.rem(at // 2, 2)
+
+    flip = flipped(lat)
+    half = lax.rem(ch, 2)
+    rank = lat + half * (flip - lat)
     ch_peer = [lax.rem(ch + s, NCH) for s in range(NCH)]
     lat_peer = [lax.rem(lat + s, NLAT) for s in range(NLAT)]
 
     barrier = pltpu.get_barrier_semaphore()
     for s in range(1, NCH):
         pl.semaphore_signal(barrier, inc=1, device_id={"ch": ch_peer[s]}, device_id_type=MESH)
-        if s % 2:
-            pl.semaphore_signal(
-                barrier, inc=1, device_id={"lat": flip, "ch": ch_peer[s]}, device_id_type=MESH
-            )
+        pl.semaphore_signal(
+            barrier, inc=1, device_id={"lat": flip, "ch": ch_peer[s]}, device_id_type=MESH
+        )
     for s in range(1, NLAT):
         pl.semaphore_signal(barrier, inc=1, device_id={"lat": lat_peer[s]}, device_id_type=MESH)
 
@@ -110,15 +117,6 @@
             src_ref=src, dst_ref=dst, send_sem=send, recv_sem=recv,
             device_id=where, device_id_type=MESH,
         )
-
-    def over_ch(src, dst, send, recv):
-        copies = [
-            remote(src(ch_peer[s]), dst, send.at[s], recv.at[s], {"ch": ch_peer[s]})
-            for s in range(1, NCH)
-        ]
-        for copy in copies:
-            copy.start()
-        return copies
 
     def over_near(src, dst, send, recv):
         copies = []
@@ -127,6 +125,37 @@
             copies.append(remote(src(ch_peer[s]), dst, send.at[s], recv.at[s], where))
         return copies
 
+    def between(src, dst, at, inward):
+        copies = []
+        for s in range(NCH):
+            there = lat + lax.rem(half + s, 2) * (flip - lat) if inward else rank
+            where = {"lat": there, "ch": ch_peer[s]}
+            copies.append(remote(src(ch_peer[s]), dst, bsem_s.at[at, s], bsem_r.at[at, s], where))
+        return copies
+
+    def between_start(src, dst, at, inward, keep):
+        copies = between(src, dst, at, inward)
+        for copy in copies[1:]:
+            copy.start()
+
+        @pl.when(half == 1)
+        def _():
+            copies[0].start()
+
+        @pl.when(half == 0)
+        def _():
+            keep()
+
+        return copies
+
+    def between_done(copies):
+        for copy in copies[1:]:
+            copy.wait()
+
+        @pl.when(half == 1)
+        def _():
+            copies[0].wait()
+
     def to_lat(src, dst, send, recv):
         return [
             remote(src(lat_peer[s]), dst, send.at[s], recv.at[s], {"lat": lat_peer[s]})
@@ -160,28 +189,42 @@
         block = wall.at[layer, core]
         return remote(block, block, psem_s.at[layer], psem_r.at[layer], {"lat": partner})
 
+    def own_weights(layer):
+        mine = wall.at[layer, core, pl.ds(pl.multiple_of(ch * FB, FB), FB)]
+        return pltpu.make_async_copy(wsh.at[layer, core], mine, t_sem.at[2 + layer])
+
     def weights_start(layer):
         for copy in weights_near(layer):
             copy.start()
+        own_weights(layer).start()
 
     def weights_pass(layer):
-        wall[layer, core, pl.ds(pl.multiple_of(ch * FB, FB), FB)] = wsh[layer, core]
         done(weights_near(layer))
+        own_weights(layer).wait()
         weights_pair(layer).start()
 
     def weights_done(layer):
         weights_pair(layer).wait()
 
-    xin[0, ch] = x0[ch]
-    xin[1, ch] = ct[ch]
+    get_k = pltpu.make_async_copy(all_k, k_s, t_sem.at[0])
+    get_v = pltpu.make_async_copy(all_v, v_s, t_sem.at[1])
+    get_k.start()
+    get_v.start()
     pbuf[ch] = prm[...]
-    pl.semaphore_wait(barrier, 2 * (NCH - 1) + NLAT - 1 - 3)
-    first = over_ch(lambda p: x0.at[p], xin.at[0, ch], bsem_s.at[0], bsem_r.at[0])
-    first += over_ch(lambda p: prm, pbuf.at[ch], bsem_s.at[1], bsem_r.at[1])
+    pl.semaphore_wait(barrier, 2 * (NCH - 1) + NLAT - 1)
+
+    def keep_x():
+        xin[0, ch] = x0[ch]
+
+    def keep_ct():
+        xin[1, ch] = ct[ch]
+
+    first = between_start(lambda p: x0.at[p], xin.at[0, ch], 0, True, keep_x)
+    params = start(over_near(lambda p: prm, pbuf.at[ch], bsem_s.at[1], bsem_r.at[1]))
     weights_start(0)
     pc[...] = jnp.zeros(pc.shape, F32)
     bc[...] = jnp.zeros(bc.shape, F32)
-    late[...] = jnp.zeros(late.shape, F32)
+    pr[...] = jnp.zeros(pr.shape, F32)
     bwf[...] = jnp.zeros(bwf.shape, F32)
 
     def picker(at):
@@ -193,31 +236,44 @@
 
     ends = (idx[0:1, :] < 2) | (idx[0:1, :] >= 180)
     mode_weight = jnp.where(ends, 1.0, 2.0)
-    pick = picker(0)
-    pick_t = jnp.concatenate([turn(pick), turn(pick * mode_weight)], axis=0).astype(BF16)
-    pick = pick.astype(BF16)
-    for part in range(2):
-        for r in range(ROWS):
-            table = mb(all_k[part, r], pick)
-            lk[part, 0, r] = table.astype(BF16)
-            lk[part, 1, r] = (table * mode_weight).astype(BF16)
-            table = mb(pick_t, all_v[part, r]).astype(BF16)
-            lv[part, 0, r] = table[:TILE]
-            lv[part, 1, r] = table[TILE:]
-    pick = picker(1)
-    pick_t = turn(pick).astype(BF16)
-    pick = pick.astype(BF16)
-    for part in range(2):
-        la[part] = mb(pick_t, all_a[part]).astype(BF16)
-        lt[part] = mb(all_t[part], pick).astype(BF16)
-    done(first)
-    second = over_ch(lambda p: ct.at[p], xin.at[1, ch], bsem_s.at[2], bsem_r.at[2])
-    for j in range(NCH):
-        turned = jnp.transpose(pbuf[j])
-        for layer in range(LAYERS):
-            part = turned[:, layer * 8 : layer * 8 + 8]
-            pcol[layer, j * CB : (j + 1) * CB, 0:8] = part[:CB]
-            bcol[layer, j * FB : (j + 1) * FB, 0:8] = part[:FB]
+
+    def first_tables():
+        get_k.wait()
+        pick = picker(0).astype(BF16)
+        for part in range(2):
+            for r in range(ROWS):
+                table = mb(k_s[part, r], pick)
+                lk[part, 0, r] = table.astype(BF16)
+                lk[part, 1, r] = (table * mode_weight).astype(BF16)
+
+    def other_tables():
+        get_v.wait()
+        pick = picker(0)
+        pick_t = jnp.concatenate([turn(pick), turn(pick * mode_weight)], axis=0).astype(BF16)
+        for part in range(2):
+            for r in range(ROWS):
+                table = mb(pick_t, v_s[part, r]).astype(BF16)
+                lv[part, 0, r] = table[:TILE]
+                lv[part, 1, r] = table[TILE:]
+        pick = picker(1)
+        pick_t = turn(pick).astype(BF16)
+        pick = pick.astype(BF16)
+        for part in range(2):
+            la[part] = mb(pick_t, all_a[part]).astype(BF16)
+            lt[part] = mb(all_t[part], pick).astype(BF16)
+
+    def columns(held, width, count):
+        for j in range(NCH):
+            turned = jnp.transpose(pbuf[j, :, :width])
+            for layer in range(LAYERS):
+                part = turned[:, layer * 8 : layer * 8 + 8]
+                held[layer, j * count : (j + 1) * count, 0:8] = part[:count]
+
+    first_tables()
+    done(params)
+    columns(pcol, TILE, CB)
+    between_done(first)
+    second = between_start(lambda p: ct.at[p], xin.at[1, ch], 2, True, keep_ct)
     h_s[...] = xin[0]
 
     lane = lax.broadcasted_iota(jnp.int32, (NLAT, TILE), 1)
@@ -318,18 +374,25 @@
 
     def exchange_one(value):
         mbuf[...] = value.reshape(NCH, CB, TILE)
-        copies = over_ch(lambda p: mbuf.at[p], fbuf.at[ch], c_s.at[0], c_r.at[0])
+        copies = start(over_near(lambda p: mbuf.at[p], fbuf.at[ch], c_s.at[0], c_r.at[0]))
         fbuf[ch] = mbuf[ch]
         return copies
 
     def exchange_four():
-        copies = over_ch(lambda p: cbuf.at[p], bbuf.at[ch], c_s.at[1], c_r.at[1])
+        copies = start(over_near(lambda p: cbuf.at[p], bbuf.at[ch], c_s.at[1], c_r.at[1]))
         bbuf[ch] = cbuf[ch]
         return copies
 
     def exchange_lat(src, dst, at):
-        copies = start(to_lat(lambda p: src.at[p], dst.at[lat], l_s.at[at], l_r.at[at]))
-        dst[lat] = src[lat]
+        copies = []
+        for s in range(1, NLAT):
+            peer = lax.rem(rank + s, NLAT)
+            there = peer + half * (flipped(peer) - peer)
+            copies.append(
+                remote(src.at[peer], dst.at[rank], l_s.at[at, s], l_r.at[at, s], {"lat": there})
+            )
+        start(copies)
+        dst[rank] = src[rank]
         return copies
 
     def col(layer, at):
@@ -346,11 +409,21 @@
         mixed = n1 * col(layer, 0) + col(layer, 1)
         one = exchange_one(mixed)
         ig_s[...] = h + mixed
+
+        @pl.when(layer == 0)
+        def _():
+            other_tables()
+
         filter_tables(layer)
         arrived(one)
         lon_to_modes(0)
         two = exchange_lat(sbuf, xbuf, 0)
         sent(one)
+        mixr_s[layer] = fbuf[...]
+
+        @pl.when(layer == 0)
+        def _():
+            columns(bcol, 256, FB)
 
         @pl.when(layer < LAYERS - 1)
         def _():
@@ -398,9 +471,15 @@
         return carry
 
     lax.fori_loop(0, LAYERS, forward, 0)
-    last_h = over_ch(lambda p: h_s.at[p], out_h.at[ch], bsem_s.at[3], bsem_r.at[3])
-    out_h[ch] = h_s[ch]
-    done(second)
+
+    def keep_h():
+        out_h[ch] = h_s[ch]
+
+    def keep_g():
+        out_g[ch] = g_s[ch]
+
+    last_h = between_start(lambda p: h_s.at[p], out_h.at[ch], 3, False, keep_h)
+    between_done(second)
     g_s[...] = xin[1]
     ones = jnp.ones((8, TILE), F32)
 
@@ -450,33 +529,80 @@
         total = gget[slot, 0].astype(F32)
         for j in range(1, NCH):
             total = total + gget[slot, j].astype(F32)
-        gw[layer] = total.reshape(8, WROWS, D)
+        gw[layer] = total.astype(BF16).reshape(SHARES, WROWS, D)
 
     near = lat // 2
+    evens = range(2, NLAT, 2)
 
     def sum_share(layer):
-        return [
-            remote(
-                gw.at[layer, lat_peer[s] // 2], wget.at[layer, near],
-                w1_s.at[layer, s], w1_r.at[layer, s], {"lat": lat_peer[s]},
-            )
-            for s in range(2, NLAT, 2)
-        ]
-
-    def sum_give(layer):
-        return to_lat(
-            lambda p: wsum.at[layer], wout.at[layer, core, near], w2_s.at[layer], w2_r.at[layer]
+        for s in evens:
+            there = lat_peer[s] // 2
+
+            @pl.when(there < SHARES)
+            def _():
+                share_copy(layer, s).start()
+
+    def share_copy(layer, s):
+        return remote(
+            gw.at[layer, lat_peer[s] // 2], wget.at[layer, near],
+            w1_s.at[layer, s], w1_r.at[layer, s], {"lat": lat_peer[s]},
         )
 
+    def arriving(layer, s):
+        return remote(
+            wget.at[layer, near], wget.at[layer, near],
+            w1_s.at[layer, s], w1_r.at[layer, s], {"lat": lat_peer[s]},
+        )
+
+    def give_copy(layer, s):
+        return remote(
+            wsum.at[layer], wout.at[core, layer, near],
+            w2_s.at[layer, s], w2_r.at[layer, s], {"lat": lat_peer[s]},
+        )
+
+    def given(layer, s):
+        return remote(
+            wsum.at[layer], wsum.at[layer],
+            w2_s.at[layer, s], w2_r.at[layer, s], {"lat": lat_peer[s]},
+        )
+
     def sum_pass(layer):
-        wget[layer, near] = gw[layer, near]
-        done(sum_share(layer))
-        total = wget[layer, 0]
-        for j in range(1, 8):
-            total = total + wget[layer, j]
-        wsum[layer] = total
-        wout[layer, core, near] = total
-        start(sum_give(layer))
+        for s in evens:
+
+            @pl.when(lat_peer[s] // 2 < SHARES)
+            def _():
+                share_copy(layer, s).wait_send()
+
+        @pl.when(near < SHARES)
+        def _():
+            wget[layer, near] = gw[layer, near]
+            for s in evens:
+                arriving(layer, s).wait_recv()
+            total = wget[layer, 0].astype(F32)
+            for j in range(1, 8):
+                total = total + wget[layer, j].astype(F32)
+            wsum[layer] = total.astype(BF16)
+            for s in evens:
+                give_copy(layer, s).start()
+            wout[core, layer, near] = wsum[layer]
+
+    def hand_copy(layer):
+        whole = wout.at[core, layer]
+        return remote(whole, whole, w2_s.at[layer, 0], w2_r.at[layer, 0], {"lat": partner})
+
+    def sum_hand(layer):
+        @pl.when(near < SHARES)
+        def _():
+            for s in evens:
+                give_copy(layer, s).wait_send()
+
+        for s in evens:
+
+            @pl.when(lax.rem(near + 8 - s // 2, 8) < SHARES)
+            def _():
+                given(layer, s).wait_recv()
+
+        hand_copy(layer).start()
 
     def filters_share():
         return to_lat(lambda p: gf.at[p], fget.at[lat], f_s.at[0], f_r.at[0])
@@ -487,7 +613,8 @@
     def rows_share():
         copies = []
         for s in range(1, NCH):
-            p, where = ch_peer[s], {"ch": ch_peer[s]}
+            p = ch_peer[s]
+            where = {"lat": flip, "ch": p} if s % 2 else {"ch": p}
             copies.append(remote(pc.at[p], pin.at[ch], bsem_s.at[5, s], bsem_r.at[5, s], where))
             copies.append(
                 remote(brow.at[p], bin_s.at[ch], bsem_s.at[7, s], bsem_r.at[7, s], where)
@@ -501,7 +628,7 @@
         pin[ch] = pc[ch]
         bin_s[ch] = brow[ch]
         done(rows_share())
-        total, hidden = pin[0], bin_s[0]
+        total, hidden = pin[0] + pr[...], bin_s[0]
         for j in range(1, NCH):
             total, hidden = total + pin[j], hidden + bin_s[j]
         tall = jnp.concatenate([total, jnp.zeros((TILE - CB, TILE), F32)], axis=0)
@@ -543,11 +670,16 @@
         lon_to_modes(1)
         two = exchange_lat(sbuf, xbuf, 0)
         sent(one)
+        igr[...] = fbuf[...]
 
         @pl.when(layer < LAYERS - 1)
         def _():
             grads_done(layer + 1)
-            start(sum_share(layer + 1))
+            sum_share(layer + 1)
+
+        @pl.when(layer < LAYERS - 2)
+        def _():
+            sum_hand(layer + 2)
 
         grads_pair(layer).wait()
         gsend[...] = (gr[core] + pget[...].astype(F32)).astype(BF16).reshape(NCH, FB, D)
@@ -602,6 +734,11 @@
         lon_to_cells(0)
         four = exchange_four()
         sent(three)
+        both = igr[...] + cbuf[...]
+        plain = jnp.sum(jnp.sum(both, axis=0), axis=1, keepdims=True)
+        cross = jnp.sum(jnp.sum(both * mixr_s[layer], axis=0), axis=1, keepdims=True)
+        lanes_c = lax.broadcasted_iota(jnp.int32, (CB, TILE), 1) - layer * 8
+        pr[...] = jnp.where(lanes_c == 0, plain, jnp.where(lanes_c == 1, cross, pr[...]))
 
         @pl.when(layer < LAYERS - 1)
         def _():
@@ -619,7 +756,7 @@
             start(filters_give())
             rows_pass()
             grads_done(0)
-            start(sum_share(0))
+            sum_share(0)
 
         arrived(four)
         inner_grad = ig_s[...]
@@ -630,59 +767,33 @@
         m2 = jnp.sum(q1 * n1, axis=0, keepdims=True) * (1.0 / D)
         g = inner_grad + r1_s[layer, 0:1, :] * (q1 - m1 - n1 * m2)
         g_s[...] = g.reshape(NCH, CB, TILE)
-        mg_s[...] = mixed_grad
-
-        @pl.when(layer > 0)
-        def _():
-            cell_sums(layer, 0, mixed_grad * n1)
-            cell_sums(layer, 1, mixed_grad)
-
         sent(four)
         return carry
 
     lax.fori_loop(0, LAYERS, backward, 0)
-    final = over_ch(lambda p: g_s.at[p], out_g.at[ch], bsem_s.at[4], bsem_r.at[4])
-    out_g[ch] = g_s[ch]
-    mixed_grad = mg_s[...]
-    for at, value in enumerate((mixed_grad * n1_s[0], mixed_grad)):
-        for j in range(NCH):
-            part = mm(ones, value[j * CB : (j + 1) * CB], NT)
-            late[j, at : at + 1, 0:CB] = part[0:1]
-    late_copies = over_ch(lambda p: late.at[p], lin.at[ch], bsem_s.at[6], bsem_r.at[6])
-    lin[ch] = late[ch]
+    final = between_start(lambda p: g_s.at[p], out_g.at[ch], 4, False, keep_g)
+    sum_hand(1)
     sum_pass(0)
-    done(late_copies)
-    total = lin[0]
-    for j in range(1, NCH):
-        total = total + lin[j]
-    lsum[...] = total
-    lget[lat] = total
-    give_late = start(to_lat(lambda p: lsum, lget.at[lat], f_s.at[3], f_r.at[3]))
-    done(last_h)
-    done(final)
+    sum_hand(0)
+    between_done(last_h)
+    between_done(final)
     done(filters_give())
     for layer in range(LAYERS):
-        done(sum_give(layer))
+        hand_copy(layer).wait()
     done(rows_give())
     total = gpget[0]
     for j in range(1, NLAT):
         total = total + gpget[j]
     rout[...] = total
-    done(give_late)
-    total = lget[0]
-    for j in range(1, NLAT):
-        total = total + lget[j]
-    eout[...] = total
 
 
 def run_stack(*args):
     shapes = [
         jax.ShapeDtypeStruct((NCH, CB, TILE), F32),
         jax.ShapeDtypeStruct((NCH, CB, TILE), F32),
-        jax.ShapeDtypeStruct((LAYERS, 2, 8, WROWS, D), F32),
+        jax.ShapeDtypeStruct((2, LAYERS, SHARES, WROWS, D), BF16),
         jax.ShapeDtypeStruct((NLAT, 32, TILE), F32),
         jax.ShapeDtypeStruct((48, TILE), F32),
-        jax.ShapeDtypeStruct((8, TILE), F32),
     ]
     v = pltpu.VMEM
     dma = pltpu.SemaphoreType.DMA
@@ -725,27 +836,27 @@
         v((FF, TILE), F32),
         v((NCH, 8, 256), F32),
         v((NCH, 8, 256), F32),
+        v((CB, TILE), F32),
         v((D, TILE), F32),
-        v((D, TILE), F32),
+        v((NCH, CB, TILE), F32),
+        v((LAYERS, NCH, CB, TILE), F32),
         v((TILE, 256), F32),
+        v((2, ROWS, SPAN, 256), BF16),
+        v((2, ROWS, 256, SPAN), BF16),
         v((2, LAYERS, 2, TILE, 256), BF16),
         v((2, LAYERS, 2, TILE, 256), BF16),
         v((2, TILE, 2 * ROWS * NLAT), BF16),
         v((2, 2 * ROWS * NLAT, TILE), BF16),
         v((2, 2, ROWS, SPAN, TILE), BF16),
         v((2, 2, ROWS, TILE, SPAN), BF16),
-        v((LAYERS, 8, WROWS, D), F32),
-        v((LAYERS, 8, WROWS, D), F32),
-        v((LAYERS, WROWS, D), F32),
+        v((LAYERS, SHARES, WROWS, D), BF16),
+        v((LAYERS, 8, WROWS, D), BF16),
+        v((LAYERS, WROWS, D), BF16),
         v((NLAT, 32, TILE), F32),
         v((NLAT, 32, TILE), F32),
         v((32, TILE), F32),
         v((48, TILE), F32),
         v((NLAT, 48, TILE), F32),
-        v((NCH, 8, TILE), F32),
-        v((NCH, 8, TILE), F32),
-        v((8, TILE), F32),
-        v((NLAT, 8, TILE), F32),
         dma((8, NCH)),
         dma((8, NCH)),
         dma((LAYERS, NCH)),
@@ -760,6 +871,7 @@
         dma((2, NCH)),
         dma((2, NLAT)),
         dma((2, NLAT)),
+        dma((2 + LAYERS,)),
         dma((LAYERS, NLAT)),
         dma((LAYERS, NLAT)),
         dma((LAYERS, NLAT)),
@@ -770,7 +882,10 @@
     return pl.pallas_call(
         stack_kernel,
         out_shape=shapes,
-        in_specs=[pl.BlockSpec(memory_space=pltpu.VMEM)] * len(args),
+        in_specs=[
+            pl.BlockSpec(memory_space=pl.ANY if at in (3, 10, 11) else pltpu.VMEM)
+            for at in range(len(args))
+        ],
         out_specs=[pl.BlockSpec(memory_space=pltpu.VMEM)] * len(shapes),
         scratch_shapes=scratch,
         compiler_params=pltpu.CompilerParams(
@@ -860,32 +975,32 @@
     index = jnp.concatenate([lon_index, lat_index, jnp.zeros((6, TILE), jnp.int32)], axis=0)
     all_a, all_t = lat_all()
     all_k, all_v = lon_all()
-    out_h, out_g, wout, sout, sums, edge = run_stack(
+    out_h, out_g, wout, sout, sums = run_stack(
         to_tiles(inputs), to_tiles(cotangent), prm, shards,
         filter_inner.reshape(LAYERS, 2, CB, CB), filter_outer.reshape(LAYERS, 2, CB, CB),
         biases, index, all_a, all_t, all_k, all_v,
     )
     rows = sums[:32].reshape(LAYERS, 8, TILE)
     up_shift_grad = jnp.concatenate([sums[32:36], sums[40:44]], axis=1)[:, :FB]
-    wout = wout.reshape(LAYERS, 2, FB, D)
+    wout = wout.reshape(2, LAYERS, FB, D)
     filters = sout.reshape(LAYERS, 2, CP, 2, CP).transpose(1, 0, 3, 2, 4)
     fbias = filters[:, :, :, CB, :CB]
     filters = filters[:, :, :, :CB, :CB]
-    first_rows = jnp.concatenate([edge[None, :2, :CB], rows[1:, :2, :CB]], axis=0)
+    plain, cross = rows[:, 0, :CB], rows[:, 1, :CB]
     return (
         from_tiles(out_h),
         from_tiles(out_g),
-        first_rows[:, 0],
-        first_rows[:, 1],
+        (cross - first_shift * plain) / first_gain,
+        plain,
         filters[0][:, :, None],
         fbias[0][:, :, None],
         filters[1][:, :, None],
         fbias[1][:, :, None],
         rows[:, 2, :CB],
         rows[:, 3, :CB],
-        wout[:, 0].transpose(0, 2, 1),
+        wout[0].transpose(0, 2, 1).astype(F32),
         up_shift_grad,
-        wout[:, 1],
+        wout[1].astype(F32),
         rows[:, 4, :CB],
     )
 

time: 279 us -> 269 us (0.964)
  Pallas kernels: 262 us -> 252 us
    pallas_call x1, Pallas kernels: 262 us -> 252 us  [run_stack(): pl.pallas_call(stack_kernel, out_shape=shapes, in_specs=[pl.BlockSpec(mem...]
where the time goes in v4:
time: 269 us
  Pallas kernels  252 us (94%)
  local copies, waits for them, and re-layouts  11 us (4%)
  other arithmetic  5.35 us (2%)
    pallas_call x1, Pallas kernels, run_stack(): pl.pallas_call(stack_kernel, out_shape=shapes, in_specs=[pl.BlockSpec(mem...  252 us

profile of v4, /device:TPU:1, one launch (start us, length us, event | category | flops | bytes accessed | tf_op | source)
XLA Modules:
  0.0 269.1 jit_solution(18028772734571033799)
XLA Ops:
  0.6 0.0 copy-start.3
  0.7 1.1 copy.41
  1.8 0.0 copy-start.1
  1.8 0.0 copy-start.2
  1.8 0.1 reshape.138
  2.0 0.0 copy-done.3
  2.0 0.2 copy.43
  2.1 0.1 reshape.140
  2.3 0.8 bitcast_bitcast_fusion
  3.0 0.0 copy-done.1
  3.1 0.0 copy-done.2
  3.1 0.0 copy-start.7
  3.1 0.0 copy-start.8
  3.1 0.0 copy-start.12
  3.1 0.0 copy-start.13
  3.1 0.0 copy-start.14
  3.1 0.0 copy-start.9
  3.1 0.0 copy-start.10
  3.1 0.0 copy-start.11
  3.1 0.0 copy-start.15
  3.1 0.0 copy-start.16
  3.2 1.1 pad_maximum_fusion.wsh
  4.3 0.0 copy-done.7
  4.3 0.0 copy-done.8
  4.3 0.0 copy-done.12
  4.3 0.0 copy-done.13
  4.4 0.0 copy-done.14
  4.4 0.0 copy-done.9
  4.4 0.6 copy.76
  5.0 0.0 copy-done.10
  5.0 0.0 copy-done.11
  5.1 0.7 tile.10.fb
  5.8 0.0 copy-done.15
  5.8 0.1 iota_add_fusion
  5.9 0.1 add.61
  6.0 0.0 copy-done.16
  6.0 0.1 broadcast_add_fusion
  6.1 0.1 add.65
  6.2 0.1 pad.33.clone
  6.3 0.7 add_add_fusion.idx
  6.9 251.9 %stack.37 = (f32[8,48,128]{2,1,0:T(8,128)}, f32[8,48,128]{2,1,0:T(8,128)}, bf16[2,4,6,32,384]{4,3,2,1,0:T(8,128)(2,1)}, f32[16,32,128]{2,1,0:T(8,128)}, f32[48,128]{1,0:T(8,128)}) custom-call(f32[8,48,128]{2,1,0:T(8,128)} %get-tuple-element.52.x0, f32[8,48,128]{2,1,0:T(8,128)} %get-tuple-element.51.ct, f32[32,256]{1,0:T(8,128)} %bitcast.102, ...), custom_call_target="tpu_custom_call" | custom-call | tf_op jit(solution)/shard_map/stack/pallas_call | solution.py:882
  258.8 0.7 slice_bitcast_fusion.2
  259.5 0.6 fusion.2
  260.1 0.0 copy-start.6
  260.1 0.6 subtract_divide_fusion
  260.7 0.7 fusion.1
  261.4 0.6 pad_maximum_fusion.1
  262.0 0.0 copy-start
  262.0 1.4 reshape.150
  263.4 0.8 slice_bitcast_fusion
  264.2 0.0 copy-done.6
  264.2 0.6 slice_bitcast_fusion.3
  264.8 0.0 copy-done
  264.8 0.1 fusion
  264.9 1.1 convert.4
  266.0 0.0 copy-start.5
  266.0 1.1 convert_bitcast_fusion
  267.1 0.0 copy-start.4
  267.1 0.0 copy-done.5
  267.1 0.2 reshape.146
  267.3 0.8 copy.54
  268.1 0.0 copy-done.4
  268.1 0.2 reshape.148
  268.3 0.8 copy.55
  (15 shorter events, 0.2 us)
Async XLA Ops:
  0.6 1.3 copy-start.3
  1.8 1.3 copy-start.1
  1.8 1.2 copy-start.2
  3.1 1.3 copy-start.7
  3.1 1.3 copy-start.8
  3.1 1.3 copy-start.12
  3.1 1.3 copy-start.13
  3.1 1.3 copy-start.14
  3.1 1.3 copy-start.9
  3.1 1.9 copy-start.10
  3.1 1.9 copy-start.11
  3.1 2.6 copy-start.15
  3.1 2.9 %copy-start.16 = (s32[60]{0:T(128)S(1)}, s32[60]{0:T(128)}, u32[]{:S(2)}) copy-start(s32[60]{0:T(128)} %param.34) | copy-start | bytes 724
  260.1 4.1 %copy-start.6 = (f32[4,1,48]{2,1,0:T(1,128)}, f32[4,1,48]{2,1,0:T(1,128)S(1)}, u32[]{:S(2)}) copy-start(f32[4,1,48]{2,1,0:T(1,128)S(1)} %get-tuple-element.49) | copy-start | bytes 2308
  262.0 2.8 %copy-start = (bf16[2,4,6,32,384]{4,3,2,1,0:T(8,128)(2,1)S(1)}, bf16[2,4,6,32,384]{4,3,2,1,0:T(8,128)(2,1)}, u32[]{:S(2)}) copy-start(bf16[2,4,6,32,384]{4,3,2,1,0:T(8,128)(2,1)} %get-tuple-element.23) | copy-start | bytes 3538948
  266.0 1.1 copy-start.5
  267.1 1.0 copy-start.4

commit v5 on v4

--- a/solution.py
+++ b/solution.py
@@ -29,6 +29,7 @@
 FB = 192
 FF = NCH * FB
 CHUNK = 384
+QB = FB // 4
 WROWS = 32
 SHARES = FB // WROWS
 TILE_FROM = [r * LON // TILE for r in range(ROWS)]
@@ -86,7 +87,7 @@
     bw, bt, la, lt, lk, lv,
     gw, wget, wsum, gf, fget, fsum, gpsum, gpget,
     bsem_s, bsem_r, asem_s, asem_r, psem_s, psem_r, gsem_s, gsem_r, qsem_s, qsem_r,
-    c_s, c_r, l_s, l_r, t_sem, w1_s, w1_r, w2_s, w2_r, f_s, f_r,
+    c_s, c_r, l_s, l_r, t_sem, ysem_s, ysem_r, w1_s, w1_r, w2_s, w2_r, f_s, f_r,
 ):
     ch = lax.axis_index("ch")
     lat = lax.axis_index("lat")
@@ -179,28 +180,40 @@
         for copy in copies:
             copy.wait()
 
+    quarter = lat // 4
+
     def weights_near(layer):
-        mine = wall.at[layer, core, pl.ds(pl.multiple_of(ch * FB, FB), FB)]
-        return over_near(
-            lambda p: wsh.at[layer, core], mine, asem_s.at[layer], asem_r.at[layer]
-        )
+        source = wsh.at[layer, core, pl.ds(pl.multiple_of(quarter * QB, QB), QB)]
+        mine = wall.at[layer, core, quarter, pl.ds(pl.multiple_of(ch * QB, QB), QB)]
+        return over_near(lambda p: source, mine, asem_s.at[layer], asem_r.at[layer])
+
+    def own_weights(layer):
+        source = wsh.at[layer, core, pl.ds(pl.multiple_of(quarter * QB, QB), QB)]
+        mine = wall.at[layer, core, quarter, pl.ds(pl.multiple_of(ch * QB, QB), QB)]
+        return pltpu.make_async_copy(source, mine, t_sem.at[2 + layer])
+
+    def weights_along(layer):
+        block = wall.at[layer, core, quarter]
+        return [
+            remote(block, block, ysem_s.at[layer, s], ysem_r.at[layer, s], {"lat": lat_peer[4 * s]})
+            for s in range(1, 4)
+        ]
 
     def weights_pair(layer):
         block = wall.at[layer, core]
         return remote(block, block, psem_s.at[layer], psem_r.at[layer], {"lat": partner})
 
-    def own_weights(layer):
-        mine = wall.at[layer, core, pl.ds(pl.multiple_of(ch * FB, FB), FB)]
-        return pltpu.make_async_copy(wsh.at[layer, core], mine, t_sem.at[2 + layer])
-
     def weights_start(layer):
-        for copy in weights_near(layer):
-            copy.start()
+        start(weights_near(layer))
         own_weights(layer).start()
 
-    def weights_pass(layer):
+    def weights_spread(layer):
         done(weights_near(layer))
         own_weights(layer).wait()
+        start(weights_along(layer))
+
+    def weights_pass(layer):
+        done(weights_along(layer))
         weights_pair(layer).start()
 
     def weights_done(layer):
@@ -267,7 +280,12 @@
             turned = jnp.transpose(pbuf[j, :, :width])
             for layer in range(LAYERS):
                 part = turned[:, layer * 8 : layer * 8 + 8]
-                held[layer, j * count : (j + 1) * count, 0:8] = part[:count]
+                if count == CB:
+                    held[layer, j * CB : (j + 1) * CB, 0:8] = part[:CB]
+                else:
+                    for y in range(4):
+                        at = y * CHUNK + j * QB
+                        held[layer, at : at + QB, 0:8] = part[y * QB : (y + 1) * QB]
 
     first_tables()
     done(params)
@@ -412,12 +430,14 @@
 
         @pl.when(layer == 0)
         def _():
+            weights_spread(0)
             other_tables()
 
         filter_tables(layer)
         arrived(one)
         lon_to_modes(0)
         two = exchange_lat(sbuf, xbuf, 0)
+        weights_pass(layer)
         sent(one)
         mixr_s[layer] = fbuf[...]
 
@@ -441,14 +461,18 @@
         scatter_lat(table_times(lt[0], lt[1], b - shrink_level * t))
         three = exchange_lat(sbuf2, zbuf, 1)
         sent(two)
-        weights_pass(layer)
         arrived(three)
         lon_to_cells(1)
         four = exchange_four()
         sent(three)
+
+        @pl.when(layer < LAYERS - 1)
+        def _():
+            weights_spread(layer + 1)
+
         weights_done(layer)
         for at in range(0, FF, CHUNK):
-            wT[:, at : at + CHUNK] = jnp.transpose(wall[layer, 1, at : at + CHUNK, :])
+            wT[:, at : at + CHUNK] = jnp.transpose(wall[layer, 1, at // CHUNK])
         arrived(four)
         inner = ig_s[...] + bbuf[...].reshape(D, TILE)
         mean = jnp.sum(inner, axis=0, keepdims=True) * (1.0 / D)
@@ -461,7 +485,7 @@
         lifted_s[layer] = lifted
         total = inner + col(layer, 4)
         for at in range(0, FF, CHUNK):
-            pre = mb(wall[layer, 0, at : at + CHUNK, :], lifted) + bcol[layer, at : at + CHUNK, 5:6]
+            pre = mb(wall[layer, 0, at // CHUNK], lifted) + bcol[layer, at : at + CHUNK, 5:6]
             pre_s[layer, at : at + CHUNK] = pre
             hidden = gelu_exact(pre).astype(BF16)
             hid_s[layer, at : at + CHUNK] = hidden
@@ -485,7 +509,7 @@
 
     def turn_up(layer):
         for at in range(0, FF, CHUNK):
-            wT[:, at : at + CHUNK] = jnp.transpose(wall[layer, 0, at : at + CHUNK, :])
+            wT[:, at : at + CHUNK] = jnp.transpose(wall[layer, 0, at // CHUNK])
 
     turn_up(LAYERS - 1)
 
@@ -507,7 +531,8 @@
     def turn_hidden_sums():
         blank = jnp.zeros((2 * TILE - FB, TILE), F32)
         for j in range(NCH):
-            tall = jnp.concatenate([bc[j * FB : (j + 1) * FB], blank], axis=0)
+            pieces = [bc[y * CHUNK + j * QB : y * CHUNK + (j + 1) * QB] for y in range(4)]
+            tall = jnp.concatenate(pieces + [blank], axis=0)
             for t in range(2):
                 turned = jnp.transpose(tall[t * TILE : (t + 1) * TILE])
                 brow[j, :, t * TILE : (t + 1) * TILE] = turned[:8]
@@ -644,7 +669,7 @@
         g_round = g.astype(BF16)
         lift = jnp.zeros((D, TILE), F32)
         for at in range(0, FF, CHUNK):
-            hidden_grad = mb(wall[layer, 1, at : at + CHUNK, :], g_round)
+            hidden_grad = mb(wall[layer, 1, at // CHUNK], g_round)
             pre_grad = hidden_grad * gelu_slope(pre_s[layer, at : at + CHUNK])
             pre_s[layer, at : at + CHUNK] = pre_grad
             pre_round = pre_grad.astype(BF16)
@@ -682,7 +707,11 @@
             sum_hand(layer + 2)
 
         grads_pair(layer).wait()
-        gsend[...] = (gr[core] + pget[...].astype(F32)).astype(BF16).reshape(NCH, FB, D)
+        for y in range(4):
+            cut = slice(y * CHUNK, (y + 1) * CHUNK)
+            part = (gr[core, cut] + pget[cut].astype(F32)).astype(BF16)
+            for j in range(NCH):
+                gsend[j, y * QB : (y + 1) * QB] = part[j * QB : (j + 1) * QB]
         start(grads_near(layer))
         hidden_sums(layer)
         arrived(two)
@@ -812,7 +841,7 @@
         v((NLAT, 8, 2 * TILE), F32),
         v((NCH, CB, TILE), F32),
         v((NCH, CB, TILE), F32),
-        v((LAYERS, 2, FF, D), BF16),
+        v((LAYERS, 2, 4, CHUNK, D), BF16),
         v((D, FF), BF16),
         v((LAYERS, D, TILE), F32),
         v((LAYERS, D, TILE), F32),
@@ -872,6 +901,8 @@
         dma((2, NLAT)),
         dma((2, NLAT)),
         dma((2 + LAYERS,)),
+        dma((LAYERS, 4)),
+        dma((LAYERS, 4)),
         dma((LAYERS, NLAT)),
         dma((LAYERS, NLAT)),
         dma((LAYERS, NLAT)),
@@ -983,9 +1014,10 @@
     rows = sums[:32].reshape(LAYERS, 8, TILE)
     up_shift_grad = jnp.concatenate([sums[32:36], sums[40:44]], axis=1)[:, :FB]
     wout = wout.reshape(2, LAYERS, FB, D)
-    filters = sout.reshape(LAYERS, 2, CP, 2, CP).transpose(1, 0, 3, 2, 4)
-    fbias = filters[:, :, :, CB, :CB]
-    filters = filters[:, :, :, :CB, :CB]
+    sout = sout.reshape(LAYERS, 2, CP, TILE)
+    both = jnp.stack([sout[..., :CB], sout[..., CP : CP + CB]], axis=1)
+    filters = [both[:, :, at, :CB] for at in range(2)]
+    fbias = [both[:, :, at, CB] for at in range(2)]
     plain, cross = rows[:, 0, :CB], rows[:, 1, :CB]
     return (
         from_tiles(out_h),

time: 269 us -> 260 us (0.967)
  Pallas kernels: 252 us -> 241 us
    pallas_call x1, Pallas kernels: 252 us -> 241 us  [run_stack(): pl.pallas_call(stack_kernel, out_shape=shapes, in_specs=[pl.BlockSpec(mem...]
where the time goes in v5:
time: 260 us
  Pallas kernels  241 us (93%)
  local copies, waits for them, and re-layouts  11.1 us (4%)
  other arithmetic  6.39 us (2%)
    pallas_call x1, Pallas kernels, run_stack(): pl.pallas_call(stack_kernel, out_shape=shapes, in_specs=[pl.BlockSpec(mem...  241 us

profile of v5, /device:TPU:1, one launch (start us, length us, event | category | flops | bytes accessed | tf_op | source)
XLA Modules:
  0.0 259.5 jit_solution(18292318535617275345)
XLA Ops:
  0.6 0.0 copy-start.3
  0.7 1.1 copy.44
  1.8 0.0 copy-start.1
  1.8 0.0 copy-start.2
  1.8 0.1 reshape.134
  2.0 0.0 copy-done.3
  2.0 0.2 copy.46
  2.1 0.1 reshape.136
  2.3 0.8 bitcast_bitcast_fusion
  3.1 0.0 copy-done.1
  3.1 0.0 copy-done.2
  3.1 0.0 copy-start.7
  3.1 0.0 copy-start.12
  3.1 0.0 copy-start.13
  3.1 0.0 copy-start.14
  3.1 0.0 copy-start.9
  3.1 0.0 copy-start.10
  3.1 0.0 copy-start.11
  3.1 0.0 copy-start.15
  3.2 0.0 copy-start.16
  3.2 1.1 pad_maximum_fusion.wsh
  4.3 0.0 copy-done.7
  4.3 0.0 copy-done.8
  4.3 0.0 copy-done.12
  4.3 0.0 copy-done.13
  4.4 0.0 copy-done.14
  4.4 0.0 copy-done.9
  4.4 0.6 copy.78
  5.0 0.0 copy-done.10
  5.0 0.0 copy-done.11
  5.1 0.7 tile.10.fb
  5.8 0.0 copy-done.15
  5.8 0.1 iota_add_fusion
  5.9 0.1 add.61
  6.0 0.0 copy-done.16
  6.0 0.1 broadcast_add_fusion
  6.1 0.1 add.65
  6.2 0.1 pad.35.clone
  6.3 0.7 add_add_fusion.idx
  6.9 241.1 %stack.49 = (f32[8,48,128]{2,1,0:T(8,128)}, f32[8,48,128]{2,1,0:T(8,128)}, bf16[2,4,6,32,384]{4,3,2,1,0:T(8,128)(2,1)}, f32[16,32,128]{2,1,0:T(8,128)}, f32[48,128]{1,0:T(8,128)}) custom-call(f32[8,48,128]{2,1,0:T(8,128)} %get-tuple-element.68.x0, f32[8,48,128]{2,1,0:T(8,128)} %get-tuple-element.67.ct, f32[32,256]{1,0:T(8,128)} %bitcast.91, ...), custom_call_target="tpu_custom_call" | custom-call | tf_op jit(solution)/shard_map/stack/pallas_call | solution.py:913
  248.1 0.7 slice_bitcast_fusion
  248.8 0.6 fusion.6
  249.4 0.6 subtract_divide_fusion
  250.0 1.2 fusion.4
  251.1 0.2 copy.64
  251.3 0.2 copy.65
  251.5 0.0 copy-start
  251.5 0.6 pad_maximum_fusion.2
  252.1 0.0 copy-done.6
  252.1 0.4 fusion
  252.5 0.7 copy.60
  253.3 0.7 copy.61
  254.0 0.7 fusion.5
  254.7 0.6 pad_maximum_fusion.1
  255.3 0.0 copy-done
  255.3 0.1 fusion.3
  255.4 1.1 convert.4
  256.5 1.1 convert_bitcast_fusion
  257.6 0.0 copy-done.5
  257.6 0.2 reshape.142
  257.8 0.8 copy.58
  258.6 0.0 copy-done.4
  258.6 0.2 reshape.144
  258.8 0.8 copy.59
  (18 shorter events, 0.1 us)
Async XLA Ops:
  0.6 1.3 copy-start.3
  1.8 1.3 copy-start.1
  1.8 1.2 copy-start.2
  3.1 1.3 copy-start.7
  3.1 1.3 copy-start.8
  3.1 1.3 copy-start.12
  3.1 1.3 copy-start.13
  3.1 1.3 copy-start.14
  3.1 1.3 copy-start.9
  3.1 1.9 copy-start.10
  3.1 1.9 copy-start.11
  3.1 2.6 %copy-start.15 = (s32[64]{0:T(128)S(1)}, s32[64]{0:T(128)}, u32[]{:S(2)}) copy-start(s32[64]{0:T(128)} %param.35) | copy-start | bytes 772
  3.2 2.9 %copy-start.16 = (s32[60]{0:T(128)S(1)}, s32[60]{0:T(128)}, u32[]{:S(2)}) copy-start(s32[60]{0:T(128)} %param.34) | copy-start | bytes 724
  249.4 2.7 %copy-start.6 = (f32[4,1,48]{2,1,0:T(1,128)}, f32[4,1,48]{2,1,0:T(1,128)S(1)}, u32[]{:S(2)}) copy-start(f32[4,1,48]{2,1,0:T(1,128)S(1)} %get-tuple-element.65) | copy-start | bytes 2308
  251.5 3.8 %copy-start = (bf16[2,4,6,32,384]{4,3,2,1,0:T(8,128)(2,1)S(1)}, bf16[2,4,6,32,384]{4,3,2,1,0:T(8,128)(2,1)}, u32[]{:S(2)}) copy-start(bf16[2,4,6,32,384]{4,3,2,1,0:T(8,128)(2,1)} %get-tuple-element.23) | copy-start | bytes 3538948
  256.5 1.1 copy-start.5
  257.6 1.0 copy-start.4

commit v6 on v5

--- a/solution.py
+++ b/solution.py
@@ -291,7 +291,6 @@
     done(params)
     columns(pcol, TILE, CB)
     between_done(first)
-    second = between_start(lambda p: ct.at[p], xin.at[1, ch], 2, True, keep_ct)
     h_s[...] = xin[0]
 
     lane = lax.broadcasted_iota(jnp.int32, (NLAT, TILE), 1)
@@ -435,6 +434,11 @@
 
         filter_tables(layer)
         arrived(one)
+
+        @pl.when(layer < LAYERS - 1)
+        def _():
+            weights_start(layer + 1)
+
         lon_to_modes(0)
         two = exchange_lat(sbuf, xbuf, 0)
         weights_pass(layer)
@@ -444,10 +448,6 @@
         @pl.when(layer == 0)
         def _():
             columns(bcol, 256, FB)
-
-        @pl.when(layer < LAYERS - 1)
-        def _():
-            weights_start(layer + 1)
 
         arrived(two)
         gather_lat()
@@ -461,6 +461,11 @@
         scatter_lat(table_times(lt[0], lt[1], b - shrink_level * t))
         three = exchange_lat(sbuf2, zbuf, 1)
         sent(two)
+
+        @pl.when(layer == 1)
+        def _():
+            between_start(lambda p: ct.at[p], xin.at[1, ch], 2, True, keep_ct)
+
         arrived(three)
         lon_to_cells(1)
         four = exchange_four()
@@ -503,7 +508,7 @@
         out_g[ch] = g_s[ch]
 
     last_h = between_start(lambda p: h_s.at[p], out_h.at[ch], 3, False, keep_h)
-    between_done(second)
+    between_done(between(lambda p: ct.at[p], xin.at[1, ch], 2, True))
     g_s[...] = xin[1]
     ones = jnp.ones((8, TILE), F32)
 

time: 260 us -> 259 us (level)
  no operation moved by 1% of the time
where the time goes in v6:
time: 259 us
  Pallas kernels  240 us (93%)
  local copies, waits for them, and re-layouts  11.1 us (4%)
  other arithmetic  6.39 us (2%)
    pallas_call x1, Pallas kernels, run_stack(): pl.pallas_call(stack_kernel, out_shape=shapes, in_specs=[pl.BlockSpec(mem...  240 us

profile of v6, /device:TPU:1, one launch (start us, length us, event | category | flops | bytes accessed | tf_op | source)
XLA Modules:
  0.0 258.8 jit_solution(15965760880987118421)
XLA Ops:
  0.6 0.0 copy-start.3
  0.7 1.1 copy.44
  1.8 0.0 copy-start.1
  1.8 0.0 copy-start.2
  1.8 0.1 reshape.134
  2.0 0.0 copy-done.3
  2.0 0.2 copy.46
  2.1 0.1 reshape.136
  2.3 0.8 bitcast_bitcast_fusion
  3.1 0.0 copy-done.1
  3.1 0.0 copy-done.2
  3.1 0.0 copy-start.7
  3.1 0.0 copy-start.12
  3.1 0.0 copy-start.13
  3.1 0.0 copy-start.14
  3.1 0.0 copy-start.9
  3.1 0.0 copy-start.10
  3.1 0.0 copy-start.11
  3.1 0.0 copy-start.15
  3.2 0.0 copy-start.16
  3.2 1.1 pad_maximum_fusion.wsh
  4.3 0.0 copy-done.7
  4.3 0.0 copy-done.8
  4.3 0.0 copy-done.12
  4.3 0.0 copy-done.13
  4.4 0.0 copy-done.14
  4.4 0.0 copy-done.9
  4.4 0.6 copy.78
  5.0 0.0 copy-done.10
  5.0 0.0 copy-done.11
  5.1 0.7 tile.10.fb
  5.8 0.0 copy-done.15
  5.8 0.1 iota_add_fusion
  5.9 0.1 add.61
  6.0 0.0 copy-done.16
  6.0 0.1 broadcast_add_fusion
  6.1 0.1 add.65
  6.2 0.1 pad.35.clone
  6.3 0.7 add_add_fusion.idx
  6.9 240.4 %stack.49 = (f32[8,48,128]{2,1,0:T(8,128)}, f32[8,48,128]{2,1,0:T(8,128)}, bf16[2,4,6,32,384]{4,3,2,1,0:T(8,128)(2,1)}, f32[16,32,128]{2,1,0:T(8,128)}, f32[48,128]{1,0:T(8,128)}) custom-call(f32[8,48,128]{2,1,0:T(8,128)} %get-tuple-element.68.x0, f32[8,48,128]{2,1,0:T(8,128)} %get-tuple-element.67.ct, f32[32,256]{1,0:T(8,128)} %bitcast.91, ...), custom_call_target="tpu_custom_call" | custom-call | tf_op jit(solution)/shard_map/stack/pallas_call | solution.py:918
  247.3 0.7 slice_bitcast_fusion
  248.1 0.6 fusion.6
  248.6 0.6 subtract_divide_fusion
  249.2 1.2 fusion.4
  250.4 0.2 copy.64
  250.6 0.2 copy.65
  250.8 0.0 copy-start
  250.8 0.6 pad_maximum_fusion.2
  251.4 0.0 copy-done.6
  251.4 0.4 fusion
  251.8 0.7 copy.60
  252.5 0.7 copy.61
  253.2 0.7 fusion.5
  253.9 0.6 pad_maximum_fusion.1
  254.5 0.0 copy-done
  254.5 0.1 fusion.3
  254.7 1.1 convert.4
  255.7 1.1 convert_bitcast_fusion
  256.8 0.0 copy-done.5
  256.9 0.2 reshape.142
  257.0 0.8 copy.58
  257.8 0.0 copy-done.4
  257.8 0.2 reshape.144
  258.0 0.8 copy.59
  (18 shorter events, 0.1 us)
Async XLA Ops:
  0.6 1.3 copy-start.3
  1.8 1.3 copy-start.1
  1.8 1.2 copy-start.2
  3.1 1.3 copy-start.7
  3.1 1.3 copy-start.8
  3.1 1.3 copy-start.12
  3.1 1.3 copy-start.13
  3.1 1.3 copy-start.14
  3.1 1.3 copy-start.9
  3.1 1.9 copy-start.10
  3.1 1.9 copy-start.11
  3.1 2.6 %copy-start.15 = (s32[64]{0:T(128)S(1)}, s32[64]{0:T(128)}, u32[]{:S(2)}) copy-start(s32[64]{0:T(128)} %param.35) | copy-start | bytes 772
  3.2 2.9 %copy-start.16 = (s32[60]{0:T(128)S(1)}, s32[60]{0:T(128)}, u32[]{:S(2)}) copy-start(s32[60]{0:T(128)} %param.34) | copy-start | bytes 724
  248.6 2.7 %copy-start.6 = (f32[4,1,48]{2,1,0:T(1,128)}, f32[4,1,48]{2,1,0:T(1,128)S(1)}, u32[]{:S(2)}) copy-start(f32[4,1,48]{2,1,0:T(1,128)S(1)} %get-tuple-element.65) | copy-start | bytes 2308
  250.8 3.8 %copy-start = (bf16[2,4,6,32,384]{4,3,2,1,0:T(8,128)(2,1)S(1)}, bf16[2,4,6,32,384]{4,3,2,1,0:T(8,128)(2,1)}, u32[]{:S(2)}) copy-start(bf16[2,4,6,32,384]{4,3,2,1,0:T(8,128)(2,1)} %get-tuple-element.23) | copy-start | bytes 3538948
  255.7 1.1 copy-start.5
  256.8 1.0 copy-start.4
